TPU v7x, 128 devices: a whole 4x4x4 slice. The times are simulated.
128 devices in a mesh: rep: 4 (over y_lo, core), gx: 8 (over z, y_hi), gy: 4 (over x).
Axes of the slice: x: 4, y: 4 (y_hi: 2, y_lo: 2; y = y_hi * 2 + y_lo), z: 4, core: 2. Of those that a mesh axis runs over, the one named last changes fastest.
Arguments:
- node_feat: bfloat16 [32768, 256], P(('rep', 'gx', 'gy')), may hold values from -6 to 6
- edge_feat: bfloat16 [1048576, 256], P(('rep', 'gx', 'gy')), may hold values from -6 to 6
- edge_src: int32 [1048576], P(('rep', 'gx', 'gy')), may hold values from 0 to 1023
- edge_dst: int32 [1048576], P(('rep', 'gx', 'gy')), may hold values from 0 to 255
- edge_count: int32 [128], P(('rep', 'gx', 'gy')), may hold values from 2048 to 8192, as said below
- send_idx: int32 [4, 8, 4, 2, 2, 64], P('rep', 'gx', 'gy'), may hold values from 0 to 255
- w_qkv: bfloat16 [2, 256, 768], replicated, may hold values from -0.375 to 0.375
- w_edge: bfloat16 [2, 256, 256], replicated, may hold values from -0.375 to 0.375
- gains: float32 [2, 256], replicated, may hold values from 0.1 to 1.9
- head_in: bfloat16 [256, 256], replicated, may hold values from -0.375 to 0.375
- head_out: bfloat16 [256, 169], replicated, may hold values from -0.375 to 0.375
- targets: bfloat16 [169, 1048576], P(None, ('rep', 'gx', 'gy')), may hold values from -15 to 15
Outputs:
- node_out: bfloat16 [32768, 256], P(('rep', 'gx', 'gy'))
- grad_head_in: float32 [256, 256], replicated
- grad_head_out: float32 [256, 169], replicated
Inputs may be any that keep to these rules, and one draw needn't show every extreme that they name: `edge_count`: edge slots of a tile at positions from its count on are padding; some tile holds 8192 live edges.
All inputs are finite; a program needn't handle non-finite values.
Results may differ from a plain program's by a relative error of at most 0.0025.
The roundings to bfloat16 on the way count: a program that leaves them out, or rounds other values in their place, can miss the bound.
Values may be sent and summed in bfloat16 or wider, within the bound.
No kernel may reach another device: no remote copies, remote signals or barrier semaphores. Data moves between devices by JAX's collectives and lax.ppermute only.
A program may use at most 128 MiB of HBM per device.

v0:
```python
import math

import jax
import jax.numpy as jnp
from jax import lax
from jax.sharding import PartitionSpec as P

OUTER_CELLS = (
    (0, 0),
    (0, 1),
    (0, 2),
    (0, 3),
    (1, 0),
    (1, 3),
    (2, 0),
    (2, 3),
    (3, 0),
    (3, 1),
    (3, 2),
    (3, 3),
)


def with_halo(x, sides, width):
    for axis, dim in sides:
        count, length = (lax.axis_size(axis), x.shape[dim])
        up = [(i, (i + 1) % count) for i in range(count)]
        down = [(j, i) for i, j in up]
        last = lax.slice_in_dim(x, length - width, length, axis=dim)
        initial = lax.slice_in_dim(x, 0, width, axis=dim)
        before = lax.ppermute(last, axis, up)
        after = lax.ppermute(initial, axis, down)
        x = jnp.concatenate([before, x, after], axis=dim)
    return x


def layer_norm(values):
    centre = values - jnp.mean(values, axis=-1, keepdims=True)
    spread = jnp.mean(centre * centre, axis=-1, keepdims=True)
    return centre * lax.rsqrt(spread + 1e-05)


def outer_rows(padded):
    return jnp.concatenate([padded[cell_i, cell_j] for cell_i, cell_j in OUTER_CELLS], axis=0)


def edge_pass(table, query_part, edges, edge_src, edge_dst, live_column, weight_edge):
    edge_slots, feature_width = edges.shape
    atom_count = query_part.shape[0]
    table_rows = table.shape[0]
    block_rows = math.gcd(edge_slots, 2048)
    block_count = edge_slots // block_rows
    table_iota = jnp.arange(table_rows, dtype=jnp.int32)
    atom_iota = jnp.arange(atom_count, dtype=jnp.int32)

    def one_block(carry, items):
        edge_rows, source_rows, target_rows, live_rows = items
        source_hot = (source_rows[:, None] == table_iota[None, :]).astype(jnp.bfloat16)
        target_hot = (target_rows[:, None] == atom_iota[None, :]).astype(jnp.bfloat16)
        gathered = jnp.dot(source_hot, table, preferred_element_type=jnp.float32)
        queries = jnp.dot(target_hot, query_part, preferred_element_type=jnp.float32)
        pre_act = queries + gathered[:, :feature_width]
        pre_act = pre_act + jnp.dot(edge_rows, weight_edge, preferred_element_type=jnp.float32)
        new_rows = (edge_rows.astype(jnp.float32) + live_rows * jax.nn.silu(pre_act)).astype(
            jnp.bfloat16
        )
        weighted = live_rows * jax.nn.sigmoid(pre_act) * gathered[:, feature_width:]
        added = lax.dot_general(
            target_hot.astype(jnp.float32),
            weighted,
            (((0,), (0,)), ((), ())),
            precision=lax.Precision.HIGHEST,
            preferred_element_type=jnp.float32,
        )
        return (carry + added, new_rows)

    start = jnp.zeros((atom_count, feature_width), jnp.float32)
    items = (
        edges.reshape(block_count, block_rows, feature_width),
        edge_src.reshape(block_count, block_rows),
        edge_dst.reshape(block_count, block_rows),
        live_column.reshape(block_count, block_rows, 1),
    )
    summed, new_blocks = lax.scan(one_block, start, items)
    return (summed, new_blocks.reshape(edge_slots, feature_width))


def body(
    node_feat,
    edge_feat,
    edge_src,
    edge_dst,
    edge_count,
    send_idx,
    w_qkv,
    w_edge,
    gains,
    head_in,
    head_out,
    targets,
):
    feature_width = node_feat.shape[1]
    edge_slots = edge_feat.shape[0]
    cell_rows = send_idx.shape[-1]
    corner_index = send_idx.reshape(2, 2, cell_rows)
    positions = jnp.arange(edge_slots, dtype=jnp.int32)
    live_column = (positions < edge_count[0]).astype(jnp.float32)[:, None]
    nodes = node_feat
    edges = edge_feat
    for layer_index in range(w_qkv.shape[0]):
        weight_qkv = w_qkv[layer_index]
        projected = jnp.dot(nodes, weight_qkv, preferred_element_type=jnp.float32).astype(
            jnp.bfloat16
        )
        local_kv = projected[:, feature_width:]
        padded = with_halo(nodes[corner_index], (("gx", 0), ("gy", 1)), 1)
        ghost_kv = jnp.dot(
            outer_rows(padded), weight_qkv[:, feature_width:], preferred_element_type=jnp.float32
        ).astype(jnp.bfloat16)
        table = jnp.concatenate([local_kv, ghost_kv], axis=0)
        summed, edges = edge_pass(
            table,
            projected[:, :feature_width],
            edges,
            edge_src,
            edge_dst,
            live_column,
            w_edge[layer_index],
        )
        nodes = (nodes.astype(jnp.float32) + gains[layer_index] * layer_norm(summed)).astype(
            jnp.bfloat16
        )
    scale = 0.125 / (edge_slots * lax.axis_size(("rep", "gx", "gy"))) ** 0.5
    act_in = jnp.dot(edges, head_in, preferred_element_type=jnp.float32)
    hidden_head = jax.nn.silu(act_in).astype(jnp.bfloat16)
    pred = lax.dot_general(
        head_out, hidden_head, (((0,), (1,)), ((), ())), preferred_element_type=jnp.float32
    )
    live_row = live_column[:, 0][None, :]
    dpred = (live_row * (pred - targets.astype(jnp.float32)) * scale).astype(jnp.bfloat16)
    dhidden = lax.dot_general(
        dpred, head_out, (((0,), (1,)), ((), ())), preferred_element_type=jnp.float32
    )
    sigmoid_in = jax.nn.sigmoid(act_in)
    dact = (dhidden * sigmoid_in * (1.0 + act_in * (1.0 - sigmoid_in))).astype(jnp.bfloat16)
    grad_in = lax.dot_general(
        edges, dact, (((0,), (0,)), ((), ())), preferred_element_type=jnp.float32
    )
    grad_out = lax.dot_general(
        hidden_head, dpred, (((0,), (1,)), ((), ())), preferred_element_type=jnp.float32
    )
    grad_in, grad_out = lax.psum((grad_in, grad_out), ("rep", "gx", "gy"))
    return (nodes, grad_in, grad_out)


def solution(mesh):
    return jax.shard_map(
        body,
        mesh=mesh,
        in_specs=(
            P(("rep", "gx", "gy"), None),
            P(("rep", "gx", "gy"), None),
            P(("rep", "gx", "gy")),
            P(("rep", "gx", "gy")),
            P(("rep", "gx", "gy")),
            P("rep", "gx", "gy", None, None, None),
            P(),
            P(),
            P(),
            P(),
            P(),
            P(None, ("rep", "gx", "gy")),
        ),
        out_specs=(P(("rep", "gx", "gy"), None), P(), P()),
        check_vma=False,
    )
```

profile of v0, /device:TPU:1, one launch (start us, length us, event | category | flops | bytes accessed | tf_op | source)
XLA Modules:
  0.0 348.6 jit_solution(3398888422495279461)
XLA Ops:
  10.1 3.8 %collective-permute-start = (bf16[1,2,64,256]{3,2,1,0:T(8,128)(2,1)S(1)}, bf16[1,2,64,256]{3,2,1,0:T(8,128)(2,1)S(1)}, u32[]{:S(2)}, u32[]{:S(2)}) collective-permute-start(bf16[1,2,64,256]{3,2,1,0:T(8,128)(2,1)S(1)} %bitcast.229), channel_id=1, source_target_pairs={{0,4},{4,8},{8,12},{12,16},{16,20},{20,24},{24,28},{28,0},{1,5},{5... | collective-permute-start | bytes 196616 | tf_op jit(solution)/shard_map/ppermute | solution.py:31
  13.9 3.6 %collective-permute-start.1 = (bf16[1,2,64,256]{3,2,1,0:T(8,128)(2,1)S(1)}, bf16[1,2,64,256]{3,2,1,0:T(8,128)(2,1)S(1)}, u32[]{:S(2)}, u32[]{:S(2)}) collective-permute-start(bf16[1,2,64,256]{3,2,1,0:T(8,128)(2,1)S(1)} %bitcast.228), channel_id=1, source_target_pairs={{4,0},{8,4},{12,8},{16,12},{20,16},{24,20},{28,24},{0,28},{5,1},{9... | collective-permute-start | bytes 196616 | tf_op jit(solution)/shard_map/ppermute | solution.py:32
  34.5 61.8 %while.26 = (s32[]{:T(128)}, f32[256,256]{1,0:T(8,128)S(1)}, bf16[4,2048,256]{2,1,0:T(8,128)(2,1)}, s32[4,2048]{1,0:T(4,128)S(1)}, f32[4,2048,1]{1,2,0:T(1,128)S...) while((s32[]{:T(128)}, f32[256,256]{1,0:T(8,128)S(1)}, ...), condition=%wide.region_1.2_spmd.clone, body=%wide.region_0.1_spmd.clone.sunk | while | flops 4306108416 | bytes 55403708 | solution.py:84
  34.6 3.6 %fusion.83 = f32[2048,512]{1,0:T(8,128)S(1)} fusion(bf16[1024,512]{1,0:T(8,128)(2,1)} %get-tuple-element.442, s32[2048]{0:T(1024)S(1)} %bitcast.226), kind=kOutput, calls=%fused_computation.7.clone.1 | convolution fusion | flops 2149580800 | bytes 5251072 | tf_op jit(solution)/shard_map/while/body/eval_jaxpr/dot_general | solution.py:60
  41.9 2.6 bitcast_dynamic-update-slice_fusion.4
  44.6 5.5 %fusion.84 = f32[256,256]{1,0:T(8,128)S(1)} fusion(f32[2048,512]{1,0:T(8,128)} %copy-done.1, f32[2048,256]{1,0:T(8,128)} %get-tuple-element.395, f32[2048]{0:T(1024)S(1)} %bitcast.223, s32[2048]{0:T(1024)S(1)} %bitcast.219, f32[256,256]{1,0:T(8,128)S(1)} %get-tuple-element.424, pred[]{:T(512)S(6)} %compare.6), kind=kOutput, calls=%fused_computation.17.clone.1 | convolution fusion | flops 1613889536 | bytes 4734977 | tf_op jit(solution)/shard_map/while/body/eval_jaxpr/dot_general | solution.py:68
  50.1 3.6 %fusion.83 = f32[2048,512]{1,0:T(8,128)S(1)} fusion(bf16[1024,512]{1,0:T(8,128)(2,1)} %get-tuple-element.442, s32[2048]{0:T(1024)S(1)} %bitcast.226), kind=kOutput, calls=%fused_computation.7.clone.1 | convolution fusion | flops 2149580800 | bytes 5251072 | tf_op jit(solution)/shard_map/while/body/eval_jaxpr/dot_general | solution.py:60
  57.4 2.5 bitcast_dynamic-update-slice_fusion.4
  60.0 5.5 %fusion.84 = f32[256,256]{1,0:T(8,128)S(1)} fusion(f32[2048,512]{1,0:T(8,128)} %copy-done.1, f32[2048,256]{1,0:T(8,128)} %get-tuple-element.395, f32[2048]{0:T(1024)S(1)} %bitcast.223, s32[2048]{0:T(1024)S(1)} %bitcast.219, f32[256,256]{1,0:T(8,128)S(1)} %get-tuple-element.424, pred[]{:T(512)S(6)} %compare.6), kind=kOutput, calls=%fused_computation.17.clone.1 | convolution fusion | flops 1613889536 | bytes 4734977 | tf_op jit(solution)/shard_map/while/body/eval_jaxpr/dot_general | solution.py:68
  65.5 3.6 %fusion.83 = f32[2048,512]{1,0:T(8,128)S(1)} fusion(bf16[1024,512]{1,0:T(8,128)(2,1)} %get-tuple-element.442, s32[2048]{0:T(1024)S(1)} %bitcast.226), kind=kOutput, calls=%fused_computation.7.clone.1 | convolution fusion | flops 2149580800 | bytes 5251072 | tf_op jit(solution)/shard_map/while/body/eval_jaxpr/dot_general | solution.py:60
  72.8 2.6 bitcast_dynamic-update-slice_fusion.4
  75.4 5.5 %fusion.84 = f32[256,256]{1,0:T(8,128)S(1)} fusion(f32[2048,512]{1,0:T(8,128)} %copy-done.1, f32[2048,256]{1,0:T(8,128)} %get-tuple-element.395, f32[2048]{0:T(1024)S(1)} %bitcast.223, s32[2048]{0:T(1024)S(1)} %bitcast.219, f32[256,256]{1,0:T(8,128)S(1)} %get-tuple-element.424, pred[]{:T(512)S(6)} %compare.6), kind=kOutput, calls=%fused_computation.17.clone.1 | convolution fusion | flops 1613889536 | bytes 4734977 | tf_op jit(solution)/shard_map/while/body/eval_jaxpr/dot_general | solution.py:68
  80.9 3.6 %fusion.83 = f32[2048,512]{1,0:T(8,128)S(1)} fusion(bf16[1024,512]{1,0:T(8,128)(2,1)} %get-tuple-element.442, s32[2048]{0:T(1024)S(1)} %bitcast.226), kind=kOutput, calls=%fused_computation.7.clone.1 | convolution fusion | flops 2149580800 | bytes 5251072 | tf_op jit(solution)/shard_map/while/body/eval_jaxpr/dot_general | solution.py:60
  88.3 2.6 bitcast_dynamic-update-slice_fusion.4
  90.9 5.5 %fusion.84 = f32[256,256]{1,0:T(8,128)S(1)} fusion(f32[2048,512]{1,0:T(8,128)} %copy-done.1, f32[2048,256]{1,0:T(8,128)} %get-tuple-element.395, f32[2048]{0:T(1024)S(1)} %bitcast.223, s32[2048]{0:T(1024)S(1)} %bitcast.219, f32[256,256]{1,0:T(8,128)S(1)} %get-tuple-element.424, pred[]{:T(512)S(6)} %compare.6), kind=kOutput, calls=%fused_computation.17.clone.1 | convolution fusion | flops 1613889536 | bytes 4734977 | tf_op jit(solution)/shard_map/while/body/eval_jaxpr/dot_general | solution.py:68
  98.3 4.8 %collective-permute-start.5 = (bf16[1,2,64,256]{3,2,1,0:T(8,128)(2,1)S(1)}, bf16[1,2,64,256]{3,2,1,0:T(8,128)(2,1)S(1)}, u32[]{:S(2)}, u32[]{:S(2)}) collective-permute-start(bf16[1,2,64,256]{3,2,1,0:T(8,128)(2,1)S(1)} %bitcast.230), channel_id=1, source_target_pairs={{4,0},{8,4},{12,8},{16,12},{20,16},{24,20},{28,24},{0,28},{5,1},{9... | collective-permute-start | bytes 196616 | tf_op jit(solution)/shard_map/ppermute | solution.py:32
  105.5 2.7 collective-permute-start.7
  113.0 56.8 %while.27 = (s32[]{:T(128)}, f32[256,256]{1,0:T(8,128)S(1)}, bf16[4,2048,256]{2,1,0:T(8,128)(2,1)}, s32[4,2048]{1,0:T(4,128)S(1)}, f32[4,2048,1]{1,2,0:T(1,128)S...) while((s32[]{:T(128)}, f32[256,256]{1,0:T(8,128)S(1)}, ...), condition=%wide.region_5.6_spmd.clone, body=%wide.region_4.5_spmd.clone.sunk | while | flops 4306108416 | bytes 55403708 | solution.py:84
  113.0 2.4 fusion.88
  119.1 2.6 bitcast_dynamic-update-slice_fusion.5
  121.7 5.5 %fusion.89 = f32[256,256]{1,0:T(8,128)S(1)} fusion(f32[2048,512]{1,0:T(8,128)} %copy-done.2, f32[2048,256]{1,0:T(8,128)} %get-tuple-element.409, f32[2048]{0:T(1024)S(1)} %bitcast.225, s32[2048]{0:T(1024)S(1)} %bitcast.221, f32[256,256]{1,0:T(8,128)S(1)} %get-tuple-element.460, pred[]{:T(512)S(6)} %compare.7), kind=kOutput, calls=%fused_computation.41.clone.1 | convolution fusion | flops 1613889536 | bytes 4734977 | tf_op jit(solution)/shard_map/while/body/eval_jaxpr/dot_general | solution.py:68
  133.3 2.5 bitcast_dynamic-update-slice_fusion.5
  135.9 5.5 %fusion.89 = f32[256,256]{1,0:T(8,128)S(1)} fusion(f32[2048,512]{1,0:T(8,128)} %copy-done.2, f32[2048,256]{1,0:T(8,128)} %get-tuple-element.409, f32[2048]{0:T(1024)S(1)} %bitcast.225, s32[2048]{0:T(1024)S(1)} %bitcast.221, f32[256,256]{1,0:T(8,128)S(1)} %get-tuple-element.460, pred[]{:T(512)S(6)} %compare.7), kind=kOutput, calls=%fused_computation.41.clone.1 | convolution fusion | flops 1613889536 | bytes 4734977 | tf_op jit(solution)/shard_map/while/body/eval_jaxpr/dot_general | solution.py:68
  141.4 2.4 fusion.88
  147.5 2.6 bitcast_dynamic-update-slice_fusion.5
  150.1 5.5 %fusion.89 = f32[256,256]{1,0:T(8,128)S(1)} fusion(f32[2048,512]{1,0:T(8,128)} %copy-done.2, f32[2048,256]{1,0:T(8,128)} %get-tuple-element.409, f32[2048]{0:T(1024)S(1)} %bitcast.225, s32[2048]{0:T(1024)S(1)} %bitcast.221, f32[256,256]{1,0:T(8,128)S(1)} %get-tuple-element.460, pred[]{:T(512)S(6)} %compare.7), kind=kOutput, calls=%fused_computation.41.clone.1 | convolution fusion | flops 1613889536 | bytes 4734977 | tf_op jit(solution)/shard_map/while/body/eval_jaxpr/dot_general | solution.py:68
  155.6 2.4 fusion.88
  161.7 2.6 bitcast_dynamic-update-slice_fusion.5
  164.3 5.5 %fusion.89 = f32[256,256]{1,0:T(8,128)S(1)} fusion(f32[2048,512]{1,0:T(8,128)} %copy-done.2, f32[2048,256]{1,0:T(8,128)} %get-tuple-element.409, f32[2048]{0:T(1024)S(1)} %bitcast.225, s32[2048]{0:T(1024)S(1)} %bitcast.221, f32[256,256]{1,0:T(8,128)S(1)} %get-tuple-element.460, pred[]{:T(512)S(6)} %compare.7), kind=kOutput, calls=%fused_computation.41.clone.1 | convolution fusion | flops 1613889536 | bytes 4734977 | tf_op jit(solution)/shard_map/while/body/eval_jaxpr/dot_general | solution.py:68
  169.8 6.9 %multiply_convert_fusion = (bf16[8192,256]{1,0:T(8,128)(2,1)S(1)}, f32[8192,256]{1,0:T(8,128)}) fusion(bf16[8192,256]{1,0:T(8,128)(2,1)} %bitcast.214, bf16[256,256]{1,0:T(8,128)(2,1)S(1)} %copy-done), kind=kOutput, calls=%fused_computation.62 | convolution fusion | flops 1084227584 | bytes 16908288 | tf_op jit(solution)/shard_map/dot_general | solution.py:134
  179.9 9.2 %fusion.40 = f32[256,256]{1,0:T(8,128)} fusion(bf16[8192,256]{1,0:T(8,128)(2,1)} %bitcast.215, bf16[169,8192]{1,0:T(8,128)(2,1)S(1)} %fusion.39, bf16[256,169]{0,1:T(8,128)(2,1)S(1)} %copy-done.18, f32[8192,256]{1,0:T(8,128)} %get-tuple-element.272), kind=kOutput, calls=%fused_computation.64 | convolution fusion | flops 1801453568 | bytes 15700480 | tf_op jit(solution)/shard_map/dot_general | solution.py:146
  190.3 148.2 %all-reduce.3.cloned.1.call-done = (f32[256,256]{1,0:T(8,128)}, f32[256,169]{0,1:T(8,128)}) async-done(((f32[256,256]{1,0:T(8,128)}, f32[256,169]{0,1:T(8,128)}), (f32[256,256]{1,0:T(8,128)}, f32[256,169]{0,1:T(8,128)})) %all-reduce.3.cloned.1.call-update) | async-done | bytes 435216 | tf_op jit(solution)/shard_map/psum | solution.py:152
  (172 shorter events, 67.6 us)
Async XLA Ops:
  7.2 162.6 %copy-start = (bf16[256,256]{1,0:T(8,128)(2,1)S(1)}, bf16[256,256]{1,0:T(8,128)(2,1)}, u32[]{:S(2)}) copy-start(bf16[256,256]{1,0:T(8,128)(2,1)} %param.25) | copy-start | bytes 393220
  7.2 11.4 %copy-start.3 = (bf16[256,256]{1,0:T(8,128)(2,1)S(1)}, bf16[256,256]{1,0:T(8,128)(2,1)}, u32[]{:S(2)}) copy-start(bf16[256,256]{1,0:T(8,128)(2,1)} %param.16) | copy-start | bytes 393220
  7.2 11.4 %copy-start.6 = (bf16[2,256,768]{2,1,0:T(8,128)(2,1)S(1)}, bf16[2,256,768]{2,1,0:T(8,128)(2,1)}, u32[]{:S(2)}) copy-start(bf16[2,256,768]{2,1,0:T(8,128)(2,1)} %param.22) | copy-start | bytes 2359300
  7.2 12.4 %copy-start.7 = (bf16[2,256,256]{2,1,0:T(8,128)(2,1)S(1)}, bf16[2,256,256]{2,1,0:T(8,128)(2,1)}, u32[]{:S(2)}) copy-start(bf16[2,256,256]{2,1,0:T(8,128)(2,1)} %param.23) | copy-start | bytes 786436
  7.2 13.2 %copy-start.12 = (s32[8192]{0:T(1024)S(1)}, s32[8192]{0:T(1024)}, u32[]{:S(2)}) copy-start(s32[8192]{0:T(1024)} %param.19) | copy-start | bytes 98308
  7.2 13.2 %copy-start.13 = (s32[8192]{0:T(1024)S(1)}, s32[8192]{0:T(1024)}, u32[]{:S(2)}) copy-start(s32[8192]{0:T(1024)} %param.18) | copy-start | bytes 98308
  7.2 331.3 %all-reduce.3.cloned.1.call-start = ((), (), s32[]{:S(2)}) async-start(), calls=%async_computation | async-start | bytes 884736 | tf_op jit(solution)/shard_map/psum | solution.py:152
  10.0 13.9 %copy-start.15 = (f32[2,256]{1,0:T(2,128)S(1)}, f32[2,256]{1,0:T(2,128)}, u32[]{:S(2)}) copy-start(f32[2,256]{1,0:T(2,128)} %param.24) | copy-start | bytes 6148
  10.1 10.4 %collective-permute-start = (bf16[1,2,64,256]{3,2,1,0:T(8,128)(2,1)S(1)}, bf16[1,2,64,256]{3,2,1,0:T(8,128)(2,1)S(1)}, u32[]{:S(2)}, u32[]{:S(2)}) collective-permute-start(bf16[1,2,64,256]{3,2,1,0:T(8,128)(2,1)S(1)} %bitcast.229), channel_id=1, source_target_pairs={{0,4},{4,8},{8,12},{12,16},{16,20},{20,24},{24,28},{28,0},{1,5},{5... | collective-permute-start | bytes 196616 | tf_op jit(solution)/shard_map/ppermute | solution.py:31
  13.9 6.6 %collective-permute-start.1 = (bf16[1,2,64,256]{3,2,1,0:T(8,128)(2,1)S(1)}, bf16[1,2,64,256]{3,2,1,0:T(8,128)(2,1)S(1)}, u32[]{:S(2)}, u32[]{:S(2)}) collective-permute-start(bf16[1,2,64,256]{3,2,1,0:T(8,128)(2,1)S(1)} %bitcast.228), channel_id=1, source_target_pairs={{4,0},{8,4},{12,8},{16,12},{20,16},{24,20},{28,24},{0,28},{5,1},{9... | collective-permute-start | bytes 196616 | tf_op jit(solution)/shard_map/ppermute | solution.py:32
  18.9 13.4 %copy-start.4 = (bf16[256,768]{1,0:T(8,128)(2,1)}, bf16[256,768]{1,0:T(8,128)(2,1)S(1)}, u32[]{:S(2)}) copy-start(bf16[256,768]{1,0:T(8,128)(2,1)S(1)} %convolution_convert_fusion.3) | copy-start | bytes 1179652
  22.6 5.1 %collective-permute-start.2 = (bf16[4,1,64,256]{3,2,1,0:T(8,128)(2,1)S(1)}, bf16[4,1,64,256]{3,2,1,0:T(8,128)(2,1)S(1)}, u32[]{:S(2)}, u32[]{:S(2)}) collective-permute-start(bf16[4,1,64,256]{3,2,1,0:T(8,128)(2,1)S(1)} %get-tuple-element.264), channel_id=1, source_target_pairs={{0,1},{1,2},{2,3},{3,0},{4,5},{5,6},{6,7},{7,4},{8,9},{9,10},{10,1... | collective-permute-start | bytes 393224 | tf_op jit(solution)/shard_map/ppermute | solution.py:31
  24.5 4.8 %collective-permute-start.3 = (bf16[4,1,64,256]{3,2,1,0:T(8,128)(2,1)S(1)}, bf16[4,1,64,256]{3,2,1,0:T(8,128)(2,1)S(1)}, u32[]{:S(2)}, u32[]{:S(2)}) collective-permute-start(bf16[4,1,64,256]{3,2,1,0:T(8,128)(2,1)S(1)} %get-tuple-element.263), channel_id=1, source_target_pairs={{1,0},{2,1},{3,2},{0,3},{5,4},{6,5},{7,6},{4,7},{9,8},{10,9},{11,1... | collective-permute-start | bytes 393224 | tf_op jit(solution)/shard_map/ppermute | solution.py:32
  38.2 6.4 %copy-start.1 = (f32[2048,512]{1,0:T(8,128)}, f32[2048,512]{1,0:T(8,128)S(1)}, u32[]{:S(2)}) copy-start(f32[2048,512]{1,0:T(8,128)S(1)} %fusion.83) | copy-start | bytes 12582916 | tf_op jit(solution)/shard_map/while
  38.2 3.7 %copy-start.16 = (bf16[4,2048,256]{2,1,0:T(8,128)(2,1)S(1)}, bf16[4,2048,256]{2,1,0:T(8,128)(2,1)}, u32[]{:S(2)}) copy-start(bf16[4,2048,256]{2,1,0:T(8,128)(2,1)} %get-tuple-element.443) | copy-start | bytes 12582916 | tf_op jit(solution)/shard_map/while
  53.7 6.3 %copy-start.1 = (f32[2048,512]{1,0:T(8,128)}, f32[2048,512]{1,0:T(8,128)S(1)}, u32[]{:S(2)}) copy-start(f32[2048,512]{1,0:T(8,128)S(1)} %fusion.83) | copy-start | bytes 12582916 | tf_op jit(solution)/shard_map/while
  53.7 3.7 %copy-start.16 = (bf16[4,2048,256]{2,1,0:T(8,128)(2,1)S(1)}, bf16[4,2048,256]{2,1,0:T(8,128)(2,1)}, u32[]{:S(2)}) copy-start(bf16[4,2048,256]{2,1,0:T(8,128)(2,1)} %get-tuple-element.443) | copy-start | bytes 12582916 | tf_op jit(solution)/shard_map/while
  69.1 6.3 %copy-start.1 = (f32[2048,512]{1,0:T(8,128)}, f32[2048,512]{1,0:T(8,128)S(1)}, u32[]{:S(2)}) copy-start(f32[2048,512]{1,0:T(8,128)S(1)} %fusion.83) | copy-start | bytes 12582916 | tf_op jit(solution)/shard_map/while
  69.1 3.7 %copy-start.16 = (bf16[4,2048,256]{2,1,0:T(8,128)(2,1)S(1)}, bf16[4,2048,256]{2,1,0:T(8,128)(2,1)}, u32[]{:S(2)}) copy-start(bf16[4,2048,256]{2,1,0:T(8,128)(2,1)} %get-tuple-element.443) | copy-start | bytes 12582916 | tf_op jit(solution)/shard_map/while
  84.5 6.3 %copy-start.1 = (f32[2048,512]{1,0:T(8,128)}, f32[2048,512]{1,0:T(8,128)S(1)}, u32[]{:S(2)}) copy-start(f32[2048,512]{1,0:T(8,128)S(1)} %fusion.83) | copy-start | bytes 12582916 | tf_op jit(solution)/shard_map/while
  84.5 3.7 %copy-start.16 = (bf16[4,2048,256]{2,1,0:T(8,128)(2,1)S(1)}, bf16[4,2048,256]{2,1,0:T(8,128)(2,1)}, u32[]{:S(2)}) copy-start(bf16[4,2048,256]{2,1,0:T(8,128)(2,1)} %get-tuple-element.443) | copy-start | bytes 12582916 | tf_op jit(solution)/shard_map/while
  98.0 6.8 %collective-permute-start.4 = (bf16[1,2,64,256]{3,2,1,0:T(8,128)(2,1)S(1)}, bf16[1,2,64,256]{3,2,1,0:T(8,128)(2,1)S(1)}, u32[]{:S(2)}, u32[]{:S(2)}) collective-permute-start(bf16[1,2,64,256]{3,2,1,0:T(8,128)(2,1)S(1)} %bitcast.231), channel_id=1, source_target_pairs={{0,4},{4,8},{8,12},{12,16},{16,20},{20,24},{24,28},{28,0},{1,5},{5... | collective-permute-start | bytes 196616 | tf_op jit(solution)/shard_map/ppermute | solution.py:31
  98.3 6.5 %collective-permute-start.5 = (bf16[1,2,64,256]{3,2,1,0:T(8,128)(2,1)S(1)}, bf16[1,2,64,256]{3,2,1,0:T(8,128)(2,1)S(1)}, u32[]{:S(2)}, u32[]{:S(2)}) collective-permute-start(bf16[1,2,64,256]{3,2,1,0:T(8,128)(2,1)S(1)} %bitcast.230), channel_id=1, source_target_pairs={{4,0},{8,4},{12,8},{16,12},{20,16},{24,20},{28,24},{0,28},{5,1},{9... | collective-permute-start | bytes 196616 | tf_op jit(solution)/shard_map/ppermute | solution.py:32
  104.9 5.1 %collective-permute-start.6 = (bf16[4,1,64,256]{3,2,1,0:T(8,128)(2,1)S(1)}, bf16[4,1,64,256]{3,2,1,0:T(8,128)(2,1)S(1)}, u32[]{:S(2)}, u32[]{:S(2)}) collective-permute-start(bf16[4,1,64,256]{3,2,1,0:T(8,128)(2,1)S(1)} %get-tuple-element.262), channel_id=1, source_target_pairs={{0,1},{1,2},{2,3},{3,0},{4,5},{5,6},{6,7},{7,4},{8,9},{9,10},{10,1... | collective-permute-start | bytes 393224 | tf_op jit(solution)/shard_map/ppermute | solution.py:31
  105.5 4.7 %collective-permute-start.7 = (bf16[4,1,64,256]{3,2,1,0:T(8,128)(2,1)S(1)}, bf16[4,1,64,256]{3,2,1,0:T(8,128)(2,1)S(1)}, u32[]{:S(2)}, u32[]{:S(2)}) collective-permute-start(bf16[4,1,64,256]{3,2,1,0:T(8,128)(2,1)S(1)} %get-tuple-element.261), channel_id=1, source_target_pairs={{1,0},{2,1},{3,2},{0,3},{5,4},{6,5},{7,6},{4,7},{9,8},{10,9},{11,1... | collective-permute-start | bytes 393224 | tf_op jit(solution)/shard_map/ppermute | solution.py:32
  115.4 6.3 %copy-start.2 = (f32[2048,512]{1,0:T(8,128)}, f32[2048,512]{1,0:T(8,128)S(1)}, u32[]{:S(2)}) copy-start(f32[2048,512]{1,0:T(8,128)S(1)} %fusion.88) | copy-start | bytes 12582916 | tf_op jit(solution)/shard_map/while
  129.6 6.3 %copy-start.2 = (f32[2048,512]{1,0:T(8,128)}, f32[2048,512]{1,0:T(8,128)S(1)}, u32[]{:S(2)}) copy-start(f32[2048,512]{1,0:T(8,128)S(1)} %fusion.88) | copy-start | bytes 12582916 | tf_op jit(solution)/shard_map/while
  143.8 6.3 %copy-start.2 = (f32[2048,512]{1,0:T(8,128)}, f32[2048,512]{1,0:T(8,128)S(1)}, u32[]{:S(2)}) copy-start(f32[2048,512]{1,0:T(8,128)S(1)} %fusion.88) | copy-start | bytes 12582916 | tf_op jit(solution)/shard_map/while
  158.0 6.3 %copy-start.2 = (f32[2048,512]{1,0:T(8,128)}, f32[2048,512]{1,0:T(8,128)S(1)}, u32[]{:S(2)}) copy-start(f32[2048,512]{1,0:T(8,128)S(1)} %fusion.88) | copy-start | bytes 12582916 | tf_op jit(solution)/shard_map/while
  169.8 6.9 %copy-start.17 = (bf16[169,8192]{1,0:T(8,128)(2,1)S(1)}, bf16[169,8192]{1,0:T(8,128)(2,1)}, u32[]{:S(2)}) copy-start(bf16[169,8192]{1,0:T(8,128)(2,1)} %param.27) | copy-start | bytes 8306692
  169.8 6.9 %copy-start.18 = (bf16[256,169]{0,1:T(8,128)(2,1)S(1)}, bf16[256,169]{0,1:T(8,128)(2,1)}, u32[]{:S(2)}) copy-start(bf16[256,169]{0,1:T(8,128)(2,1)} %param.26) | copy-start | bytes 259588
  179.9 9.6 %copy-start.14 = (f32[1,256]{1,0:T(1,128)S(1)}, f32[1,256]{1,0:T(1,128)}, u32[]{:S(2)}) copy-start(f32[1,256]{1,0:T(1,128)} %get-tuple-element.269) | copy-start | bytes 3076
  (9 other events, 24.0 us)
Sparse Core Ops, SparseCore 0:
  189.6 148.8 all-reduce.2
where the time goes:
time: 350 us; the launch traced here: 349 us
  waiting for transfers between devices  154 us (44%)
  matrix products  122 us (35%)
  local copies, waits for them, and re-layouts  34.6 us (10%)
  starting transfers between devices  18.3 us (5%)
  between operations  15.2 us (4%)
  other arithmetic  4.44 us (1%)
    psum x1, waiting for transfers between devices, body(): grad_in, grad_out = lax.psum((grad_in, grad_out), ('rep', 'gx', 'gy'))  148 us
    dot_general x8, matrix products, one_block(): lax.dot_general(target_hot.astype(jnp.float32), weighted, (((0,), (0,)),...  43.6 us
    dot_general x8, matrix products, one_block(): gathered = jnp.dot(source_hot, table, preferred_element_type=jnp.float32)  24.1 us
    dot_general x8, matrix products, one_block(): jnp.dot(edge_rows, weight_edge, preferred_element_type=jnp.float32)  20.7 us
    while x32, local copies, waits for them, and re-layouts  16.4 us
    dot_general x8, matrix products, one_block(): jnp.dot(target_hot, query_part, preferred_element_type=jnp.float32)  13 us
    ppermute x4, starting transfers between devices, with_halo(): after = lax.ppermute(initial, axis, down)  12.6 us
    dot_general x1, matrix products, body(): lax.dot_general(edges, dact, (((0,), (0,)), ((), ())), preferred_element_...  9.24 us
  transfers between devices with their start and end apart: 9, of which 5 were waited for; matrix products, arithmetic and copies ran while one was open for 2% of the time, Pallas kernels for 0%

commit v1 on v0

v1 whole, which is shorter than its diff:
```python
import functools

import jax
import jax.numpy as jnp
from jax import lax
from jax.experimental import pallas as pl
from jax.experimental.pallas import tpu as pltpu
from jax.sharding import PartitionSpec as P

AXES = ("rep", "gx", "gy")
BF = jnp.bfloat16
F32 = jnp.float32
BLOCK = 2048
SUB = 512


def nn(a, b):
    return jnp.dot(a, b, preferred_element_type=F32)


def nt(a, b):
    return lax.dot_general(a, b, (((1,), (1,)), ((), ())), preferred_element_type=F32)


def tn(a, b):
    return lax.dot_general(a, b, (((0,), (0,)), ((), ())), preferred_element_type=F32)


def hot(row, base, rows):
    index = lax.broadcasted_iota(jnp.int16, (rows, row.shape[1]), 0)
    same = index == (row - base).astype(jnp.int16)
    return jnp.where(same, jnp.ones((), BF), jnp.zeros((), BF))


def sigmoid(x):
    return 0.5 * jnp.tanh(0.5 * x) + 0.5


def pick_corners(nodes, index_row, c0_ref, c1_ref):
    rows = tn(hot(index_row, 0, 256), nodes).astype(BF)
    for j in range(2):
        c0_ref[j] = rows[64 * j : 64 * j + 64]
        c1_ref[j] = rows[128 + 64 * j : 192 + 64 * j]


def corner_kernel(nodes_ref, index_ref, c0_ref, c1_ref):
    pick_corners(nodes_ref[...], index_ref[...], c0_ref, c1_ref)


def prepare(nodes_ref, before_ref, after_ref, low_ref, high_ref, wqkv_ref, wedge_ref, node_t, wkv_t, wqe_t):
    nodes = nodes_ref[...]
    cells = (
        low_ref[0], before_ref[0], before_ref[1], high_ref[0],
        low_ref[1], high_ref[1], low_ref[2], high_ref[2],
        low_ref[3], after_ref[0], after_ref[1], high_ref[3],
    )
    node_t[:, 0:256] = nodes.T
    for k in range(3):
        node_t[:, 256 * (k + 1) : 256 * (k + 2)] = jnp.concatenate(cells[4 * k : 4 * k + 4], axis=0).T
    wkv_t[...] = wqkv_ref[:, 256:].T
    wqe_t[:, 0:256] = nn(nodes, wqkv_ref[:, 0:256]).astype(BF).T
    wqe_t[:, 256:512] = wedge_ref[...].T


def edge_part(edges_t, source, target, node_t, wkv_t, wqe_t):
    source_hot = jnp.concatenate([hot(source, 256 * k, 256) for k in range(4)], axis=0)
    gathered = nn(node_t[...], source_hot).astype(BF)
    kv = nn(wkv_t[...], gathered).astype(BF).astype(F32)
    pre = nn(wqe_t[...], jnp.concatenate([hot(target, 0, 256), edges_t], axis=0)) + kv[:256]
    gate = sigmoid(pre)
    new_edges = (edges_t.astype(F32) + pre * gate).astype(BF)
    return new_edges, gate * kv[256:]


def keep_weighted(weighted, target, position, count, at, hl, target_hot):
    top = weighted.astype(BF)
    hl[0:256, at] = top
    hl[256:512, at] = (weighted - top.astype(F32)).astype(BF)
    target_hot[:, at] = hot(jnp.where(position < count, target, -1), 0, 256)


def new_nodes(nodes_ref, acc, gain_ref):
    summed = (acc[0:256, :] + acc[256:512, :]).T
    centre = summed - jnp.mean(summed, axis=-1, keepdims=True)
    spread = jnp.mean(centre * centre, axis=-1, keepdims=True)
    normed = centre * lax.rsqrt(spread + 1e-05)
    return (nodes_ref[...].astype(F32) + gain_ref[...] * normed).astype(BF)


def first_kernel(
    count_ref, nodes_ref, before_ref, after_ref, low_ref, high_ref, wqkv_ref, wedge_ref, gain_ref, index_ref,
    src_ref, dst_ref, edge_ref,
    out_nodes_ref, c0_ref, c1_ref, out_edge_ref,
    node_t, wkv_t, wqe_t, acc, hl, target_hot,
):
    step = pl.program_id(0)
    count = count_ref[0]

    @pl.when(step == 0)
    def _():
        prepare(nodes_ref, before_ref, after_ref, low_ref, high_ref, wqkv_ref, wedge_ref, node_t, wkv_t, wqe_t)
        acc[...] = jnp.zeros_like(acc)

    @pl.when(step * BLOCK < count)
    def _():
        for j in range(BLOCK // SUB):
            at = slice(j * SUB, (j + 1) * SUB)
            target = dst_ref[0, :, at]
            position = step * BLOCK + j * SUB + lax.broadcasted_iota(jnp.int32, (1, SUB), 1)
            edges, weighted = edge_part(edge_ref[at, :].T, src_ref[0, :, at], target, node_t, wkv_t, wqe_t)
            out_edge_ref[0, :, at] = edges
            keep_weighted(weighted, target, position, count, at, hl, target_hot)
        acc[...] += nt(hl[...], target_hot[...])

    @pl.when(step == pl.num_programs(0) - 1)
    def _():
        nodes = new_nodes(nodes_ref, acc, gain_ref)
        out_nodes_ref[...] = nodes
        pick_corners(nodes, index_ref[...], c0_ref, c1_ref)


def second_kernel(
    count_ref, nodes_ref, before_ref, after_ref, low_ref, high_ref, wqkv_ref, wedge_ref, gain_ref,
    hin_ref, hout_ref, src_ref, dst_ref, edge_ref, goal_ref,
    out_nodes_ref, grad_ref,
    node_t, wkv_t, wqe_t, acc, hl, target_hot, hin_t, hout_t, edges_s, dact_s, hidden_s, dpred_s, grad_in, grad_out,
    *, scale,
):
    step = pl.program_id(0)
    count = count_ref[0]

    @pl.when(step == 0)
    def _():
        prepare(nodes_ref, before_ref, after_ref, low_ref, high_ref, wqkv_ref, wedge_ref, node_t, wkv_t, wqe_t)
        hin_t[...] = hin_ref[...].T
        hout_t[...] = hout_ref[...].T
        acc[...] = jnp.zeros_like(acc)
        grad_in[...] = jnp.zeros_like(grad_in)
        grad_out[...] = jnp.zeros_like(grad_out)

    @pl.when(step * BLOCK < count)
    def _():
        for j in range(BLOCK // SUB):
            at = slice(j * SUB, (j + 1) * SUB)
            target = dst_ref[0, :, at]
            position = step * BLOCK + j * SUB + lax.broadcasted_iota(jnp.int32, (1, SUB), 1)
            edges, weighted = edge_part(edge_ref[0, :, at], src_ref[0, :, at], target, node_t, wkv_t, wqe_t)
            edges_s[:, at] = edges
            keep_weighted(weighted, target, position, count, at, hl, target_hot)
            act = nn(hin_t[...], edges)
            gate = sigmoid(act)
            smooth = act * gate
            hidden = smooth.astype(BF)
            hidden_s[:, at] = hidden
            pred = nn(hout_t[...], hidden)
            weight = jnp.where(position < count, scale, 0.0)
            dpred = ((pred - goal_ref[:, at].astype(F32)) * weight).astype(BF)
            dpred_s[:, at] = dpred
            dhidden = nn(hout_ref[...], dpred)
            dact_s[:, at] = (dhidden * (gate + smooth * (1.0 - gate))).astype(BF)
        acc[...] += nt(hl[...], target_hot[...])
        grad_in[...] += nt(edges_s[...], dact_s[...])
        grad_out[...] += nt(hidden_s[...], dpred_s[...])

    @pl.when(step == pl.num_programs(0) - 1)
    def _():
        out_nodes_ref[...] = new_nodes(nodes_ref, acc, gain_ref)
        grad_ref[0] = grad_in[:, 0:128]
        grad_ref[1] = grad_in[:, 128:256]
        grad_ref[2] = grad_out[:, 0:128]
        grad_ref[3] = jnp.zeros((256, 128), F32)
        grad_ref[3, :, 0:41] = grad_out[:, 128:169]


def whole(*shape):
    return pl.BlockSpec(shape, lambda i: (0,) * len(shape))


COUNT = pl.BlockSpec(memory_space=pltpu.SMEM)
ROWS = pl.BlockSpec((1, 1, BLOCK), lambda i: (i, 0, 0))
EDGES_T = pl.BlockSpec((1, 256, BLOCK), lambda i: (i, 0, 0))
LAYER_SPECS = [
    COUNT, whole(256, 256), whole(2, 64, 256), whole(2, 64, 256), whole(4, 64, 256), whole(4, 64, 256),
    whole(256, 768), whole(256, 256), whole(1, 256),
]
LAYER_SCRATCH = [
    pltpu.VMEM((256, 1024), BF), pltpu.VMEM((512, 256), BF), pltpu.VMEM((256, 512), BF), pltpu.VMEM((512, 256), F32),
    pltpu.VMEM((512, BLOCK), BF), pltpu.VMEM((256, BLOCK), BF),
]
PARAMS = pltpu.CompilerParams(vmem_limit_bytes=48 * 2**20)
CORNER = jax.ShapeDtypeStruct((2, 64, 256), BF)


def halo(c0, c1):
    def both(low, high, axis):
        count = lax.axis_size(axis)
        up = [(i, (i + 1) % count) for i in range(count)]
        down = [(j, i) for i, j in up]
        return lax.ppermute(high, axis, up), lax.ppermute(low, axis, down)

    before, after = both(c0, c1, "gx")
    low, high = (jnp.stack([before[j], c0[j], c1[j], after[j]]) for j in range(2))
    return (before, after) + both(low, high, "gy")


def body(node_feat, edge_feat, edge_src, edge_dst, edge_count, send_idx, w_qkv, w_edge, gains, head_in, head_out, targets):
    slots = edge_feat.shape[0]
    blocks = slots // BLOCK
    scale = 0.125 / (slots * lax.axis_size(AXES)) ** 0.5
    index_row = send_idx.reshape(1, 256)
    source = edge_src.reshape(blocks, 1, BLOCK)
    target = edge_dst.reshape(blocks, 1, BLOCK)

    c0, c1 = pl.pallas_call(corner_kernel, out_shape=[CORNER, CORNER])(node_feat, index_row)
    nodes, c0, c1, edges = pl.pallas_call(
        first_kernel,
        grid=(blocks,),
        in_specs=LAYER_SPECS + [whole(1, 256), ROWS, ROWS, pl.BlockSpec((BLOCK, 256), lambda i: (i, 0))],
        out_specs=[whole(256, 256), whole(2, 64, 256), whole(2, 64, 256), EDGES_T],
        out_shape=[
            jax.ShapeDtypeStruct((256, 256), BF), CORNER, CORNER, jax.ShapeDtypeStruct((blocks, 256, BLOCK), BF),
        ],
        scratch_shapes=LAYER_SCRATCH,
        compiler_params=PARAMS,
    )(edge_count, node_feat, *halo(c0, c1), w_qkv[0], w_edge[0], gains[0:1], index_row, source, target, edge_feat)
    nodes, grads = pl.pallas_call(
        functools.partial(second_kernel, scale=scale),
        grid=(blocks,),
        in_specs=LAYER_SPECS + [
            whole(256, 256), whole(256, 169), ROWS, ROWS, EDGES_T, pl.BlockSpec((169, BLOCK), lambda i: (0, i)),
        ],
        out_specs=[whole(256, 256), whole(4, 256, 128)],
        out_shape=[jax.ShapeDtypeStruct((256, 256), BF), jax.ShapeDtypeStruct((4, 256, 128), F32)],
        scratch_shapes=LAYER_SCRATCH + [
            pltpu.VMEM((256, 256), BF), pltpu.VMEM((169, 256), BF), pltpu.VMEM((256, BLOCK), BF),
            pltpu.VMEM((256, BLOCK), BF), pltpu.VMEM((256, BLOCK), BF), pltpu.VMEM((169, BLOCK), BF),
            pltpu.VMEM((256, 256), F32), pltpu.VMEM((256, 169), F32),
        ],
        compiler_params=PARAMS,
    )(
        edge_count, nodes, *halo(c0, c1), w_qkv[1], w_edge[1], gains[1:2], head_in, head_out, source, target, edges, targets,
    )
    parts = lax.all_to_all(grads.reshape(128, 8, 128), AXES, 0, 0, tiled=True)
    share = jnp.sum(parts, axis=0)
    full = lax.all_to_all(jnp.broadcast_to(share[None], (128, 8, 128)), AXES, 0, 0, tiled=True).reshape(4, 256, 128)
    grad_in = jnp.concatenate([full[0], full[1]], axis=1)
    grad_out = jnp.concatenate([full[2], full[3, :, 0:41]], axis=1)
    return nodes, grad_in, grad_out


def solution(mesh):
    tile = P(AXES)
    return jax.shard_map(
        body,
        mesh=mesh,
        in_specs=(
            P(AXES, None), P(AXES, None), tile, tile, tile, P("rep", "gx", "gy", None, None, None),
            P(), P(), P(), P(), P(), P(None, AXES),
        ),
        out_specs=(P(AXES, None), P(), P()),
        check_vma=False,
    )
```

time: 350 us -> 138 us (0.39)
  waiting for transfers between devices: 154 us -> 14.9 us
  matrix products: 122 us -> 0 us
  blocking collectives: 0 us -> 51.6 us
  Pallas kernels: 0 us -> 30.4 us
  local copies, waits for them, and re-layouts: 34.6 us -> 17.2 us
  between operations: 15.2 us -> 1.45 us
    psum x1 -> x0, waiting for transfers between devices: 148 us -> none  [body(): grad_in, grad_out = lax.psum((grad_in, grad_out), ('rep', 'gx', 'gy'))]
    dot_general x40 -> x0, matrix products: 122 us -> none  [the longest x8 43.6 us: one_block(): lax.dot_general(target_hot.astype(jnp.float32), weighted, (((0,), (0,)),...]
    all_to_all x0 -> x2, blocking collectives: none -> 51.6 us  [the longest x1 34 us: body(): parts = lax.all_to_all(grads.reshape(128, 8, 128), AXES, 0, 0, tiled=True)]
    pallas_call x0 -> x3, Pallas kernels: none -> 30.4 us  [the longest x1 18.4 us: body(): pl.pallas_call(functools.partial(second_kernel, scale=scale), grid=(block...]
    while x32 -> x0, local copies, waits for them, and re-layouts: 16.4 us -> none
    ppermute x8, waiting for transfers between devices: 5.4 us -> 14.9 us  [both(): return (lax.ppermute(high, axis, up), lax.ppermute(low, axis, down))]
    another operation x2 -> x0, local copies, waits for them, and re-layouts: 4.51 us -> none
    unnamed x54 -> x32, local copies, waits for them, and re-layouts: 7.69 us -> 11.8 us
  transfers between devices with their start and end apart: 9 -> 8, of which waited for: 5 -> 5; matrix products, arithmetic and copies ran while one was open for 2% -> 4% of each run, Pallas kernels for 0% -> 0%
where the time goes in v1:
time: 138 us; the launch traced here: 137 us
  blocking collectives  51.6 us (37%)
  Pallas kernels  30.4 us (22%)
  starting transfers between devices  19.2 us (14%)
  local copies, waits for them, and re-layouts  17.2 us (12%)
  waiting for transfers between devices  14.9 us (11%)
  other arithmetic  2.27 us (2%)
  between operations  1.45 us (1%)
    all_to_all x1, blocking collectives, body(): parts = lax.all_to_all(grads.reshape(128, 8, 128), AXES, 0, 0, tiled=True)  34 us
    ppermute x8, starting transfers between devices, both(): return (lax.ppermute(high, axis, up), lax.ppermute(low, axis, down))  19.2 us
    pallas_call x1, Pallas kernels, body(): pl.pallas_call(functools.partial(second_kernel, scale=scale), grid=(block...  18.4 us
    all_to_all x1, blocking collectives, body(): lax.all_to_all(jnp.broadcast_to(share[None], (128, 8, 128)), AXES, 0, 0,...  17.6 us
    ppermute x8, waiting for transfers between devices, both(): return (lax.ppermute(high, axis, up), lax.ppermute(low, axis, down))  14.9 us
    unnamed x32, local copies, waits for them, and re-layouts  11.8 us
    pallas_call x1, Pallas kernels, body(): pl.pallas_call(first_kernel, grid=(blocks,), in_specs=LAYER_SPECS + [whol...  10.2 us
  transfers between devices with their start and end apart: 8, of which 5 were waited for; matrix products, arithmetic and copies ran while one was open for 4% of the time, Pallas kernels for 0%

profile of v1, /device:TPU:1, one launch (start us, length us, event | category | flops | bytes accessed | tf_op | source)
XLA Modules:
  0.0 137.0 jit_solution(3924589012674435052)
XLA Ops:
  0.6 1.3 reshape.28.index_ref
  2.0 1.8 %shard_map.139 = (bf16[2,64,256]{2,1,0:T(8,128)(2,1)}, bf16[2,64,256]{2,1,0:T(8,128)(2,1)}) custom-call(bf16[256,256]{1,0:T(8,128)(2,1)} %nodes_ref.3, s32[1,256]{1,0:T(1,128)} %reshape.28.index_ref), custom_call_target="tpu_custom_call" | custom-call | tf_op jit(solution)/shard_map/pallas_call | solution.py:214
  3.7 3.7 %collective-permute-start = (bf16[2,64,256]{2,1,0:T(8,128)(2,1)}, bf16[2,64,256]{2,1,0:T(8,128)(2,1)S(1)}, u32[]{:S(2)}, u32[]{:S(2)}) collective-permute-start(bf16[2,64,256]{2,1,0:T(8,128)(2,1)} %get-tuple-element.11), channel_id=1, source_target_pairs={{0,4},{4,8},{8,12},{12,16},{16,20},{20,24},{24,28},{28,0},{1,5},{5... | collective-permute-start | bytes 196616 | tf_op jit(solution)/shard_map/ppermute | solution.py:199
  7.5 3.5 %collective-permute-start.1 = (bf16[2,64,256]{2,1,0:T(8,128)(2,1)}, bf16[2,64,256]{2,1,0:T(8,128)(2,1)S(1)}, u32[]{:S(2)}, u32[]{:S(2)}) collective-permute-start(bf16[2,64,256]{2,1,0:T(8,128)(2,1)} %get-tuple-element.12), channel_id=1, source_target_pairs={{4,0},{8,4},{12,8},{16,12},{20,16},{24,20},{28,24},{0,28},{5,1},{9... | collective-permute-start | bytes 196616 | tf_op jit(solution)/shard_map/ppermute | solution.py:199
  11.0 1.2 slice_bitcast_fusion
  12.1 1.1 slice_bitcast_fusion.6
  13.3 0.8 fusion.5
  14.8 2.5 %collective-permute-start.3 = (bf16[4,64,256]{2,1,0:T(8,128)(2,1)S(1)}, bf16[4,64,256]{2,1,0:T(8,128)(2,1)S(1)}, u32[]{:S(2)}, u32[]{:S(2)}) collective-permute-start(bf16[4,64,256]{2,1,0:T(8,128)(2,1)S(1)} %pad_maximum_fusion.3), channel_id=1, source_target_pairs={{1,0},{2,1},{3,2},{0,3},{5,4},{6,5},{7,6},{4,7},{9,8},{10,9},{11,1... | collective-permute-start | bytes 393224 | tf_op jit(solution)/shard_map/ppermute | solution.py:199
  17.5 0.8 fusion.8
  18.3 1.1 collective-permute-done.3.high_ref
  19.3 3.2 %collective-permute-done.2.low_ref = bf16[4,64,256]{2,1,0:T(8,128)(2,1)S(1)} collective-permute-done((bf16[4,64,256]{2,1,0:T(8,128)(2,1)S(1)}, bf16[4,64,256]{2,1,0:T(8,128)(2,1)S(1)}, u32[]{:S(2)}, u32[]{:S(2)}) %collective-permute-start.2) | collective-permute-done | bytes 131104 | tf_op jit(solution)/shard_map/ppermute | solution.py:199
  22.5 0.9 copy-done.2
  23.4 0.8 copy-done.10
  24.2 0.8 copy-done.12
  25.6 10.2 %shard_map.140 = (bf16[256,256]{1,0:T(8,128)(2,1)S(1)}, bf16[2,64,256]{2,1,0:T(8,128)(2,1)S(1)}, bf16[2,64,256]{2,1,0:T(8,128)(2,1)S(1)}, bf16[4,256,2048]{2,1,0:T(8,128)(2,1)S(1)}) custom-call(s32[1]{0:T(128)S(6)} %copy.20.count_ref, bf16[256,256]{1,0:T(8,128)(2,1)S(1)} %copy-done.2, bf16[2,64,256]{2,1,0:T(8,128)(2,1)S(1)} %collective-permute-done.before_ref, ...), custom_call_target="tpu_custom_call" | custom-call | tf_op jit(solution)/shard_map/pallas_call | solution.py:215
  35.8 1.9 %copy-done = bf16[4,256,2048]{2,1,0:T(8,128)(2,1)} copy-done((bf16[4,256,2048]{2,1,0:T(8,128)(2,1)}, bf16[4,256,2048]{2,1,0:T(8,128)(2,1)S(1)}, u32[]{:S(2)}) %copy-start) | copy-done | bytes 4194328
  37.8 5.4 %collective-permute-start.5 = (bf16[2,64,256]{2,1,0:T(8,128)(2,1)S(1)}, bf16[2,64,256]{2,1,0:T(8,128)(2,1)S(1)}, u32[]{:S(2)}, u32[]{:S(2)}) collective-permute-start(bf16[2,64,256]{2,1,0:T(8,128)(2,1)S(1)} %get-tuple-element.15), channel_id=1, source_target_pairs={{4,0},{8,4},{12,8},{16,12},{20,16},{24,20},{28,24},{0,28},{5,1},{9... | collective-permute-start | bytes 196616 | tf_op jit(solution)/shard_map/ppermute | solution.py:199
  43.9 6.5 %collective-permute-done.4.before_ref = bf16[2,64,256]{2,1,0:T(8,128)(2,1)S(1)} collective-permute-done((bf16[2,64,256]{2,1,0:T(8,128)(2,1)S(1)}, bf16[2,64,256]{2,1,0:T(8,128)(2,1)S(1)}, u32[]{:S(2)}, u32[]{:S(2)}) %collective-permute-start.4) | collective-permute-done | bytes 65568 | tf_op jit(solution)/shard_map/ppermute | solution.py:199
  51.1 2.9 %collective-permute-start.7 = (bf16[4,64,256]{2,1,0:T(8,128)(2,1)}, bf16[4,64,256]{2,1,0:T(8,128)(2,1)}, u32[]{:S(2)}, u32[]{:S(2)}) collective-permute-start(bf16[4,64,256]{2,1,0:T(8,128)(2,1)} %pad_maximum_fusion.5), channel_id=1, source_target_pairs={{1,0},{2,1},{3,2},{0,3},{5,4},{6,5},{7,6},{4,7},{9,8},{10,9},{11,1... | collective-permute-start | bytes 393224 | tf_op jit(solution)/shard_map/ppermute | solution.py:199
  55.0 1.0 copy.18.hout_ref
  56.0 0.7 collective-permute-done.7.high_ref
  56.8 3.5 %collective-permute-done.6.low_ref = bf16[4,64,256]{2,1,0:T(8,128)(2,1)} collective-permute-done((bf16[4,64,256]{2,1,0:T(8,128)(2,1)}, bf16[4,64,256]{2,1,0:T(8,128)(2,1)}, u32[]{:S(2)}, u32[]{:S(2)}) %collective-permute-start.6) | collective-permute-done | bytes 131104 | tf_op jit(solution)/shard_map/ppermute | solution.py:199
  60.2 0.8 copy-done.4
  61.1 0.8 copy-done.6
  61.9 0.9 copy-done.7
  62.8 0.9 copy-done.9
  63.7 0.8 copy-done.11
  64.5 0.8 copy-done.13
  65.2 18.4 %shard_map.141 = (bf16[256,256]{1,0:T(8,128)(2,1)}, f32[4,256,128]{2,1,0:T(8,128)S(1)}) custom-call(s32[1]{0:T(128)S(6)} %copy.20.count_ref, bf16[256,256]{1,0:T(8,128)(2,1)S(1)} %copy-done.9, bf16[2,64,256]{2,1,0:T(8,128)(2,1)S(1)} %copy-done.6, bf16[2,64,256]{2,1,0:T(8,128)(2,1)S(1)} %copy-done.4, bf16[4,64,256]{2,1,0:T(8,128)(2,1)} %collective-permute-done.6.low_ref, ...), custom_call_target="tpu_custom_call" | custom-call | tf_op jit(solution)/shard_map/pallas_call | solution.py:226
  83.7 34.0 %all_to_all.10 = f32[128,8,128]{2,1,0:T(8,128)S(1)} all-to-all(f32[128,8,128]{2,1,0:T(8,128)S(1)} %bitcast.20), channel_id=1, replica_groups=mesh['rep'=4,'gx'=8,'gy'=4] {'rep','gx','gy'}, dimensions={0} | all-to-all | bytes 1048576 | tf_op jit(solution)/shard_map/all_to_all | solution.py:243
  117.9 17.6 %all_to_all.11 = f32[128,8,128]{2,1,0:T(8,128)S(1)} all-to-all(f32[128,8,128]{2,1,0:T(8,128)S(1)} %broadcast_in_dim.2), channel_id=1, replica_groups=mesh['rep'=4,'gx'=8,'gy'=4] {'rep','gx','gy'}, dimensions={0} | all-to-all | bytes 1048576 | tf_op jit(solution)/shard_map/all_to_all | solution.py:245
  135.5 0.8 copy.19
  (42 shorter events, 4.3 us)
Async XLA Ops:
  3.7 11.0 %collective-permute-start = (bf16[2,64,256]{2,1,0:T(8,128)(2,1)}, bf16[2,64,256]{2,1,0:T(8,128)(2,1)S(1)}, u32[]{:S(2)}, u32[]{:S(2)}) collective-permute-start(bf16[2,64,256]{2,1,0:T(8,128)(2,1)} %get-tuple-element.11), channel_id=1, source_target_pairs={{0,4},{4,8},{8,12},{12,16},{16,20},{20,24},{24,28},{28,0},{1,5},{5... | collective-permute-start | bytes 196616 | tf_op jit(solution)/shard_map/ppermute | solution.py:199
  7.5 7.3 %collective-permute-start.1 = (bf16[2,64,256]{2,1,0:T(8,128)(2,1)}, bf16[2,64,256]{2,1,0:T(8,128)(2,1)S(1)}, u32[]{:S(2)}, u32[]{:S(2)}) collective-permute-start(bf16[2,64,256]{2,1,0:T(8,128)(2,1)} %get-tuple-element.12), channel_id=1, source_target_pairs={{4,0},{8,4},{12,8},{16,12},{20,16},{24,20},{28,24},{0,28},{5,1},{9... | collective-permute-start | bytes 196616 | tf_op jit(solution)/shard_map/ppermute | solution.py:199
  12.1 48.1 %copy-start.1 = (bf16[169,8192]{1,0:T(8,128)(2,1)S(1)}, bf16[169,8192]{1,0:T(8,128)(2,1)}, u32[]{:S(2)}) copy-start(bf16[169,8192]{1,0:T(8,128)(2,1)} %goal_ref.1) | copy-start | bytes 8306692
  14.8 4.5 %collective-permute-start.3 = (bf16[4,64,256]{2,1,0:T(8,128)(2,1)S(1)}, bf16[4,64,256]{2,1,0:T(8,128)(2,1)S(1)}, u32[]{:S(2)}, u32[]{:S(2)}) collective-permute-start(bf16[4,64,256]{2,1,0:T(8,128)(2,1)S(1)} %pad_maximum_fusion.3), channel_id=1, source_target_pairs={{1,0},{2,1},{3,2},{0,3},{5,4},{6,5},{7,6},{4,7},{9,8},{10,9},{11,1... | collective-permute-start | bytes 393224 | tf_op jit(solution)/shard_map/ppermute | solution.py:199
  17.4 5.1 %collective-permute-start.2 = (bf16[4,64,256]{2,1,0:T(8,128)(2,1)S(1)}, bf16[4,64,256]{2,1,0:T(8,128)(2,1)S(1)}, u32[]{:S(2)}, u32[]{:S(2)}) collective-permute-start(bf16[4,64,256]{2,1,0:T(8,128)(2,1)S(1)} %pad_maximum_fusion.2), channel_id=1, source_target_pairs={{0,1},{1,2},{2,3},{3,0},{4,5},{5,6},{6,7},{7,4},{8,9},{9,10},{10,1... | collective-permute-start | bytes 393224 | tf_op jit(solution)/shard_map/ppermute | solution.py:199
  22.5 0.9 copy-start.2
  23.4 0.8 copy-start.10
  24.2 0.8 copy-start.12
  24.9 0.7 copy-start.14
  35.8 2.0 %copy-start = (bf16[4,256,2048]{2,1,0:T(8,128)(2,1)}, bf16[4,256,2048]{2,1,0:T(8,128)(2,1)S(1)}, u32[]{:S(2)}) copy-start(bf16[4,256,2048]{2,1,0:T(8,128)(2,1)S(1)} %get-tuple-element.16.edge_ref) | copy-start | bytes 12582916
  37.8 16.9 %copy-start.8 = (bf16[256,256]{1,0:T(8,128)(2,1)}, bf16[256,256]{1,0:T(8,128)(2,1)S(1)}, u32[]{:S(2)}) copy-start(bf16[256,256]{1,0:T(8,128)(2,1)S(1)} %get-tuple-element.13.nodes_ref) | copy-start | bytes 393220
  37.8 12.6 %collective-permute-start.5 = (bf16[2,64,256]{2,1,0:T(8,128)(2,1)S(1)}, bf16[2,64,256]{2,1,0:T(8,128)(2,1)S(1)}, u32[]{:S(2)}, u32[]{:S(2)}) collective-permute-start(bf16[2,64,256]{2,1,0:T(8,128)(2,1)S(1)} %get-tuple-element.15), channel_id=1, source_target_pairs={{4,0},{8,4},{12,8},{16,12},{20,16},{24,20},{28,24},{0,28},{5,1},{9... | collective-permute-start | bytes 196616 | tf_op jit(solution)/shard_map/ppermute | solution.py:199
  43.1 7.2 %collective-permute-start.4 = (bf16[2,64,256]{2,1,0:T(8,128)(2,1)S(1)}, bf16[2,64,256]{2,1,0:T(8,128)(2,1)S(1)}, u32[]{:S(2)}, u32[]{:S(2)}) collective-permute-start(bf16[2,64,256]{2,1,0:T(8,128)(2,1)S(1)} %get-tuple-element.14), channel_id=1, source_target_pairs={{0,4},{4,8},{8,12},{12,16},{16,20},{20,24},{24,28},{28,0},{1,5},{5... | collective-permute-start | bytes 196616 | tf_op jit(solution)/shard_map/ppermute | solution.py:199
  50.3 4.3 %copy-start.5 = (bf16[2,64,256]{2,1,0:T(8,128)(2,1)}, bf16[2,64,256]{2,1,0:T(8,128)(2,1)S(1)}, u32[]{:S(2)}) copy-start(bf16[2,64,256]{2,1,0:T(8,128)(2,1)S(1)} %collective-permute-done.4.before_ref) | copy-start | bytes 196612
  50.4 4.3 %copy-start.3 = (bf16[2,64,256]{2,1,0:T(8,128)(2,1)}, bf16[2,64,256]{2,1,0:T(8,128)(2,1)S(1)}, u32[]{:S(2)}) copy-start(bf16[2,64,256]{2,1,0:T(8,128)(2,1)S(1)} %collective-permute-done.5.after_ref) | copy-start | bytes 196612
  51.1 5.7 %collective-permute-start.7 = (bf16[4,64,256]{2,1,0:T(8,128)(2,1)}, bf16[4,64,256]{2,1,0:T(8,128)(2,1)}, u32[]{:S(2)}, u32[]{:S(2)}) collective-permute-start(bf16[4,64,256]{2,1,0:T(8,128)(2,1)} %pad_maximum_fusion.5), channel_id=1, source_target_pairs={{1,0},{2,1},{3,2},{0,3},{5,4},{6,5},{7,6},{4,7},{9,8},{10,9},{11,1... | collective-permute-start | bytes 393224 | tf_op jit(solution)/shard_map/ppermute | solution.py:199
  54.6 5.6 %collective-permute-start.6 = (bf16[4,64,256]{2,1,0:T(8,128)(2,1)}, bf16[4,64,256]{2,1,0:T(8,128)(2,1)}, u32[]{:S(2)}, u32[]{:S(2)}) collective-permute-start(bf16[4,64,256]{2,1,0:T(8,128)(2,1)} %pad_maximum_fusion.4), channel_id=1, source_target_pairs={{0,1},{1,2},{2,3},{3,0},{4,5},{5,6},{6,7},{7,4},{8,9},{9,10},{10,1... | collective-permute-start | bytes 393224 | tf_op jit(solution)/shard_map/ppermute | solution.py:199
  60.2 0.8 copy-start.4
  61.1 0.8 copy-start.6
  61.9 0.9 copy-start.7
  62.8 0.9 copy-start.9
  63.7 0.8 copy-start.11
  64.5 0.8 copy-start.13

commit v2 on v1

v2 whole, which is shorter than its diff:
```python
import functools

import jax
import jax.numpy as jnp
from jax import lax
from jax.experimental import pallas as pl
from jax.experimental.pallas import tpu as pltpu
from jax.sharding import PartitionSpec as P

AXES = ("rep", "gx", "gy")
BF = jnp.bfloat16
F32 = jnp.float32
BLOCK = 2048
SUB = 256
LAGS = (1, 1, 1)
VMEM_MIB = 28


def nn(a, b):
    return jnp.dot(a, b, preferred_element_type=F32)


def nt(a, b):
    return lax.dot_general(a, b, (((1,), (1,)), ((), ())), preferred_element_type=F32)


def tn(a, b):
    return lax.dot_general(a, b, (((0,), (0,)), ((), ())), preferred_element_type=F32)


def hot(row, base, rows):
    index = lax.broadcasted_iota(jnp.int16, (rows, row.shape[1]), 0)
    same = index == (row - base).astype(jnp.int16)
    return jnp.where(same, jnp.ones((), BF), jnp.zeros((), BF))


def sigmoid(x):
    return 0.5 * jnp.tanh(0.5 * x) + 0.5


def pick_corners(nodes, index_ref, c0_ref, c1_ref):
    for i, out_ref in enumerate((c0_ref, c1_ref)):
        for j in range(2):
            out_ref[j] = tn(hot(index_ref[i, j : j + 1, :], 0, 256), nodes).astype(BF)


def corner_kernel(nodes_ref, index_ref, c0_ref, c1_ref):
    pick_corners(nodes_ref[...], index_ref, c0_ref, c1_ref)


def prepare(nodes_ref, before_ref, after_ref, low_ref, high_ref, wqkv_ref, wedge_ref, node_t, wkv_t, wqe_t):
    nodes = nodes_ref[...]
    cells = (
        low_ref[0], before_ref[0], before_ref[1], high_ref[0],
        low_ref[1], high_ref[1], low_ref[2], high_ref[2],
        low_ref[3], after_ref[0], after_ref[1], high_ref[3],
    )
    node_t[:, 0:256] = nodes.T
    for k in range(3):
        node_t[:, 256 * (k + 1) : 256 * (k + 2)] = jnp.concatenate(cells[4 * k : 4 * k + 4], axis=0).T
    wkv_t[...] = wqkv_ref[:, 256:].T
    wqe_t[:, 0:256] = nn(nodes, wqkv_ref[:, 0:256]).astype(BF).T
    wqe_t[:, 256:512] = wedge_ref[...].T


def new_nodes(nodes_ref, acc, gain):
    summed = (acc[0:256, :] + acc[256:512, :]).T
    centre = summed - jnp.mean(summed, axis=-1, keepdims=True)
    spread = jnp.mean(centre * centre, axis=-1, keepdims=True)
    normed = centre * lax.rsqrt(spread + 1e-05)
    return (nodes_ref[...].astype(F32) + gain * normed).astype(BF)


def staged(stages):
    parts = BLOCK // SUB
    held = [{} for _ in range(parts)]
    lag = 0
    lags = [lag := lag + step for _, step in stages]
    for tick in range(parts + lag):
        for (stage, _), late in zip(stages, lags):
            j = tick - late
            if 0 <= j < parts:
                stage(held[j], slice(j * SUB, (j + 1) * SUB), j * SUB)


def message_stages(first, count, src_ref, dst_ref, read_edges, node_t, wkv_t, wqe_t, hl, target_hot, keep_edges):
    def gather(held, at, start):
        source = src_ref[0, :, at]
        source_hot = jnp.concatenate([hot(source, 256 * k, 256) for k in range(4)], axis=0)
        held["rows"] = nn(node_t[...], source_hot).astype(BF)

    def message(held, at, start):
        target = dst_ref[0, :, at]
        edges = read_edges(at)
        kv = nn(wkv_t[...], held["rows"]).astype(BF).astype(F32)
        pre = nn(wqe_t[...], jnp.concatenate([hot(target, 0, 256), edges], axis=0)) + kv[:256]
        gate = sigmoid(pre)
        held["edges"] = (edges.astype(F32) + pre * gate).astype(BF)
        keep_edges(at, held["edges"])
        weighted = gate * kv[256:]
        top = weighted.astype(BF)
        hl[0:256, at] = top
        hl[256:512, at] = (weighted - top.astype(F32)).astype(BF)
        held["live"] = first + start + lax.broadcasted_iota(jnp.int32, (1, SUB), 1) < count
        target_hot[:, at] = hot(jnp.where(held["live"], target, -1), 0, 256)

    return [(gather, 0), (message, 1)]


def first_kernel(
    count_ref, nodes_ref, before_ref, after_ref, low_ref, high_ref, wqkv_ref, wedge_ref, gain_ref, index_ref,
    src_ref, dst_ref, edge_ref,
    out_nodes_ref, c0_ref, c1_ref, out_edge_ref,
    node_t, wkv_t, wqe_t, acc, hl, target_hot,
):
    step = pl.program_id(0)
    count = count_ref[0]

    @pl.when(step == 0)
    def _():
        prepare(nodes_ref, before_ref, after_ref, low_ref, high_ref, wqkv_ref, wedge_ref, node_t, wkv_t, wqe_t)
        acc[...] = jnp.zeros_like(acc)

    @pl.when(step * BLOCK < count)
    def _():
        def keep_edges(at, edges):
            out_edge_ref[0, :, at] = edges

        staged(
            message_stages(
                step * BLOCK, count, src_ref, dst_ref, lambda at: edge_ref[at, :].T, node_t, wkv_t, wqe_t, hl, target_hot,
                keep_edges,
            )
        )
        acc[...] += nt(hl[...], target_hot[...])

    @pl.when(step == pl.num_programs(0) - 1)
    def _():
        nodes = new_nodes(nodes_ref, acc, gain_ref[0:1, :])
        out_nodes_ref[...] = nodes
        pick_corners(nodes, index_ref, c0_ref, c1_ref)


def second_kernel(
    count_ref, nodes_ref, before_ref, after_ref, low_ref, high_ref, wqkv_ref, wedge_ref, gain_ref,
    hin_ref, hout_ref, src_ref, dst_ref, edge_ref, goal_ref,
    out_nodes_ref, grad_ref,
    node_t, wkv_t, wqe_t, acc, hl, target_hot, hin_t, hout, edges_s, dact_s, hidden_s, dpred_s, grad_in, grad_out,
    *, scale,
):
    step = pl.program_id(0)
    count = count_ref[0]

    @pl.when(step == 0)
    def _():
        prepare(nodes_ref, before_ref, after_ref, low_ref, high_ref, wqkv_ref, wedge_ref, node_t, wkv_t, wqe_t)
        hin_t[...] = hin_ref[...].T
        hout[...] = hout_ref[...].T
        acc[...] = jnp.zeros_like(acc)
        grad_in[...] = jnp.zeros_like(grad_in)
        grad_out[...] = jnp.zeros_like(grad_out)

    @pl.when(step * BLOCK < count)
    def _():
        def keep_edges(at, edges):
            edges_s[:, at] = edges

        def activate(held, at, start):
            act = nn(hin_t[...], held["edges"])
            gate = sigmoid(act)
            smooth = act * gate
            held["hidden"] = smooth.astype(BF)
            hidden_s[:, at] = held["hidden"]
            held["slope"] = gate + smooth * (1.0 - gate)

        def compare(held, at, start):
            pred = nn(hout_ref[...], held["hidden"])
            weight = jnp.where(held["live"], scale, 0.0)
            held["dpred"] = ((pred - goal_ref[:, at].astype(F32)) * weight).astype(BF)
            dpred_s[:, at] = held["dpred"]

        def back(held, at, start):
            dact_s[:, at] = (nn(hout[...], held["dpred"]) * held["slope"]).astype(BF)

        staged(
            message_stages(
                step * BLOCK, count, src_ref, dst_ref, lambda at: edge_ref[0, :, at], node_t, wkv_t, wqe_t, hl, target_hot,
                keep_edges,
            )
            + [(activate, LAGS[0]), (compare, LAGS[1]), (back, LAGS[2])]
        )
        acc[...] += nt(hl[...], target_hot[...])
        grad_in[...] += nt(edges_s[...], dact_s[...])
        grad_out[0:169, :] += nt(dpred_s[...], hidden_s[...])

    @pl.when(step == pl.num_programs(0) - 1)
    def _():
        out_nodes_ref[...] = new_nodes(nodes_ref, acc, gain_ref[1:2, :])
        tile = 0
        for total, rows in ((grad_in, 32), (grad_out, 22)):
            for i in range(rows):
                for j in range(2):
                    grad_ref[tile] = total[8 * i : 8 * i + 8, 128 * j : 128 * j + 128]
                    tile += 1
        grad_ref[tile:128] = jnp.zeros((128 - tile, 8, 128), F32)


def whole(*shape):
    return pl.BlockSpec(shape, lambda i: (0,) * len(shape))


def layer_specs(layer):
    return [
        pl.BlockSpec(memory_space=pltpu.SMEM),
        whole(256, 256), whole(2, 64, 256), whole(2, 64, 256), whole(4, 64, 256), whole(4, 64, 256),
        pl.BlockSpec((None, 256, 768), lambda i: (layer, 0, 0)), pl.BlockSpec((None, 256, 256), lambda i: (layer, 0, 0)),
        whole(2, 256),
    ]


ROWS = pl.BlockSpec((1, 1, BLOCK), lambda i: (i, 0, 0))
EDGES_T = pl.BlockSpec((1, 256, BLOCK), lambda i: (i, 0, 0))
LAYER_SCRATCH = [
    pltpu.VMEM((256, 1024), BF), pltpu.VMEM((512, 256), BF), pltpu.VMEM((256, 512), BF), pltpu.VMEM((512, 256), F32),
    pltpu.VMEM((512, BLOCK), BF), pltpu.VMEM((256, BLOCK), BF),
]
FIRST_PARAMS = pltpu.CompilerParams(vmem_limit_bytes=54 * 2**20)
PARAMS = pltpu.CompilerParams(vmem_limit_bytes=VMEM_MIB * 2**20)
CORNER = jax.ShapeDtypeStruct((2, 64, 256), BF)


def halo(c0, c1):
    def both(low, high, axis):
        count = lax.axis_size(axis)
        up = [(i, (i + 1) % count) for i in range(count)]
        down = [(j, i) for i, j in up]
        return lax.ppermute(high, axis, up), lax.ppermute(low, axis, down)

    before, after = both(c0, c1, "gx")
    low, high = (jnp.stack([before[j], c0[j], c1[j], after[j]]) for j in range(2))
    return (before, after) + both(low, high, "gy")


def body(node_feat, edge_feat, edge_src, edge_dst, edge_count, send_idx, w_qkv, w_edge, gains, head_in, head_out, targets):
    slots = edge_feat.shape[0]
    blocks = slots // BLOCK
    scale = 0.125 / (slots * lax.axis_size(AXES)) ** 0.5
    index = send_idx.reshape(2, 2, 64)
    source = edge_src.reshape(blocks, 1, BLOCK)
    target = edge_dst.reshape(blocks, 1, BLOCK)

    c0, c1 = pl.pallas_call(corner_kernel, out_shape=[CORNER, CORNER])(node_feat, index)
    nodes, c0, c1, edges = pl.pallas_call(
        first_kernel,
        grid=(blocks,),
        in_specs=layer_specs(0) + [whole(2, 2, 64), ROWS, ROWS, pl.BlockSpec((BLOCK, 256), lambda i: (i, 0))],
        out_specs=[whole(256, 256), whole(2, 64, 256), whole(2, 64, 256), EDGES_T],
        out_shape=[
            jax.ShapeDtypeStruct((256, 256), BF), CORNER, CORNER, jax.ShapeDtypeStruct((blocks, 256, BLOCK), BF),
        ],
        scratch_shapes=LAYER_SCRATCH,
        compiler_params=FIRST_PARAMS,
    )(edge_count, node_feat, *halo(c0, c1), w_qkv, w_edge, gains, index, source, target, edge_feat)
    nodes, grads = pl.pallas_call(
        functools.partial(second_kernel, scale=scale),
        grid=(blocks,),
        in_specs=layer_specs(1) + [
            whole(256, 256), whole(169, 256), ROWS, ROWS, EDGES_T, pl.BlockSpec((169, BLOCK), lambda i: (0, i)),
        ],
        out_specs=[whole(256, 256), whole(128, 8, 128)],
        out_shape=[jax.ShapeDtypeStruct((256, 256), BF), jax.ShapeDtypeStruct((128, 8, 128), F32)],
        scratch_shapes=LAYER_SCRATCH + [
            pltpu.VMEM((256, 256), BF), pltpu.VMEM((256, 169), BF), pltpu.VMEM((256, BLOCK), BF),
            pltpu.VMEM((256, BLOCK), BF), pltpu.VMEM((256, BLOCK), BF), pltpu.VMEM((169, BLOCK), BF),
            pltpu.VMEM((256, 256), F32), pltpu.VMEM((176, 256), F32),
        ],
        compiler_params=PARAMS,
    )(
        edge_count, nodes, *halo(c0, c1), w_qkv, w_edge, gains, head_in, head_out.T, source, target, edges, targets,
    )
    parts = lax.all_to_all(grads, AXES, 0, 0, tiled=True)
    share = jnp.sum(parts, axis=0)
    full = lax.all_to_all(jnp.broadcast_to(share[None], (128, 8, 128)), AXES, 0, 0, tiled=True)
    grad_in = full[0:64].reshape(32, 2, 8, 128).transpose(0, 2, 1, 3).reshape(256, 256)
    grad_out = full[64:108].reshape(22, 2, 8, 128).transpose(0, 2, 1, 3).reshape(176, 256)[0:169].T
    return nodes, grad_in, grad_out


def solution(mesh):
    tile = P(AXES)
    return jax.shard_map(
        body,
        mesh=mesh,
        in_specs=(
            P(AXES, None), P(AXES, None), tile, tile, tile, P("rep", "gx", "gy", None, None, None),
            P(), P(), P(), P(), P(), P(None, AXES),
        ),
        out_specs=(P(AXES, None), P(), P()),
        check_vma=False,
    )
```

time: 138 us -> 120 us (0.87)
  local copies, waits for them, and re-layouts: 17.2 us -> 7.64 us
  waiting for transfers between devices: 14.9 us -> 6.99 us
  starting transfers between devices: 19.2 us -> 21.7 us
  other arithmetic: 2.27 us -> 0.21 us
  blocking collectives: 51.6 us -> 49.6 us
  Pallas kernels: 30.4 us -> 32.1 us
    unnamed x32 -> x28, local copies, waits for them, and re-layouts: 11.8 us -> 3.79 us
    ppermute x8, waiting for transfers between devices: 14.9 us -> 6.99 us  [both(): return (lax.ppermute(high, axis, up), lax.ppermute(low, axis, down))]
    pallas_call x2, Pallas kernels: 12 us -> 15.2 us  [the longest x1 13.3 us: body(): pl.pallas_call(first_kernel, grid=(blocks,), in_specs=layer_specs(0) + [w...]
    ppermute x8, starting transfers between devices: 19.2 us -> 21.7 us  [both(): return (lax.ppermute(high, axis, up), lax.ppermute(low, axis, down))]
    squeeze x4 -> x0, local copies, waits for them, and re-layouts: 2.34 us -> none  [the longest x1 1.17 us: body(): w_qkv[1]]
    all_to_all x1, blocking collectives: 34 us -> 32 us  [body(): parts = lax.all_to_all(grads, AXES, 0, 0, tiled=True)]
    pallas_call x1, Pallas kernels: 18.4 us -> 16.9 us  [body(): pl.pallas_call(functools.partial(second_kernel, scale=scale), grid=(block...]
  transfers between devices with their start and end apart: 8 -> 8, of which waited for: 5 -> 6; matrix products, arithmetic and copies ran while one was open for 4% -> 1% of each run, Pallas kernels for 0% -> 0%
where the time goes in v2:
time: 120 us
  blocking collectives  49.6 us (41%)
  Pallas kernels  32.1 us (27%)
  starting transfers between devices  21.7 us (18%)
  local copies, waits for them, and re-layouts  7.64 us (6%)
  waiting for transfers between devices  6.99 us (6%)
  between operations  1.47 us (1%)
    all_to_all x1, blocking collectives, body(): parts = lax.all_to_all(grads, AXES, 0, 0, tiled=True)  32 us
    ppermute x8, starting transfers between devices, both(): return (lax.ppermute(high, axis, up), lax.ppermute(low, axis, down))  21.7 us
    all_to_all x1, blocking collectives, body(): lax.all_to_all(jnp.broadcast_to(share[None], (128, 8, 128)), AXES, 0, 0,...  17.6 us
    pallas_call x1, Pallas kernels, body(): pl.pallas_call(functools.partial(second_kernel, scale=scale), grid=(block...  16.9 us
    pallas_call x1, Pallas kernels, body(): pl.pallas_call(first_kernel, grid=(blocks,), in_specs=layer_specs(0) + [w...  13.3 us
    ppermute x8, waiting for transfers between devices, both(): return (lax.ppermute(high, axis, up), lax.ppermute(low, axis, down))  6.99 us
    unnamed x28, local copies, waits for them, and re-layouts  3.79 us
  transfers between devices with their start and end apart: 8, of which 6 were waited for; matrix products, arithmetic and copies ran while one was open for 1% of the time, Pallas kernels for 0%

profile of v2, /device:TPU:1, one launch (start us, length us, event | category | flops | bytes accessed | tf_op | source)
XLA Modules:
  0.0 119.7 jit_solution(4010744557142044596)
XLA Ops:
  0.6 0.0 copy-start.9
  0.7 0.0 copy-start.1
  0.7 0.0 copy-start.7
  0.7 1.9 %shard_map.139 = (bf16[2,64,256]{2,1,0:T(8,128)(2,1)}, bf16[2,64,256]{2,1,0:T(8,128)(2,1)}) custom-call(bf16[256,256]{1,0:T(8,128)(2,1)} %nodes_ref.3, s32[2,2,64]{2,1,0:T(2,128)} %bitcast.23), custom_call_target="tpu_custom_call" | custom-call | tf_op jit(solution)/shard_map/pallas_call | solution.py:252
  2.6 3.7 %collective-permute-start = (bf16[2,64,256]{2,1,0:T(8,128)(2,1)}, bf16[2,64,256]{2,1,0:T(8,128)(2,1)S(1)}, u32[]{:S(2)}, u32[]{:S(2)}) collective-permute-start(bf16[2,64,256]{2,1,0:T(8,128)(2,1)} %get-tuple-element.11), channel_id=1, source_target_pairs={{0,4},{4,8},{8,12},{12,16},{16,20},{20,24},{24,28},{28,0},{1,5},{5... | collective-permute-start | bytes 196616 | tf_op jit(solution)/shard_map/ppermute | solution.py:237
  6.3 3.5 %collective-permute-start.1 = (bf16[2,64,256]{2,1,0:T(8,128)(2,1)}, bf16[2,64,256]{2,1,0:T(8,128)(2,1)S(1)}, u32[]{:S(2)}, u32[]{:S(2)}) collective-permute-start(bf16[2,64,256]{2,1,0:T(8,128)(2,1)} %get-tuple-element.12), channel_id=1, source_target_pairs={{4,0},{8,4},{12,8},{16,12},{20,16},{24,20},{28,24},{0,28},{5,1},{9... | collective-permute-start | bytes 196616 | tf_op jit(solution)/shard_map/ppermute | solution.py:237
  9.9 0.8 fusion.5
  10.7 1.0 collective-permute-done.before_ref
  11.7 1.3 %collective-permute-start.2 = (bf16[4,64,256]{2,1,0:T(8,128)(2,1)S(1)}, bf16[4,64,256]{2,1,0:T(8,128)(2,1)S(1)}, u32[]{:S(2)}, u32[]{:S(2)}) collective-permute-start(bf16[4,64,256]{2,1,0:T(8,128)(2,1)S(1)} %pad_maximum_fusion), channel_id=1, source_target_pairs={{0,1},{1,2},{2,3},{3,0},{4,5},{5,6},{6,7},{7,4},{8,9},{9,10},{10,1... | collective-permute-start | bytes 393224 | tf_op jit(solution)/shard_map/ppermute | solution.py:237
  13.0 1.5 %collective-permute-start.3 = (bf16[4,64,256]{2,1,0:T(8,128)(2,1)S(1)}, bf16[4,64,256]{2,1,0:T(8,128)(2,1)S(1)}, u32[]{:S(2)}, u32[]{:S(2)}) collective-permute-start(bf16[4,64,256]{2,1,0:T(8,128)(2,1)S(1)} %pad_maximum_fusion.1), channel_id=1, source_target_pairs={{1,0},{2,1},{3,2},{0,3},{5,4},{6,5},{7,6},{4,7},{9,8},{10,9},{11,1... | collective-permute-start | bytes 393224 | tf_op jit(solution)/shard_map/ppermute | solution.py:237
  15.2 1.6 %collective-permute-done.2.low_ref = bf16[4,64,256]{2,1,0:T(8,128)(2,1)S(1)} collective-permute-done((bf16[4,64,256]{2,1,0:T(8,128)(2,1)S(1)}, bf16[4,64,256]{2,1,0:T(8,128)(2,1)S(1)}, u32[]{:S(2)}, u32[]{:S(2)}) %collective-permute-start.2) | collective-permute-done | bytes 131104 | tf_op jit(solution)/shard_map/ppermute | solution.py:237
  16.8 0.1 collective-permute-done.3.high_ref
  16.9 0.6 copy-done.12
  17.5 0.1 copy-done.13
  17.6 13.3 %shard_map.140 = (bf16[256,256]{1,0:T(8,128)(2,1)}, bf16[2,64,256]{2,1,0:T(8,128)(2,1)}, bf16[2,64,256]{2,1,0:T(8,128)(2,1)}, bf16[4,256,2048]{2,1,0:T(8,128)(2,1)}) custom-call(s32[1]{0:T(128)S(6)} %copy.15.count_ref, bf16[256,256]{1,0:T(8,128)(2,1)} %nodes_ref.3, bf16[2,64,256]{2,1,0:T(8,128)(2,1)} %copy-done.10, bf16[2,64,256]{2,1,0:T(8,128)(2,1)} %copy-done.11, ...), custom_call_target="tpu_custom_call" | custom-call | tf_op jit(solution)/shard_map/pallas_call | solution.py:253
  30.9 0.8 fusion.2
  31.7 5.5 %collective-permute-start.4 = (bf16[2,64,256]{2,1,0:T(8,128)(2,1)}, bf16[2,64,256]{2,1,0:T(8,128)(2,1)S(1)}, u32[]{:S(2)}, u32[]{:S(2)}) collective-permute-start(bf16[2,64,256]{2,1,0:T(8,128)(2,1)} %get-tuple-element.14), channel_id=1, source_target_pairs={{0,4},{4,8},{8,12},{12,16},{16,20},{20,24},{24,28},{28,0},{1,5},{5... | collective-permute-start | bytes 196616 | tf_op jit(solution)/shard_map/ppermute | solution.py:237
  37.1 0.8 fusion.1
  37.9 2.8 %collective-permute-start.5 = (bf16[2,64,256]{2,1,0:T(8,128)(2,1)}, bf16[2,64,256]{2,1,0:T(8,128)(2,1)S(1)}, u32[]{:S(2)}, u32[]{:S(2)}) collective-permute-start(bf16[2,64,256]{2,1,0:T(8,128)(2,1)} %get-tuple-element.15), channel_id=1, source_target_pairs={{4,0},{8,4},{12,8},{16,12},{20,16},{24,20},{28,24},{0,28},{5,1},{9... | collective-permute-start | bytes 196616 | tf_op jit(solution)/shard_map/ppermute | solution.py:237
  40.7 1.8 %collective-permute-done.4.before_ref = bf16[2,64,256]{2,1,0:T(8,128)(2,1)S(1)} collective-permute-done((bf16[2,64,256]{2,1,0:T(8,128)(2,1)}, bf16[2,64,256]{2,1,0:T(8,128)(2,1)S(1)}, u32[]{:S(2)}, u32[]{:S(2)}) %collective-permute-start.4) | collective-permute-done | bytes 65568 | tf_op jit(solution)/shard_map/ppermute | solution.py:237
  42.5 0.4 collective-permute-done.5.after_ref
  43.0 0.5 collective-permute-start.6
  43.5 2.9 %collective-permute-start.7 = (bf16[4,64,256]{2,1,0:T(8,128)(2,1)S(1)}, bf16[4,64,256]{2,1,0:T(8,128)(2,1)S(1)}, u32[]{:S(2)}, u32[]{:S(2)}) collective-permute-start(bf16[4,64,256]{2,1,0:T(8,128)(2,1)S(1)} %pad_maximum_fusion.3), channel_id=1, source_target_pairs={{1,0},{2,1},{3,2},{0,3},{5,4},{6,5},{7,6},{4,7},{9,8},{10,9},{11,1... | collective-permute-start | bytes 393224 | tf_op jit(solution)/shard_map/ppermute | solution.py:237
  46.4 2.1 %collective-permute-done.6.low_ref = bf16[4,64,256]{2,1,0:T(8,128)(2,1)S(1)} collective-permute-done((bf16[4,64,256]{2,1,0:T(8,128)(2,1)S(1)}, bf16[4,64,256]{2,1,0:T(8,128)(2,1)S(1)}, u32[]{:S(2)}, u32[]{:S(2)}) %collective-permute-start.6) | collective-permute-done | bytes 131104 | tf_op jit(solution)/shard_map/ppermute | solution.py:237
  48.5 2.2 %copy-done = bf16[4,256,2048]{2,1,0:T(8,128)(2,1)S(1)} copy-done((bf16[4,256,2048]{2,1,0:T(8,128)(2,1)S(1)}, bf16[4,256,2048]{2,1,0:T(8,128)(2,1)}, u32[]{:S(2)}) %copy-start) | copy-done | bytes 4194328
  50.7 0.9 copy-done.5
  51.6 16.9 %shard_map.141 = (bf16[256,256]{1,0:T(8,128)(2,1)}, f32[128,8,128]{2,1,0:T(8,128)S(1)}) custom-call(s32[1]{0:T(128)S(6)} %copy.15.count_ref, bf16[256,256]{1,0:T(8,128)(2,1)S(1)} %copy-done.5, bf16[2,64,256]{2,1,0:T(8,128)(2,1)S(1)} %collective-permute-done.4.before_ref, bf16[2,64,256]{2,1,0:T(8,128)(2,1)S(1)} %collective-permute-done.5.after_ref, ...), custom_call_target="tpu_custom_call" | custom-call | tf_op jit(solution)/shard_map/pallas_call | solution.py:264
  68.5 32.0 %all_to_all.10 = f32[128,8,128]{2,1,0:T(8,128)S(1)} all-to-all(f32[128,8,128]{2,1,0:T(8,128)S(1)} %get-tuple-element.18), channel_id=1, replica_groups=mesh['rep'=4,'gx'=8,'gy'=4] {'rep','gx','gy'}, dimensions={0} | all-to-all | bytes 1048576 | tf_op jit(solution)/shard_map/all_to_all | solution.py:281
  100.5 0.1 reduce_sum.9
  100.7 17.6 %all_to_all.11 = f32[128,8,128]{2,1,0:T(8,128)S(1)} all-to-all(f32[128,8,128]{2,1,0:T(8,128)S(1)} %broadcast_in_dim.2), channel_id=1, replica_groups=mesh['rep'=4,'gx'=8,'gy'=4] {'rep','gx','gy'}, dimensions={0} | all-to-all | bytes 1048576 | tf_op jit(solution)/shard_map/all_to_all | solution.py:283
  118.3 0.7 slice_bitcast_fusion
  119.0 0.7 slice.84
  (33 shorter events, 0.2 us)
Async XLA Ops:
  0.6 47.8 %copy-start.9 = (f32[2,256]{1,0:T(2,128)S(1)}, f32[2,256]{1,0:T(2,128)}, u32[]{:S(2)}) copy-start(f32[2,256]{1,0:T(2,128)} %gain_ref.3) | copy-start | bytes 6148
  0.6 47.8 %copy-start.3 = (bf16[2,256,256]{2,1,0:T(8,128)(2,1)S(1)}, bf16[2,256,256]{2,1,0:T(8,128)(2,1)}, u32[]{:S(2)}) copy-start(bf16[2,256,256]{2,1,0:T(8,128)(2,1)} %wedge_ref.3) | copy-start | bytes 786436
  0.7 47.8 %copy-start.1 = (bf16[2,256,768]{2,1,0:T(8,128)(2,1)S(1)}, bf16[2,256,768]{2,1,0:T(8,128)(2,1)}, u32[]{:S(2)}) copy-start(bf16[2,256,768]{2,1,0:T(8,128)(2,1)} %wqkv_ref.3) | copy-start | bytes 2359300
  0.7 47.8 %copy-start.7 = (s32[8192]{0:T(1024)S(1)}, s32[8192]{0:T(1024)}, u32[]{:S(2)}) copy-start(s32[8192]{0:T(1024)} %param.15) | copy-start | bytes 98308
  0.7 47.8 %copy-start.6 = (s32[8192]{0:T(1024)S(1)}, s32[8192]{0:T(1024)}, u32[]{:S(2)}) copy-start(s32[8192]{0:T(1024)} %param.14) | copy-start | bytes 98308
  0.7 47.8 %copy-start.8 = (bf16[256,169]{0,1:T(8,128)(2,1)S(1)}, bf16[256,169]{0,1:T(8,128)(2,1)}, u32[]{:S(2)}) copy-start(bf16[256,169]{0,1:T(8,128)(2,1)} %param.22) | copy-start | bytes 259588
  0.7 47.8 %copy-start.4 = (bf16[256,256]{1,0:T(8,128)(2,1)S(1)}, bf16[256,256]{1,0:T(8,128)(2,1)}, u32[]{:S(2)}) copy-start(bf16[256,256]{1,0:T(8,128)(2,1)} %hin_ref.1) | copy-start | bytes 393220
  2.6 45.9 %copy-start.2 = (bf16[169,8192]{1,0:T(8,128)(2,1)S(1)}, bf16[169,8192]{1,0:T(8,128)(2,1)}, u32[]{:S(2)}) copy-start(bf16[169,8192]{1,0:T(8,128)(2,1)} %goal_ref.1) | copy-start | bytes 8306692
  2.6 9.1 %collective-permute-start = (bf16[2,64,256]{2,1,0:T(8,128)(2,1)}, bf16[2,64,256]{2,1,0:T(8,128)(2,1)S(1)}, u32[]{:S(2)}, u32[]{:S(2)}) collective-permute-start(bf16[2,64,256]{2,1,0:T(8,128)(2,1)} %get-tuple-element.11), channel_id=1, source_target_pairs={{0,4},{4,8},{8,12},{12,16},{16,20},{20,24},{24,28},{28,0},{1,5},{5... | collective-permute-start | bytes 196616 | tf_op jit(solution)/shard_map/ppermute | solution.py:237
  6.3 5.3 %collective-permute-start.1 = (bf16[2,64,256]{2,1,0:T(8,128)(2,1)}, bf16[2,64,256]{2,1,0:T(8,128)(2,1)S(1)}, u32[]{:S(2)}, u32[]{:S(2)}) collective-permute-start(bf16[2,64,256]{2,1,0:T(8,128)(2,1)} %get-tuple-element.12), channel_id=1, source_target_pairs={{4,0},{8,4},{12,8},{16,12},{20,16},{24,20},{28,24},{0,28},{5,1},{9... | collective-permute-start | bytes 196616 | tf_op jit(solution)/shard_map/ppermute | solution.py:237
  11.7 5.3 %copy-start.10 = (bf16[2,64,256]{2,1,0:T(8,128)(2,1)}, bf16[2,64,256]{2,1,0:T(8,128)(2,1)S(1)}, u32[]{:S(2)}) copy-start(bf16[2,64,256]{2,1,0:T(8,128)(2,1)S(1)} %collective-permute-done.before_ref) | copy-start | bytes 196612
  11.7 5.3 %copy-start.11 = (bf16[2,64,256]{2,1,0:T(8,128)(2,1)}, bf16[2,64,256]{2,1,0:T(8,128)(2,1)S(1)}, u32[]{:S(2)}) copy-start(bf16[2,64,256]{2,1,0:T(8,128)(2,1)S(1)} %collective-permute-done.1.after_ref) | copy-start | bytes 196612
  11.7 5.1 %collective-permute-start.2 = (bf16[4,64,256]{2,1,0:T(8,128)(2,1)S(1)}, bf16[4,64,256]{2,1,0:T(8,128)(2,1)S(1)}, u32[]{:S(2)}, u32[]{:S(2)}) collective-permute-start(bf16[4,64,256]{2,1,0:T(8,128)(2,1)S(1)} %pad_maximum_fusion), channel_id=1, source_target_pairs={{0,1},{1,2},{2,3},{3,0},{4,5},{5,6},{6,7},{7,4},{8,9},{9,10},{10,1... | collective-permute-start | bytes 393224 | tf_op jit(solution)/shard_map/ppermute | solution.py:237
  13.0 3.9 %collective-permute-start.3 = (bf16[4,64,256]{2,1,0:T(8,128)(2,1)S(1)}, bf16[4,64,256]{2,1,0:T(8,128)(2,1)S(1)}, u32[]{:S(2)}, u32[]{:S(2)}) collective-permute-start(bf16[4,64,256]{2,1,0:T(8,128)(2,1)S(1)} %pad_maximum_fusion.1), channel_id=1, source_target_pairs={{1,0},{2,1},{3,2},{0,3},{5,4},{6,5},{7,6},{4,7},{9,8},{10,9},{11,1... | collective-permute-start | bytes 393224 | tf_op jit(solution)/shard_map/ppermute | solution.py:237
  16.8 0.7 copy-start.12
  16.9 0.7 copy-start.13
  31.7 10.9 %collective-permute-start.4 = (bf16[2,64,256]{2,1,0:T(8,128)(2,1)}, bf16[2,64,256]{2,1,0:T(8,128)(2,1)S(1)}, u32[]{:S(2)}, u32[]{:S(2)}) collective-permute-start(bf16[2,64,256]{2,1,0:T(8,128)(2,1)} %get-tuple-element.14), channel_id=1, source_target_pairs={{0,4},{4,8},{8,12},{12,16},{16,20},{20,24},{24,28},{28,0},{1,5},{5... | collective-permute-start | bytes 196616 | tf_op jit(solution)/shard_map/ppermute | solution.py:237
  37.9 5.0 %collective-permute-start.5 = (bf16[2,64,256]{2,1,0:T(8,128)(2,1)}, bf16[2,64,256]{2,1,0:T(8,128)(2,1)S(1)}, u32[]{:S(2)}, u32[]{:S(2)}) collective-permute-start(bf16[2,64,256]{2,1,0:T(8,128)(2,1)} %get-tuple-element.15), channel_id=1, source_target_pairs={{4,0},{8,4},{12,8},{16,12},{20,16},{24,20},{28,24},{0,28},{5,1},{9... | collective-permute-start | bytes 196616 | tf_op jit(solution)/shard_map/ppermute | solution.py:237
  43.0 5.4 %collective-permute-start.6 = (bf16[4,64,256]{2,1,0:T(8,128)(2,1)S(1)}, bf16[4,64,256]{2,1,0:T(8,128)(2,1)S(1)}, u32[]{:S(2)}, u32[]{:S(2)}) collective-permute-start(bf16[4,64,256]{2,1,0:T(8,128)(2,1)S(1)} %pad_maximum_fusion.2), channel_id=1, source_target_pairs={{0,1},{1,2},{2,3},{3,0},{4,5},{5,6},{6,7},{7,4},{8,9},{9,10},{10,1... | collective-permute-start | bytes 393224 | tf_op jit(solution)/shard_map/ppermute | solution.py:237
  43.5 5.0 %collective-permute-start.7 = (bf16[4,64,256]{2,1,0:T(8,128)(2,1)S(1)}, bf16[4,64,256]{2,1,0:T(8,128)(2,1)S(1)}, u32[]{:S(2)}, u32[]{:S(2)}) collective-permute-start(bf16[4,64,256]{2,1,0:T(8,128)(2,1)S(1)} %pad_maximum_fusion.3), channel_id=1, source_target_pairs={{1,0},{2,1},{3,2},{0,3},{5,4},{6,5},{7,6},{4,7},{9,8},{10,9},{11,1... | collective-permute-start | bytes 393224 | tf_op jit(solution)/shard_map/ppermute | solution.py:237
  48.5 2.2 %copy-start = (bf16[4,256,2048]{2,1,0:T(8,128)(2,1)S(1)}, bf16[4,256,2048]{2,1,0:T(8,128)(2,1)}, u32[]{:S(2)}) copy-start(bf16[4,256,2048]{2,1,0:T(8,128)(2,1)} %get-tuple-element.16.edge_ref) | copy-start | bytes 12582916
  50.7 0.9 copy-start.5

commit v3 on v2

--- a/solution.py
+++ b/solution.py
@@ -48,19 +48,28 @@
     pick_corners(nodes_ref[...], index_ref, c0_ref, c1_ref)
 
 
-def prepare(nodes_ref, before_ref, after_ref, low_ref, high_ref, wqkv_ref, wedge_ref, node_t, wkv_t, wqe_t):
+def stack_kernel(before_ref, after_ref, c0_ref, c1_ref, low_ref, high_ref):
+    for j, out_ref in enumerate((low_ref, high_ref)):
+        for i, cell_ref in enumerate((before_ref, c0_ref, c1_ref, after_ref)):
+            out_ref[i] = cell_ref[j]
+
+
+def prepare_own(nodes_ref, wqkv_ref, wedge_ref, node_t, wqe_t):
     nodes = nodes_ref[...]
+    node_t[...] = nodes.T
+    wqe_t[:, 0:256] = nn(nodes, wqkv_ref[:, 0:256]).astype(BF).T
+    wqe_t[:, 256:512] = wedge_ref[...].T
+
+
+def prepare_ghosts(before_ref, after_ref, low_ref, high_ref, wqkv_ref, ghost_t, wkv_t):
     cells = (
         low_ref[0], before_ref[0], before_ref[1], high_ref[0],
         low_ref[1], high_ref[1], low_ref[2], high_ref[2],
         low_ref[3], after_ref[0], after_ref[1], high_ref[3],
     )
-    node_t[:, 0:256] = nodes.T
     for k in range(3):
-        node_t[:, 256 * (k + 1) : 256 * (k + 2)] = jnp.concatenate(cells[4 * k : 4 * k + 4], axis=0).T
+        ghost_t[:, 256 * k : 256 * (k + 1)] = jnp.concatenate(cells[4 * k : 4 * k + 4], axis=0).T
     wkv_t[...] = wqkv_ref[:, 256:].T
-    wqe_t[:, 0:256] = nn(nodes, wqkv_ref[:, 0:256]).astype(BF).T
-    wqe_t[:, 256:512] = wedge_ref[...].T
 
 
 def new_nodes(nodes_ref, acc, gain):
@@ -83,17 +92,74 @@
                 stage(held[j], slice(j * SUB, (j + 1) * SUB), j * SUB)
 
 
-def message_stages(first, count, src_ref, dst_ref, read_edges, node_t, wkv_t, wqe_t, hl, target_hot, keep_edges):
+def own_rows(at, source, target, edges, node_t, wqe_t, own_ref, part_ref):
+    own_ref[0, :, at] = nn(node_t[...], hot(source, 0, 256)).astype(BF)
+    part_ref[0, :, at] = nn(wqe_t[...], jnp.concatenate([hot(target, 0, 256), edges], axis=0))
+
+
+def own_first_kernel(
+    count_ref, nodes_hbm, wqkv_hbm, wedge_hbm, src_hbm, dst_hbm, edge_hbm, own_ref, part_ref, turned_ref,
+    node_t, wqe_t, nodes, wqkv, wedge, src, dst, edge, sems,
+):
+    step = pl.program_id(0)
+    steps = edge.shape[0]
+    small = [
+        pltpu.make_async_copy(nodes_hbm, nodes, sems.at[0]),
+        pltpu.make_async_copy(wqkv_hbm.at[0, :, pl.ds(0, 256)], wqkv, sems.at[1]),
+        pltpu.make_async_copy(wedge_hbm.at[0], wedge, sems.at[2]),
+        pltpu.make_async_copy(src_hbm, src, sems.at[3]),
+        pltpu.make_async_copy(dst_hbm, dst, sems.at[4]),
+    ]
+
+    def edge_copy(i):
+        return pltpu.make_async_copy(edge_hbm.at[pl.ds(i * BLOCK, BLOCK), :], edge.at[i], sems.at[5 + i])
+
+    @pl.when(step == 0)
+    def _():
+        for copy in small:
+            copy.start()
+        for i in range(steps):
+            edge_copy(i).start()
+        for copy in small:
+            copy.wait()
+        prepare_own(nodes, wqkv, wedge, node_t, wqe_t)
+
+    edge_copy(step).wait()
+
+    @pl.when(step * BLOCK < count_ref[0])
+    def _():
+        for j in range(BLOCK // SUB):
+            at = slice(j * SUB, (j + 1) * SUB)
+            edges = edge[step, at, :].T
+            turned_ref[0, :, at] = edges
+            own_rows(at, src[step, :, at], dst[step, :, at], edges, node_t, wqe_t, own_ref, part_ref)
+
+
+def own_kernel(count_ref, nodes_ref, wqkv_ref, wedge_ref, src_ref, dst_ref, edge_ref, own_ref, part_ref, node_t, wqe_t):
+    step = pl.program_id(0)
+
+    @pl.when(step == 0)
+    def _():
+        prepare_own(nodes_ref, wqkv_ref, wedge_ref, node_t, wqe_t)
+
+    @pl.when(step * BLOCK < count_ref[0])
+    def _():
+        for j in range(BLOCK // SUB):
+            at = slice(j * SUB, (j + 1) * SUB)
+            own_rows(at, src_ref[0, :, at], dst_ref[0, :, at], edge_ref[0, :, at], node_t, wqe_t, own_ref, part_ref)
+
+
+def message_stages(first, count, src_ref, dst_ref, own_ref, part_ref, edge_ref, ghost_t, wkv_t, hl, target_hot, keep_edges):
     def gather(held, at, start):
         source = src_ref[0, :, at]
-        source_hot = jnp.concatenate([hot(source, 256 * k, 256) for k in range(4)], axis=0)
-        held["rows"] = nn(node_t[...], source_hot).astype(BF)
+        source_hot = jnp.concatenate([hot(source, 256 * (k + 1), 256) for k in range(3)], axis=0)
+        held["rows"] = nn(ghost_t[...], source_hot).astype(BF) + own_ref[0, :, at]
 
     def message(held, at, start):
         target = dst_ref[0, :, at]
-        edges = read_edges(at)
+        edges = edge_ref[0, :, at]
         kv = nn(wkv_t[...], held["rows"]).astype(BF).astype(F32)
-        pre = nn(wqe_t[...], jnp.concatenate([hot(target, 0, 256), edges], axis=0)) + kv[:256]
+        pre = part_ref[0, :, at] + kv[:256]
         gate = sigmoid(pre)
         held["edges"] = (edges.astype(F32) + pre * gate).astype(BF)
         keep_edges(at, held["edges"])
@@ -108,17 +174,17 @@
 
 
 def first_kernel(
-    count_ref, nodes_ref, before_ref, after_ref, low_ref, high_ref, wqkv_ref, wedge_ref, gain_ref, index_ref,
-    src_ref, dst_ref, edge_ref,
+    count_ref, nodes_ref, before_ref, after_ref, low_ref, high_ref, wqkv_ref, gain_ref,
+    src_ref, dst_ref, own_ref, part_ref, edge_ref, index_ref,
     out_nodes_ref, c0_ref, c1_ref, out_edge_ref,
-    node_t, wkv_t, wqe_t, acc, hl, target_hot,
+    ghost_t, wkv_t, acc, hl, target_hot,
 ):
     step = pl.program_id(0)
     count = count_ref[0]
 
     @pl.when(step == 0)
     def _():
-        prepare(nodes_ref, before_ref, after_ref, low_ref, high_ref, wqkv_ref, wedge_ref, node_t, wkv_t, wqe_t)
+        prepare_ghosts(before_ref, after_ref, low_ref, high_ref, wqkv_ref, ghost_t, wkv_t)
         acc[...] = jnp.zeros_like(acc)
 
     @pl.when(step * BLOCK < count)
@@ -128,8 +194,7 @@
 
         staged(
             message_stages(
-                step * BLOCK, count, src_ref, dst_ref, lambda at: edge_ref[at, :].T, node_t, wkv_t, wqe_t, hl, target_hot,
-                keep_edges,
+                step * BLOCK, count, src_ref, dst_ref, own_ref, part_ref, edge_ref, ghost_t, wkv_t, hl, target_hot, keep_edges
             )
         )
         acc[...] += nt(hl[...], target_hot[...])
@@ -142,10 +207,10 @@
 
 
 def second_kernel(
-    count_ref, nodes_ref, before_ref, after_ref, low_ref, high_ref, wqkv_ref, wedge_ref, gain_ref,
-    hin_ref, hout_ref, src_ref, dst_ref, edge_ref, goal_ref,
+    count_ref, nodes_ref, before_ref, after_ref, low_ref, high_ref, wqkv_ref, gain_ref,
+    src_ref, dst_ref, own_ref, part_ref, edge_ref, hin_ref, hout_ref, goal_ref,
     out_nodes_ref, grad_ref,
-    node_t, wkv_t, wqe_t, acc, hl, target_hot, hin_t, hout, edges_s, dact_s, hidden_s, dpred_s, grad_in, grad_out,
+    ghost_t, wkv_t, acc, hl, target_hot, hin_t, hout, edges_s, dact_s, hidden_s, dpred_s, grad_in, grad_out,
     *, scale,
 ):
     step = pl.program_id(0)
@@ -153,7 +218,7 @@
 
     @pl.when(step == 0)
     def _():
-        prepare(nodes_ref, before_ref, after_ref, low_ref, high_ref, wqkv_ref, wedge_ref, node_t, wkv_t, wqe_t)
+        prepare_ghosts(before_ref, after_ref, low_ref, high_ref, wqkv_ref, ghost_t, wkv_t)
         hin_t[...] = hin_ref[...].T
         hout[...] = hout_ref[...].T
         acc[...] = jnp.zeros_like(acc)
@@ -184,8 +249,7 @@
 
         staged(
             message_stages(
-                step * BLOCK, count, src_ref, dst_ref, lambda at: edge_ref[0, :, at], node_t, wkv_t, wqe_t, hl, target_hot,
-                keep_edges,
+                step * BLOCK, count, src_ref, dst_ref, own_ref, part_ref, edge_ref, ghost_t, wkv_t, hl, target_hot, keep_edges
             )
             + [(activate, LAGS[0]), (compare, LAGS[1]), (back, LAGS[2])]
         )
@@ -209,24 +273,33 @@
     return pl.BlockSpec(shape, lambda i: (0,) * len(shape))
 
 
+def layer_of(layer, *shape):
+    return pl.BlockSpec((None,) + shape, lambda i: (layer, 0, 0))
+
+
+SCALAR = pl.BlockSpec(memory_space=pltpu.SMEM)
+ROWS = pl.BlockSpec((1, 1, BLOCK), lambda i: (i, 0, 0))
+TURNED = pl.BlockSpec((1, 256, BLOCK), lambda i: (i, 0, 0))
+
+
 def layer_specs(layer):
     return [
-        pl.BlockSpec(memory_space=pltpu.SMEM),
-        whole(256, 256), whole(2, 64, 256), whole(2, 64, 256), whole(4, 64, 256), whole(4, 64, 256),
-        pl.BlockSpec((None, 256, 768), lambda i: (layer, 0, 0)), pl.BlockSpec((None, 256, 256), lambda i: (layer, 0, 0)),
-        whole(2, 256),
+        SCALAR, whole(256, 256), whole(2, 64, 256), whole(2, 64, 256), whole(4, 64, 256), whole(4, 64, 256),
+        layer_of(layer, 256, 768), whole(2, 256), ROWS, ROWS, TURNED, TURNED, TURNED,
     ]
 
 
-ROWS = pl.BlockSpec((1, 1, BLOCK), lambda i: (i, 0, 0))
-EDGES_T = pl.BlockSpec((1, 256, BLOCK), lambda i: (i, 0, 0))
 LAYER_SCRATCH = [
-    pltpu.VMEM((256, 1024), BF), pltpu.VMEM((512, 256), BF), pltpu.VMEM((256, 512), BF), pltpu.VMEM((512, 256), F32),
+    pltpu.VMEM((256, 768), BF), pltpu.VMEM((512, 256), BF), pltpu.VMEM((512, 256), F32),
     pltpu.VMEM((512, BLOCK), BF), pltpu.VMEM((256, BLOCK), BF),
 ]
-FIRST_PARAMS = pltpu.CompilerParams(vmem_limit_bytes=54 * 2**20)
+SMALL = pltpu.CompilerParams(vmem_limit_bytes=4 * 2**20)
 PARAMS = pltpu.CompilerParams(vmem_limit_bytes=VMEM_MIB * 2**20)
 CORNER = jax.ShapeDtypeStruct((2, 64, 256), BF)
+
+
+def stays(*arrays):
+    return [pltpu.with_memory_space_constraint(x, pltpu.HBM) for x in arrays]
 
 
 def halo(c0, c1):
@@ -237,7 +310,8 @@
         return lax.ppermute(high, axis, up), lax.ppermute(low, axis, down)
 
     before, after = both(c0, c1, "gx")
-    low, high = (jnp.stack([before[j], c0[j], c1[j], after[j]]) for j in range(2))
+    side = jax.ShapeDtypeStruct((4, 64, 256), BF)
+    low, high = pl.pallas_call(stack_kernel, out_shape=[side, side], compiler_params=SMALL)(before, after, c0, c1)
     return (before, after) + both(low, high, "gy")
 
 
@@ -249,26 +323,58 @@
     source = edge_src.reshape(blocks, 1, BLOCK)
     target = edge_dst.reshape(blocks, 1, BLOCK)
 
-    c0, c1 = pl.pallas_call(corner_kernel, out_shape=[CORNER, CORNER])(node_feat, index)
+    turned = jax.ShapeDtypeStruct((blocks, 256, BLOCK), BF)
+    wide = jax.ShapeDtypeStruct((blocks, 256, BLOCK), F32)
+    square = jax.ShapeDtypeStruct((256, 256), BF)
+
+    weights = [pltpu.VMEM((256, 256), BF), pltpu.VMEM((256, 512), BF)]
+    cost = pl.CostEstimate(flops=6 * slots * 65536, bytes_accessed=24 * 2**20, transcendentals=0)
+    stay = pl.BlockSpec(memory_space=pltpu.HBM)
+
+    def own_first(nodes):
+        return pl.pallas_call(
+            own_first_kernel,
+            grid=(blocks,),
+            in_specs=[SCALAR] + [stay] * 6,
+            out_specs=[TURNED] * 3,
+            out_shape=[turned, wide, turned],
+            scratch_shapes=weights + [pltpu.VMEM((256, 256), BF)] * 3 + [pltpu.VMEM((blocks, 1, BLOCK), jnp.int32)] * 2
+            + [pltpu.VMEM((blocks, BLOCK, 256), BF), pltpu.SemaphoreType.DMA((5 + blocks,))],
+            compiler_params=PARAMS,
+            cost_estimate=cost,
+        )(edge_count, *stays(nodes, w_qkv, w_edge, source, target, edge_feat))
+
+    def own_second(nodes, edges):
+        return pl.pallas_call(
+            own_kernel,
+            grid=(blocks,),
+            in_specs=[SCALAR, whole(256, 256), layer_of(1, 256, 256), layer_of(1, 256, 256), ROWS, ROWS, TURNED],
+            out_specs=[TURNED] * 2,
+            out_shape=[turned, wide],
+            scratch_shapes=weights,
+            compiler_params=PARAMS,
+            cost_estimate=cost,
+        )(edge_count, nodes, w_qkv, w_edge, source, target, edges)
+
+    c0, c1 = pl.pallas_call(corner_kernel, out_shape=[CORNER, CORNER], compiler_params=SMALL)(*stays(node_feat, index))
+    later_nodes, _ = lax.optimization_barrier((node_feat, c0))
+    own, part, edges = own_first(later_nodes)
     nodes, c0, c1, edges = pl.pallas_call(
         first_kernel,
         grid=(blocks,),
-        in_specs=layer_specs(0) + [whole(2, 2, 64), ROWS, ROWS, pl.BlockSpec((BLOCK, 256), lambda i: (i, 0))],
-        out_specs=[whole(256, 256), whole(2, 64, 256), whole(2, 64, 256), EDGES_T],
-        out_shape=[
-            jax.ShapeDtypeStruct((256, 256), BF), CORNER, CORNER, jax.ShapeDtypeStruct((blocks, 256, BLOCK), BF),
-        ],
+        in_specs=layer_specs(0) + [whole(2, 2, 64)],
+        out_specs=[whole(256, 256), whole(2, 64, 256), whole(2, 64, 256), TURNED],
+        out_shape=[square, CORNER, CORNER, turned],
         scratch_shapes=LAYER_SCRATCH,
-        compiler_params=FIRST_PARAMS,
-    )(edge_count, node_feat, *halo(c0, c1), w_qkv, w_edge, gains, index, source, target, edge_feat)
+        compiler_params=PARAMS,
+    )(edge_count, node_feat, *halo(c0, c1), w_qkv, gains, source, target, own, part, edges, index)
+    own, part = own_second(nodes, edges)
     nodes, grads = pl.pallas_call(
         functools.partial(second_kernel, scale=scale),
         grid=(blocks,),
-        in_specs=layer_specs(1) + [
-            whole(256, 256), whole(169, 256), ROWS, ROWS, EDGES_T, pl.BlockSpec((169, BLOCK), lambda i: (0, i)),
-        ],
+        in_specs=layer_specs(1) + [whole(256, 256), whole(169, 256), pl.BlockSpec((169, BLOCK), lambda i: (0, i))],
         out_specs=[whole(256, 256), whole(128, 8, 128)],
-        out_shape=[jax.ShapeDtypeStruct((256, 256), BF), jax.ShapeDtypeStruct((128, 8, 128), F32)],
+        out_shape=[square, jax.ShapeDtypeStruct((128, 8, 128), F32)],
         scratch_shapes=LAYER_SCRATCH + [
             pltpu.VMEM((256, 256), BF), pltpu.VMEM((256, 169), BF), pltpu.VMEM((256, BLOCK), BF),
             pltpu.VMEM((256, BLOCK), BF), pltpu.VMEM((256, BLOCK), BF), pltpu.VMEM((169, BLOCK), BF),
@@ -276,7 +382,7 @@
         ],
         compiler_params=PARAMS,
     )(
-        edge_count, nodes, *halo(c0, c1), w_qkv, w_edge, gains, head_in, head_out.T, source, target, edges, targets,
+        edge_count, nodes, *halo(c0, c1), w_qkv, gains, source, target, own, part, edges, head_in, head_out.T, targets,
     )
     parts = lax.all_to_all(grads, AXES, 0, 0, tiled=True)
     share = jnp.sum(parts, axis=0)

time: 120 us -> 107 us (0.89)
  Pallas kernels: 32.1 us -> 23.2 us
  local copies, waits for them, and re-layouts: 7.64 us -> 1.5 us
  blocking collectives: 49.6 us -> 55 us
  waiting for transfers between devices: 6.99 us -> 2.67 us
  starting transfers between devices: 21.7 us -> 24 us
    pallas_call x1, Pallas kernels: 13.3 us -> 5.87 us  [body(): pl.pallas_call(first_kernel, grid=(blocks,), in_specs=layer_specs(0) + [w...]
    pallas_call x1, Pallas kernels: 16.9 us -> 10.1 us  [body(): pl.pallas_call(functools.partial(second_kernel, scale=scale), grid=(block...]
    all_to_all x1, blocking collectives: 32 us -> 37.4 us  [body(): parts = lax.all_to_all(grads, AXES, 0, 0, tiled=True)]
    pallas_call x1 -> x5, Pallas kernels: 1.88 us -> 7.24 us  [the longest x1 3.67 us: own_first(): pl.pallas_call(own_first_kernel, grid=(blocks,), in_specs=[SCALAR] + [sta...]
    ppermute x8, waiting for transfers between devices: 6.99 us -> 2.67 us  [both(): return (lax.ppermute(high, axis, up), lax.ppermute(low, axis, down))]
    unnamed x28 -> x20, local copies, waits for them, and re-layouts: 3.79 us -> 0.04 us
    slice x7 -> x0, local copies, waits for them, and re-layouts: 2.4 us -> none  [the longest x2 1.59 us: halo(): c0[j]]
    ppermute x8, starting transfers between devices: 21.7 us -> 24 us  [both(): return (lax.ppermute(high, axis, up), lax.ppermute(low, axis, down))]
  transfers between devices with their start and end apart: 8 -> 8, of which waited for: 6 -> 3; matrix products, arithmetic and copies ran while one was open for 1% -> 0% of each run, Pallas kernels for 0% -> 6%
where the time goes in v3:
time: 107 us; the launch traced here: 108 us
  blocking collectives  55 us (51%)
  starting transfers between devices  24 us (22%)
  Pallas kernels  23.2 us (22%)
  waiting for transfers between devices  2.67 us (2%)
  local copies, waits for them, and re-layouts  1.5 us (1%)
  between operations  1.45 us (1%)
    all_to_all x1, blocking collectives, body(): parts = lax.all_to_all(grads, AXES, 0, 0, tiled=True)  37.4 us
    ppermute x8, starting transfers between devices, both(): return (lax.ppermute(high, axis, up), lax.ppermute(low, axis, down))  24 us
    all_to_all x1, blocking collectives, body(): lax.all_to_all(jnp.broadcast_to(share[None], (128, 8, 128)), AXES, 0, 0,...  17.6 us
    pallas_call x1, Pallas kernels, body(): pl.pallas_call(functools.partial(second_kernel, scale=scale), grid=(block...  10.1 us
    pallas_call x1, Pallas kernels, body(): pl.pallas_call(first_kernel, grid=(blocks,), in_specs=layer_specs(0) + [w...  5.87 us
    pallas_call x1, Pallas kernels, own_first(): pl.pallas_call(own_first_kernel, grid=(blocks,), in_specs=[SCALAR] + [sta...  3.67 us
    ppermute x8, waiting for transfers between devices, both(): return (lax.ppermute(high, axis, up), lax.ppermute(low, axis, down))  2.67 us
    pallas_call x1, Pallas kernels, own_second(): pl.pallas_call(own_kernel, grid=(blocks,), in_specs=[SCALAR, whole(256, 2...  2.38 us
  transfers between devices with their start and end apart: 8, of which 3 were waited for; matrix products, arithmetic and copies ran while one was open for 0% of the time, Pallas kernels for 6%

profile of v3, /device:TPU:1, one launch (start us, length us, event | category | flops | bytes accessed | tf_op | source)
XLA Modules:
  0.0 107.9 jit_solution(3365202288392002731)
XLA Ops:
  0.6 1.2 %shard_map.139 = (bf16[2,64,256]{2,1,0:T(8,128)(2,1)S(1)}, bf16[2,64,256]{2,1,0:T(8,128)(2,1)S(1)}) custom-call(bf16[256,256]{1,0:T(8,128)(2,1)} %nodes_ref.3, s32[2,2,64]{2,1,0:T(2,128)} %bitcast.25), custom_call_target="tpu_custom_call" | custom-call | tf_op jit(solution)/shard_map/pallas_call | solution.py:359
  1.8 3.8 %collective-permute-start = (bf16[2,64,256]{2,1,0:T(8,128)(2,1)S(1)}, bf16[2,64,256]{2,1,0:T(8,128)(2,1)S(1)}, u32[]{:S(2)}, u32[]{:S(2)}) collective-permute-start(bf16[2,64,256]{2,1,0:T(8,128)(2,1)S(1)} %get-tuple-element.21.c1_ref), channel_id=1, source_target_pairs={{0,4},{4,8},{8,12},{12,16},{16,20},{20,24},{24,28},{28,0},{1,5},{5... | collective-permute-start | bytes 196616 | tf_op jit(solution)/shard_map/ppermute | solution.py:310
  5.6 3.6 %collective-permute-start.1 = (bf16[2,64,256]{2,1,0:T(8,128)(2,1)S(1)}, bf16[2,64,256]{2,1,0:T(8,128)(2,1)S(1)}, u32[]{:S(2)}, u32[]{:S(2)}) collective-permute-start(bf16[2,64,256]{2,1,0:T(8,128)(2,1)S(1)} %get-tuple-element.22.c0_ref), channel_id=1, source_target_pairs={{4,0},{8,4},{12,8},{16,12},{20,16},{24,20},{28,24},{0,28},{5,1},{9... | collective-permute-start | bytes 196616 | tf_op jit(solution)/shard_map/ppermute | solution.py:310
  9.8 0.9 collective-permute-done.before_ref
  10.7 0.0 collective-permute-done.1.after_ref
  10.8 1.3 %collective-permute-start.2 = (bf16[4,64,256]{2,1,0:T(8,128)(2,1)S(1)}, bf16[4,64,256]{2,1,0:T(8,128)(2,1)S(1)}, u32[]{:S(2)}, u32[]{:S(2)}) collective-permute-start(bf16[4,64,256]{2,1,0:T(8,128)(2,1)S(1)} %get-tuple-element.23), channel_id=1, source_target_pairs={{0,1},{1,2},{2,3},{3,0},{4,5},{5,6},{6,7},{7,4},{8,9},{9,10},{10,1... | collective-permute-start | bytes 393224 | tf_op jit(solution)/shard_map/ppermute | solution.py:310
  12.0 1.5 %collective-permute-start.3 = (bf16[4,64,256]{2,1,0:T(8,128)(2,1)S(1)}, bf16[4,64,256]{2,1,0:T(8,128)(2,1)S(1)}, u32[]{:S(2)}, u32[]{:S(2)}) collective-permute-start(bf16[4,64,256]{2,1,0:T(8,128)(2,1)S(1)} %get-tuple-element.24), channel_id=1, source_target_pairs={{1,0},{2,1},{3,2},{0,3},{5,4},{6,5},{7,6},{4,7},{9,8},{10,9},{11,1... | collective-permute-start | bytes 393224 | tf_op jit(solution)/shard_map/ppermute | solution.py:310
  13.5 0.0 copy-start.7
  13.5 0.0 copy-start.8
  13.5 3.7 %shard_map.141 = (bf16[4,256,2048]{2,1,0:T(8,128)(2,1)S(1)}, f32[4,256,2048]{2,1,0:T(8,128)S(1)}, bf16[4,256,2048]{2,1,0:T(8,128)(2,1)S(1)}) custom-call(s32[1]{0:T(128)S(6)} %copy.15.count_ref, bf16[256,256]{1,0:T(8,128)(2,1)} %nodes_ref.3, bf16[2,256,768]{2,1,0:T(8,128)(2,1)} %wqkv_ref.5, bf16[2,256,256]{2,1,0:T(8,128)(2,1)} %wedge_ref.1, ...), custom_call_target="tpu_custom_call" | custom-call | flops 3221225472 | bytes 25165824 | tf_op jit(solution)/shard_map/pallas_call | solution.py:335
  17.2 0.0 collective-permute-done.2.low_ref
  17.2 0.0 collective-permute-done.3.high_ref
  17.2 0.0 copy-done
  17.2 0.0 copy-done.2
  17.3 0.0 copy-done.4
  17.3 0.0 copy-start.9
  17.3 5.9 %shard_map.142 = (bf16[256,256]{1,0:T(8,128)(2,1)S(1)}, bf16[2,64,256]{2,1,0:T(8,128)(2,1)S(1)}, bf16[2,64,256]{2,1,0:T(8,128)(2,1)S(1)}, bf16[4,256,2048]{2,1,0:T(8,128)(2,1)S(1)}) custom-call(s32[1]{0:T(128)S(6)} %copy.15.count_ref, bf16[256,256]{1,0:T(8,128)(2,1)S(1)} %copy-done.2, bf16[2,64,256]{2,1,0:T(8,128)(2,1)S(1)} %collective-permute-done.before_ref, ...), custom_call_target="tpu_custom_call" | custom-call | tf_op jit(solution)/shard_map/pallas_call | solution.py:362
  23.2 2.4 %collective-permute-start.4 = (bf16[2,64,256]{2,1,0:T(8,128)(2,1)S(1)}, bf16[2,64,256]{2,1,0:T(8,128)(2,1)S(1)}, u32[]{:S(2)}, u32[]{:S(2)}) collective-permute-start(bf16[2,64,256]{2,1,0:T(8,128)(2,1)S(1)} %get-tuple-element.30.c1_ref), channel_id=1, source_target_pairs={{0,4},{4,8},{8,12},{12,16},{16,20},{20,24},{24,28},{28,0},{1,5},{5... | collective-permute-start | bytes 196616 | tf_op jit(solution)/shard_map/ppermute | solution.py:310
  25.6 6.4 %collective-permute-start.5 = (bf16[2,64,256]{2,1,0:T(8,128)(2,1)S(1)}, bf16[2,64,256]{2,1,0:T(8,128)(2,1)S(1)}, u32[]{:S(2)}, u32[]{:S(2)}) collective-permute-start(bf16[2,64,256]{2,1,0:T(8,128)(2,1)S(1)} %get-tuple-element.31.c0_ref), channel_id=1, source_target_pairs={{4,0},{8,4},{12,8},{16,12},{20,16},{24,20},{28,24},{0,28},{5,1},{9... | collective-permute-start | bytes 196616 | tf_op jit(solution)/shard_map/ppermute | solution.py:310
  32.0 1.6 %collective-permute-done.4.before_ref = bf16[2,64,256]{2,1,0:T(8,128)(2,1)S(1)} collective-permute-done((bf16[2,64,256]{2,1,0:T(8,128)(2,1)S(1)}, bf16[2,64,256]{2,1,0:T(8,128)(2,1)S(1)}, u32[]{:S(2)}, u32[]{:S(2)}) %collective-permute-start.4) | collective-permute-done | bytes 65568 | tf_op jit(solution)/shard_map/ppermute | solution.py:310
  33.6 0.0 collective-permute-done.5.after_ref
  33.6 3.8 %collective-permute-start.6 = (bf16[4,64,256]{2,1,0:T(8,128)(2,1)S(1)}, bf16[4,64,256]{2,1,0:T(8,128)(2,1)S(1)}, u32[]{:S(2)}, u32[]{:S(2)}) collective-permute-start(bf16[4,64,256]{2,1,0:T(8,128)(2,1)S(1)} %get-tuple-element.32), channel_id=1, source_target_pairs={{0,1},{1,2},{2,3},{3,0},{4,5},{5,6},{6,7},{7,4},{8,9},{9,10},{10,1... | collective-permute-start | bytes 393224 | tf_op jit(solution)/shard_map/ppermute | solution.py:310
  37.4 1.2 %collective-permute-start.7 = (bf16[4,64,256]{2,1,0:T(8,128)(2,1)S(1)}, bf16[4,64,256]{2,1,0:T(8,128)(2,1)S(1)}, u32[]{:S(2)}, u32[]{:S(2)}) collective-permute-start(bf16[4,64,256]{2,1,0:T(8,128)(2,1)S(1)} %get-tuple-element.33), channel_id=1, source_target_pairs={{1,0},{2,1},{3,2},{0,3},{5,4},{6,5},{7,6},{4,7},{9,8},{10,9},{11,1... | collective-permute-start | bytes 393224 | tf_op jit(solution)/shard_map/ppermute | solution.py:310
  38.7 2.4 %shard_map.144 = (bf16[4,256,2048]{2,1,0:T(8,128)(2,1)S(1)}, f32[4,256,2048]{2,1,0:T(8,128)S(1)}) custom-call(s32[1]{0:T(128)S(6)} %copy.15.count_ref, bf16[256,256]{1,0:T(8,128)(2,1)S(1)} %get-tuple-element.29.nodes_ref, bf16[2,256,768]{2,1,0:T(8,128)(2,1)S(1)} %copy-done, bf16[2,256,256]{2,1,0:T(8,128)(2,1)S(1)} %copy-done.9, s32[4,1,2048]{2,1,0:T(1,128)S(1)} %bitcast.18, ...), custom_call_target="tpu_custom_call" | custom-call | flops 3221225472 | bytes 25165824 | tf_op jit(solution)/shard_map/pallas_call | solution.py:348
  41.1 0.0 collective-permute-done.6.low_ref
  41.1 0.2 collective-permute-done.7.high_ref
  41.2 10.1 %shard_map.145 = (bf16[256,256]{1,0:T(8,128)(2,1)}, f32[128,8,128]{2,1,0:T(8,128)S(1)}) custom-call(s32[1]{0:T(128)S(6)} %copy.15.count_ref, bf16[256,256]{1,0:T(8,128)(2,1)S(1)} %get-tuple-element.29.nodes_ref, bf16[2,64,256]{2,1,0:T(8,128)(2,1)S(1)} %collective-permute-done.4.before_ref, bf16[2,64,256]{2,1,0:T(8,128)(2,1)S(1)} %collective-permute-done.5.after_ref, ...), custom_call_target="tpu_custom_call" | custom-call | tf_op jit(solution)/shard_map/pallas_call | solution.py:372
  51.3 37.4 %all_to_all.10 = f32[128,8,128]{2,1,0:T(8,128)S(1)} all-to-all(f32[128,8,128]{2,1,0:T(8,128)S(1)} %get-tuple-element.38), channel_id=1, replica_groups=mesh['rep'=4,'gx'=8,'gy'=4] {'rep','gx','gy'}, dimensions={0} | all-to-all | bytes 1048576 | tf_op jit(solution)/shard_map/all_to_all | solution.py:387
  88.7 0.1 reduce_sum.9
  88.9 17.6 %all_to_all.11 = f32[128,8,128]{2,1,0:T(8,128)S(1)} all-to-all(f32[128,8,128]{2,1,0:T(8,128)S(1)} %broadcast_in_dim.2), channel_id=1, replica_groups=mesh['rep'=4,'gx'=8,'gy'=4] {'rep','gx','gy'}, dimensions={0} | all-to-all | bytes 1048576 | tf_op jit(solution)/shard_map/all_to_all | solution.py:389
  106.5 0.7 slice_bitcast_fusion
  107.2 0.7 slice.12
  (18 shorter events, 0.1 us)
Async XLA Ops:
  1.8 8.9 %collective-permute-start = (bf16[2,64,256]{2,1,0:T(8,128)(2,1)S(1)}, bf16[2,64,256]{2,1,0:T(8,128)(2,1)S(1)}, u32[]{:S(2)}, u32[]{:S(2)}) collective-permute-start(bf16[2,64,256]{2,1,0:T(8,128)(2,1)S(1)} %get-tuple-element.21.c1_ref), channel_id=1, source_target_pairs={{0,4},{4,8},{8,12},{12,16},{16,20},{20,24},{24,28},{28,0},{1,5},{5... | collective-permute-start | bytes 196616 | tf_op jit(solution)/shard_map/ppermute | solution.py:310
  5.6 5.1 %collective-permute-start.1 = (bf16[2,64,256]{2,1,0:T(8,128)(2,1)S(1)}, bf16[2,64,256]{2,1,0:T(8,128)(2,1)S(1)}, u32[]{:S(2)}, u32[]{:S(2)}) collective-permute-start(bf16[2,64,256]{2,1,0:T(8,128)(2,1)S(1)} %get-tuple-element.22.c0_ref), channel_id=1, source_target_pairs={{4,0},{8,4},{12,8},{16,12},{20,16},{24,20},{28,24},{0,28},{5,1},{9... | collective-permute-start | bytes 196616 | tf_op jit(solution)/shard_map/ppermute | solution.py:310
  10.8 6.5 %collective-permute-start.2 = (bf16[4,64,256]{2,1,0:T(8,128)(2,1)S(1)}, bf16[4,64,256]{2,1,0:T(8,128)(2,1)S(1)}, u32[]{:S(2)}, u32[]{:S(2)}) collective-permute-start(bf16[4,64,256]{2,1,0:T(8,128)(2,1)S(1)} %get-tuple-element.23), channel_id=1, source_target_pairs={{0,1},{1,2},{2,3},{3,0},{4,5},{5,6},{6,7},{7,4},{8,9},{9,10},{10,1... | collective-permute-start | bytes 393224 | tf_op jit(solution)/shard_map/ppermute | solution.py:310
  12.0 5.2 %collective-permute-start.3 = (bf16[4,64,256]{2,1,0:T(8,128)(2,1)S(1)}, bf16[4,64,256]{2,1,0:T(8,128)(2,1)S(1)}, u32[]{:S(2)}, u32[]{:S(2)}) collective-permute-start(bf16[4,64,256]{2,1,0:T(8,128)(2,1)S(1)} %get-tuple-element.24), channel_id=1, source_target_pairs={{1,0},{2,1},{3,2},{0,3},{5,4},{6,5},{7,6},{4,7},{9,8},{10,9},{11,1... | collective-permute-start | bytes 393224 | tf_op jit(solution)/shard_map/ppermute | solution.py:310
  13.5 3.7 %copy-start = (bf16[2,256,768]{2,1,0:T(8,128)(2,1)S(1)}, bf16[2,256,768]{2,1,0:T(8,128)(2,1)}, u32[]{:S(2)}) copy-start(bf16[2,256,768]{2,1,0:T(8,128)(2,1)} %wqkv_ref.5) | copy-start | bytes 2359300
  13.5 3.7 %copy-start.2 = (bf16[256,256]{1,0:T(8,128)(2,1)S(1)}, bf16[256,256]{1,0:T(8,128)(2,1)}, u32[]{:S(2)}) copy-start(bf16[256,256]{1,0:T(8,128)(2,1)} %nodes_ref.3) | copy-start | bytes 393220
  13.5 3.8 %copy-start.4 = (s32[8192]{0:T(1024)S(1)}, s32[8192]{0:T(1024)}, u32[]{:S(2)}) copy-start(s32[8192]{0:T(1024)} %param.14) | copy-start | bytes 98308
  13.5 3.8 %copy-start.5 = (s32[8192]{0:T(1024)S(1)}, s32[8192]{0:T(1024)}, u32[]{:S(2)}) copy-start(s32[8192]{0:T(1024)} %param.15) | copy-start | bytes 98308
  13.5 3.8 %copy-start.7 = (s32[1,1,1,2,2,64]{5,4,3,2,1,0:T(2,128)S(1)}, s32[1,1,1,2,2,64]{5,4,3,2,1,0:T(2,128)}, u32[]{:S(2)}) copy-start(s32[1,1,1,2,2,64]{5,4,3,2,1,0:T(2,128)} %param.17) | copy-start | bytes 3076
  13.5 3.8 %copy-start.8 = (f32[2,256]{1,0:T(2,128)S(1)}, f32[2,256]{1,0:T(2,128)}, u32[]{:S(2)}) copy-start(f32[2,256]{1,0:T(2,128)} %gain_ref.3) | copy-start | bytes 6148
  17.3 21.4 %copy-start.9 = (bf16[2,256,256]{2,1,0:T(8,128)(2,1)S(1)}, bf16[2,256,256]{2,1,0:T(8,128)(2,1)}, u32[]{:S(2)}) copy-start(bf16[2,256,256]{2,1,0:T(8,128)(2,1)} %wedge_ref.1) | copy-start | bytes 786436
  23.2 10.4 %collective-permute-start.4 = (bf16[2,64,256]{2,1,0:T(8,128)(2,1)S(1)}, bf16[2,64,256]{2,1,0:T(8,128)(2,1)S(1)}, u32[]{:S(2)}, u32[]{:S(2)}) collective-permute-start(bf16[2,64,256]{2,1,0:T(8,128)(2,1)S(1)} %get-tuple-element.30.c1_ref), channel_id=1, source_target_pairs={{0,4},{4,8},{8,12},{12,16},{16,20},{20,24},{24,28},{28,0},{1,5},{5... | collective-permute-start | bytes 196616 | tf_op jit(solution)/shard_map/ppermute | solution.py:310
  25.6 8.0 %collective-permute-start.5 = (bf16[2,64,256]{2,1,0:T(8,128)(2,1)S(1)}, bf16[2,64,256]{2,1,0:T(8,128)(2,1)S(1)}, u32[]{:S(2)}, u32[]{:S(2)}) collective-permute-start(bf16[2,64,256]{2,1,0:T(8,128)(2,1)S(1)} %get-tuple-element.31.c0_ref), channel_id=1, source_target_pairs={{4,0},{8,4},{12,8},{16,12},{20,16},{24,20},{28,24},{0,28},{5,1},{9... | collective-permute-start | bytes 196616 | tf_op jit(solution)/shard_map/ppermute | solution.py:310
  33.6 7.5 %collective-permute-start.6 = (bf16[4,64,256]{2,1,0:T(8,128)(2,1)S(1)}, bf16[4,64,256]{2,1,0:T(8,128)(2,1)S(1)}, u32[]{:S(2)}, u32[]{:S(2)}) collective-permute-start(bf16[4,64,256]{2,1,0:T(8,128)(2,1)S(1)} %get-tuple-element.32), channel_id=1, source_target_pairs={{0,1},{1,2},{2,3},{3,0},{4,5},{5,6},{6,7},{7,4},{8,9},{9,10},{10,1... | collective-permute-start | bytes 393224 | tf_op jit(solution)/shard_map/ppermute | solution.py:310
  37.4 3.8 %collective-permute-start.7 = (bf16[4,64,256]{2,1,0:T(8,128)(2,1)S(1)}, bf16[4,64,256]{2,1,0:T(8,128)(2,1)S(1)}, u32[]{:S(2)}, u32[]{:S(2)}) collective-permute-start(bf16[4,64,256]{2,1,0:T(8,128)(2,1)S(1)} %get-tuple-element.33), channel_id=1, source_target_pairs={{1,0},{2,1},{3,2},{0,3},{5,4},{6,5},{7,6},{4,7},{9,8},{10,9},{11,1... | collective-permute-start | bytes 393224 | tf_op jit(solution)/shard_map/ppermute | solution.py:310
  38.7 2.6 %copy-start.1 = (bf16[169,8192]{1,0:T(8,128)(2,1)S(1)}, bf16[169,8192]{1,0:T(8,128)(2,1)}, u32[]{:S(2)}) copy-start(bf16[169,8192]{1,0:T(8,128)(2,1)} %goal_ref.1) | copy-start | bytes 8306692
  38.7 2.6 %copy-start.3 = (bf16[256,256]{1,0:T(8,128)(2,1)S(1)}, bf16[256,256]{1,0:T(8,128)(2,1)}, u32[]{:S(2)}) copy-start(bf16[256,256]{1,0:T(8,128)(2,1)} %hin_ref.1) | copy-start | bytes 393220
  38.7 2.6 %copy-start.6 = (bf16[256,169]{0,1:T(8,128)(2,1)S(1)}, bf16[256,169]{0,1:T(8,128)(2,1)}, u32[]{:S(2)}) copy-start(bf16[256,169]{0,1:T(8,128)(2,1)} %param.22) | copy-start | bytes 259588

commit v4 on v3

v4 whole, which is shorter than its diff:
```python
import functools

import jax
import jax.numpy as jnp
from jax import lax
from jax.experimental import pallas as pl
from jax.experimental.pallas import tpu as pltpu
from jax.sharding import Mesh
from jax.sharding import PartitionSpec as P

AXES = ("pair", "core", "gx", "gy")
BF = jnp.bfloat16
F32 = jnp.float32
BLOCK = 2048
SUB = 256
LAGS = (1, 1, 1)
VMEM_MIB = 28


def nn(a, b):
    return jnp.dot(a, b, preferred_element_type=F32)


def nt(a, b):
    return lax.dot_general(a, b, (((1,), (1,)), ((), ())), preferred_element_type=F32)


def tn(a, b):
    return lax.dot_general(a, b, (((0,), (0,)), ((), ())), preferred_element_type=F32)


def hot(row, base, rows):
    index = lax.broadcasted_iota(jnp.int16, (rows, row.shape[1]), 0)
    same = index == (row - base).astype(jnp.int16)
    return jnp.where(same, jnp.ones((), BF), jnp.zeros((), BF))


def sigmoid(x):
    return 0.5 * jnp.tanh(0.5 * x) + 0.5


def pick_corners(nodes, index_ref, c0_ref, c1_ref):
    for i, out_ref in enumerate((c0_ref, c1_ref)):
        for j in range(2):
            out_ref[j] = tn(hot(index_ref[i, j : j + 1, :], 0, 256), nodes).astype(BF)


def corner_kernel(nodes_ref, index_ref, c0_ref, c1_ref):
    pick_corners(nodes_ref[...], index_ref, c0_ref, c1_ref)


def stack_kernel(before_ref, after_ref, c0_ref, c1_ref, low_ref, high_ref):
    for j, out_ref in enumerate((low_ref, high_ref)):
        for i, cell_ref in enumerate((before_ref, c0_ref, c1_ref, after_ref)):
            out_ref[i] = cell_ref[j]


def prepare_own(nodes, wqkv, wedge, wqe_t):
    wqe_t[:, 0:256] = nn(nodes[...], wqkv[:, 0:256]).astype(BF).T
    wqe_t[:, 256:512] = wedge[...].T


def near_hot(source):
    return jnp.concatenate([hot(source, 0, 256), hot(source, 320, 128), hot(source, 832, 128)], axis=0)


def far_hot(source):
    return jnp.concatenate([hot(source, 256, 64), hot(source, 448, 384), hot(source, 960, 64)], axis=0)


def prepare_far(low_ref, high_ref, wqkv_ref, far_t, wkv_t):
    for k in range(2):
        cells = [low_ref[2 * k], high_ref[2 * k], low_ref[2 * k + 1], high_ref[2 * k + 1]]
        far_t[:, 256 * k : 256 * (k + 1)] = jnp.concatenate(cells, axis=0).T
    wkv_t[...] = wqkv_ref[:, 256:].T


def new_nodes(nodes_ref, acc, gain):
    summed = (acc[0:256, :] + acc[256:512, :]).T
    centre = summed - jnp.mean(summed, axis=-1, keepdims=True)
    spread = jnp.mean(centre * centre, axis=-1, keepdims=True)
    normed = centre * lax.rsqrt(spread + 1e-05)
    return (nodes_ref[...].astype(F32) + gain * normed).astype(BF)


def staged(stages):
    parts = BLOCK // SUB
    held = [{} for _ in range(parts)]
    lag = 0
    lags = [lag := lag + step for _, step in stages]
    for tick in range(parts + lag):
        for (stage, _), late in zip(stages, lags):
            j = tick - late
            if 0 <= j < parts:
                stage(held[j], slice(j * SUB, (j + 1) * SUB), j * SUB)


def part_of(target, edges, wqe_t):
    return nn(wqe_t[...], jnp.concatenate([hot(target, 0, 256), edges], axis=0))


def near_tables(nodes, before_ref, after_ref, near_t):
    near_t[:, 0:256] = nodes[...].T
    cells = [before_ref[0], before_ref[1], after_ref[0], after_ref[1]]
    near_t[:, 256:512] = jnp.concatenate(cells, axis=0).T


def first_part_kernel(
    count_ref, before_ref, after_ref, nodes_hbm, wqkv_hbm, wedge_hbm, src_hbm, dst_hbm, edge_hbm,
    near_ref, part_ref, turned_ref,
    near_t, wqe_t, nodes, wqkv, wedge, src, dst, edge, sems,
):
    step = pl.program_id(0)
    steps = edge.shape[0]
    small = [
        pltpu.make_async_copy(nodes_hbm, nodes, sems.at[0]),
        pltpu.make_async_copy(wqkv_hbm.at[0, :, pl.ds(0, 256)], wqkv, sems.at[1]),
        pltpu.make_async_copy(wedge_hbm.at[0], wedge, sems.at[2]),
        pltpu.make_async_copy(src_hbm, src, sems.at[3]),
        pltpu.make_async_copy(dst_hbm, dst, sems.at[4]),
    ]

    def edge_copy(i):
        return pltpu.make_async_copy(edge_hbm.at[pl.ds(i * BLOCK, BLOCK), :], edge.at[i], sems.at[5 + i])

    @pl.when(step == 0)
    def _():
        for copy in small:
            copy.start()
        for i in range(steps):
            edge_copy(i).start()
        for copy in small:
            copy.wait()
        prepare_own(nodes, wqkv, wedge, wqe_t)
        near_tables(nodes, before_ref, after_ref, near_t)

    edge_copy(step).wait()

    @pl.when(step * BLOCK < count_ref[0])
    def _():
        for j in range(BLOCK // SUB):
            at = slice(j * SUB, (j + 1) * SUB)
            near_ref[0, :, at] = nn(near_t[...], near_hot(src[step, :, at])).astype(BF)
            edges = edge[step, at, :].T
            turned_ref[0, :, at] = edges
            part_ref[0, :, at] = part_of(dst[step, :, at], edges, wqe_t)


def part_kernel(count_ref, nodes_ref, wqkv_ref, wedge_ref, dst_ref, edge_ref, part_ref, wqe_t):
    step = pl.program_id(0)

    @pl.when(step == 0)
    def _():
        prepare_own(nodes_ref, wqkv_ref, wedge_ref, wqe_t)

    @pl.when(step * BLOCK < count_ref[0])
    def _():
        for j in range(BLOCK // SUB):
            at = slice(j * SUB, (j + 1) * SUB)
            part_ref[0, :, at] = part_of(dst_ref[0, :, at], edge_ref[0, :, at], wqe_t)


def near_kernel(count_ref, nodes_ref, before_ref, after_ref, src_ref, near_ref, near_t):
    step = pl.program_id(0)

    @pl.when(step == 0)
    def _():
        near_tables(nodes_ref, before_ref, after_ref, near_t)

    @pl.when(step * BLOCK < count_ref[0])
    def _():
        for j in range(BLOCK // SUB):
            at = slice(j * SUB, (j + 1) * SUB)
            near_ref[0, :, at] = nn(near_t[...], near_hot(src_ref[0, :, at])).astype(BF)


def message_stages(first, count, src_ref, dst_ref, near_ref, part_ref, edge_ref, far_t, wkv_t, hl, target_hot, keep_edges):
    def gather(held, at, start):
        held["rows"] = nn(far_t[...], far_hot(src_ref[0, :, at])).astype(BF) + near_ref[0, :, at]

    def message(held, at, start):
        target = dst_ref[0, :, at]
        edges = edge_ref[0, :, at]
        kv = nn(wkv_t[...], held["rows"]).astype(BF).astype(F32)
        pre = part_ref[0, :, at] + kv[:256]
        gate = sigmoid(pre)
        held["edges"] = (edges.astype(F32) + pre * gate).astype(BF)
        keep_edges(at, held["edges"])
        weighted = gate * kv[256:]
        top = weighted.astype(BF)
        hl[0:256, at] = top
        hl[256:512, at] = (weighted - top.astype(F32)).astype(BF)
        held["live"] = first + start + lax.broadcasted_iota(jnp.int32, (1, SUB), 1) < count
        target_hot[:, at] = hot(jnp.where(held["live"], target, -1), 0, 256)

    return [(gather, 0), (message, 1)]


def first_kernel(
    count_ref, nodes_ref, low_ref, high_ref, wqkv_ref, gain_ref,
    src_ref, dst_ref, near_ref, part_ref, edge_ref, index_ref,
    out_nodes_ref, c0_ref, c1_ref, out_edge_ref,
    far_t, wkv_t, acc, hl, target_hot,
):
    step = pl.program_id(0)
    count = count_ref[0]

    @pl.when(step == 0)
    def _():
        prepare_far(low_ref, high_ref, wqkv_ref, far_t, wkv_t)
        acc[...] = jnp.zeros_like(acc)

    @pl.when(step * BLOCK < count)
    def _():
        def keep_edges(at, edges):
            out_edge_ref[0, :, at] = edges

        staged(
            message_stages(
                step * BLOCK, count, src_ref, dst_ref, near_ref, part_ref, edge_ref, far_t, wkv_t, hl, target_hot, keep_edges
            )
        )
        acc[...] += nt(hl[...], target_hot[...])

    @pl.when(step == pl.num_programs(0) - 1)
    def _():
        nodes = new_nodes(nodes_ref, acc, gain_ref[0:1, :])
        out_nodes_ref[...] = nodes
        pick_corners(nodes, index_ref, c0_ref, c1_ref)


def second_kernel(
    count_ref, nodes_ref, low_ref, high_ref, wqkv_ref, gain_ref,
    src_ref, dst_ref, near_ref, part_ref, edge_ref, core_ref, hin_ref, hout_ref, goal_ref,
    out_nodes_ref, keep_ref, send_ref,
    far_t, wkv_t, acc, hl, target_hot, hin_t, hout, edges_s, dact_s, hidden_s, dpred_s, grad_in, grad_out,
    *, scale,
):
    step = pl.program_id(0)
    count = count_ref[0]

    @pl.when(step == 0)
    def _():
        prepare_far(low_ref, high_ref, wqkv_ref, far_t, wkv_t)
        hin_t[...] = hin_ref[...].T
        hout[...] = hout_ref[...].T
        acc[...] = jnp.zeros_like(acc)
        grad_in[...] = jnp.zeros_like(grad_in)
        grad_out[...] = jnp.zeros_like(grad_out)

    @pl.when(step * BLOCK < count)
    def _():
        def keep_edges(at, edges):
            edges_s[:, at] = edges

        def activate(held, at, start):
            act = nn(hin_t[...], held["edges"])
            gate = sigmoid(act)
            smooth = act * gate
            held["hidden"] = smooth.astype(BF)
            hidden_s[:, at] = held["hidden"]
            held["slope"] = gate + smooth * (1.0 - gate)

        def compare(held, at, start):
            pred = nn(hout_ref[...], held["hidden"])
            weight = jnp.where(held["live"], scale, 0.0)
            held["dpred"] = ((pred - goal_ref[:, at].astype(F32)) * weight).astype(BF)
            dpred_s[:, at] = held["dpred"]

        def back(held, at, start):
            dact_s[:, at] = (nn(hout[...], held["dpred"]) * held["slope"]).astype(BF)

        staged(
            message_stages(
                step * BLOCK, count, src_ref, dst_ref, near_ref, part_ref, edge_ref, far_t, wkv_t, hl, target_hot, keep_edges
            )
            + [(activate, LAGS[0]), (compare, LAGS[1]), (back, LAGS[2])]
        )
        acc[...] += nt(hl[...], target_hot[...])
        grad_in[...] += nt(edges_s[...], dact_s[...])
        grad_out[0:169, :] += nt(dpred_s[...], hidden_s[...])

    @pl.when(step == pl.num_programs(0) - 1)
    def _():
        out_nodes_ref[...] = new_nodes(nodes_ref, acc, gain_ref[1:2, :])

        def tiles_to(total, rows, to_ref):
            for i in range(rows):
                for j in range(2):
                    to_ref[2 * i + j] = total[8 * i : 8 * i + 8, 128 * j : 128 * j + 128]
            if rows < 32:
                to_ref[2 * rows : 64] = jnp.zeros((64 - 2 * rows, 8, 128), F32)

        @pl.when(core_ref[0] == 0)
        def _():
            tiles_to(grad_in, 32, keep_ref)
            tiles_to(grad_out, 22, send_ref)

        @pl.when(core_ref[0] == 1)
        def _():
            tiles_to(grad_out, 22, keep_ref)
            tiles_to(grad_in, 32, send_ref)


def whole(*shape):
    return pl.BlockSpec(shape, lambda i: (0,) * len(shape))


def layer_of(layer, *shape):
    return pl.BlockSpec((None,) + shape, lambda i: (layer, 0, 0))


SCALAR = pl.BlockSpec(memory_space=pltpu.SMEM)
ROWS = pl.BlockSpec((1, 1, BLOCK), lambda i: (i, 0, 0))
TURNED = pl.BlockSpec((1, 256, BLOCK), lambda i: (i, 0, 0))


def layer_specs(layer):
    return [
        SCALAR, whole(256, 256), whole(4, 64, 256), whole(4, 64, 256),
        layer_of(layer, 256, 768), whole(2, 256), ROWS, ROWS, TURNED, TURNED, TURNED,
    ]


LAYER_SCRATCH = [
    pltpu.VMEM((256, 512), BF), pltpu.VMEM((512, 256), BF), pltpu.VMEM((512, 256), F32),
    pltpu.VMEM((512, BLOCK), BF), pltpu.VMEM((256, BLOCK), BF),
]
LIGHT = pltpu.CompilerParams(vmem_limit_bytes=16 * 2**20)
SMALL = pltpu.CompilerParams(vmem_limit_bytes=4 * 2**20)
PARAMS = pltpu.CompilerParams(vmem_limit_bytes=VMEM_MIB * 2**20)
CORNER = jax.ShapeDtypeStruct((2, 64, 256), BF)


def stays(*arrays):
    return [pltpu.with_memory_space_constraint(x, pltpu.HBM) for x in arrays]


def shift(low, high, axis):
    count = lax.axis_size(axis)
    up = [(i, (i + 1) % count) for i in range(count)]
    down = [(j, i) for i, j in up]
    return lax.ppermute(high, axis, up), lax.ppermute(low, axis, down)


def turn_sides(before, after, c0, c1):
    side = jax.ShapeDtypeStruct((4, 64, 256), BF)
    low, high = pl.pallas_call(stack_kernel, out_shape=[side, side], compiler_params=SMALL)(before, after, c0, c1)
    return shift(low, high, "gy")


def swap_cores(x):
    return lax.ppermute(x, "core", [(0, 1), (1, 0)])


def body(node_feat, edge_feat, edge_src, edge_dst, edge_count, send_idx, w_qkv, w_edge, gains, head_in, head_out, targets):
    slots = edge_feat.shape[0]
    blocks = slots // BLOCK
    scale = 0.125 / (slots * lax.axis_size(AXES)) ** 0.5
    index = send_idx.reshape(2, 2, 64)
    source = edge_src.reshape(blocks, 1, BLOCK)
    target = edge_dst.reshape(blocks, 1, BLOCK)

    turned = jax.ShapeDtypeStruct((blocks, 256, BLOCK), BF)
    wide = jax.ShapeDtypeStruct((blocks, 256, BLOCK), F32)
    square = jax.ShapeDtypeStruct((256, 256), BF)

    def cost(units):
        return pl.CostEstimate(flops=2 * units * slots * 65536, bytes_accessed=units * 6 * 2**20, transcendentals=0)

    def first_part(before, after):
        stay = pl.BlockSpec(memory_space=pltpu.HBM)
        index_rows = pltpu.VMEM((blocks, 1, BLOCK), jnp.int32)
        return pl.pallas_call(
            first_part_kernel,
            grid=(blocks,),
            in_specs=[SCALAR, whole(2, 64, 256), whole(2, 64, 256)] + [stay] * 6,
            out_specs=[TURNED] * 3,
            out_shape=[turned, wide, turned],
            scratch_shapes=[pltpu.VMEM((256, 512), BF)] * 2 + [pltpu.VMEM((256, 256), BF)] * 3
            + [index_rows, index_rows, pltpu.VMEM((blocks, BLOCK, 256), BF), pltpu.SemaphoreType.DMA((5 + blocks,))],
            compiler_params=PARAMS,
            cost_estimate=cost(4),
        )(edge_count, before, after, *stays(node_feat, w_qkv, w_edge, source, target, edge_feat))

    def second_part(nodes, edges):
        return pl.pallas_call(
            part_kernel,
            grid=(blocks,),
            in_specs=[SCALAR, whole(256, 256), layer_of(1, 256, 256), layer_of(1, 256, 256), ROWS, TURNED],
            out_specs=TURNED,
            out_shape=wide,
            scratch_shapes=[pltpu.VMEM((256, 512), BF)],
            compiler_params=LIGHT,
            cost_estimate=cost(2),
        )(edge_count, nodes, w_qkv, w_edge, target, edges)

    def near(nodes, before, after):
        return pl.pallas_call(
            near_kernel,
            grid=(blocks,),
            in_specs=[SCALAR, whole(256, 256), whole(2, 64, 256), whole(2, 64, 256), ROWS],
            out_specs=TURNED,
            out_shape=turned,
            scratch_shapes=[pltpu.VMEM((256, 512), BF)],
            compiler_params=LIGHT,
            cost_estimate=cost(2),
        )(edge_count, nodes, before, after, source)

    c0, c1 = pl.pallas_call(corner_kernel, out_shape=[CORNER, CORNER], compiler_params=SMALL)(*stays(node_feat, index))
    before, after = shift(c0, c1, "gx")
    low, high = turn_sides(before, after, c0, c1)
    rows, part, edges = first_part(before, after)
    nodes, c0, c1, edges = pl.pallas_call(
        first_kernel,
        grid=(blocks,),
        in_specs=layer_specs(0) + [whole(2, 2, 64)],
        out_specs=[whole(256, 256), whole(2, 64, 256), whole(2, 64, 256), TURNED],
        out_shape=[square, CORNER, CORNER, turned],
        scratch_shapes=LAYER_SCRATCH,
        compiler_params=PARAMS,
    )(edge_count, node_feat, low, high, w_qkv, gains, source, target, rows, part, edges, index)

    before, after = shift(c0, c1, "gx")
    part = second_part(nodes, edges)
    before, after, part = lax.optimization_barrier((before, after, part))
    low, high = turn_sides(before, after, c0, c1)
    rows = near(nodes, before, after)
    half = jax.ShapeDtypeStruct((64, 8, 128), F32)
    core = lax.axis_index("core")
    nodes, keep, send = pl.pallas_call(
        functools.partial(second_kernel, scale=scale),
        grid=(blocks,),
        in_specs=layer_specs(1) + [SCALAR, whole(256, 256), whole(169, 256), pl.BlockSpec((169, BLOCK), lambda i: (0, i))],
        out_specs=[whole(256, 256), whole(64, 8, 128), whole(64, 8, 128)],
        out_shape=[square, half, half],
        scratch_shapes=LAYER_SCRATCH + [
            pltpu.VMEM((256, 256), BF), pltpu.VMEM((256, 169), BF), pltpu.VMEM((256, BLOCK), BF),
            pltpu.VMEM((256, BLOCK), BF), pltpu.VMEM((256, BLOCK), BF), pltpu.VMEM((169, BLOCK), BF),
            pltpu.VMEM((256, 256), F32), pltpu.VMEM((176, 256), F32),
        ],
        compiler_params=PARAMS,
    )(
        edge_count, nodes, low, high, w_qkv, gains, source, target, rows, part, edges,
        core.astype(jnp.int32).reshape(1), head_in, head_out.T, targets,
    )
    chips = ("pair", "gx", "gy")
    parts = lax.all_to_all(keep + swap_cores(send), chips, 0, 0, tiled=True)
    share = jnp.sum(parts, axis=0)
    mine = lax.all_to_all(jnp.broadcast_to(share[None], (64, 8, 128)), chips, 0, 0, tiled=True)
    other = swap_cores(mine)
    grad_in = jnp.where(core == 0, mine, other)
    grad_out = jnp.where(core == 0, other, mine)[0:44]
    grad_in = grad_in.reshape(32, 2, 8, 128).transpose(0, 2, 1, 3).reshape(256, 256)
    grad_out = grad_out.reshape(22, 2, 8, 128).transpose(0, 2, 1, 3).reshape(176, 256)[0:169].T
    return nodes, grad_in, grad_out


def solution(mesh):
    shape = dict(mesh.shape)
    cut = Mesh(mesh.devices.reshape(shape["rep"] // 2, 2, shape["gx"], shape["gy"]), AXES)
    tile = P(AXES)
    return jax.shard_map(
        body,
        mesh=cut,
        in_specs=(
            P(AXES, None), P(AXES, None), tile, tile, tile, P(("pair", "core"), "gx", "gy", None, None, None),
            P(), P(), P(), P(), P(), P(None, AXES),
        ),
        out_specs=(P(AXES, None), P(), P()),
        check_vma=False,
    )
```

time: 107 us -> 109 us (1.019)
  blocking collectives: 55 us -> 38.8 us
  Pallas kernels: 23.2 us -> 35.2 us
  starting transfers between devices: 24 us -> 26.9 us
  waiting for transfers between devices: 2.67 us -> 5.32 us
    all_to_all x2, blocking collectives: 55 us -> 38.8 us  [the longest x1 24.5 us: body(): parts = lax.all_to_all(keep + swap_cores(send), chips, 0, 0, tiled=True)]
    pallas_call x4 -> x5, Pallas kernels: 6.09 us -> 10.4 us  [the longest x1 5.48 us: first_part(): pl.pallas_call(first_part_kernel, grid=(blocks,), in_specs=[SCALAR, whole...]
    pallas_call x1, Pallas kernels: 5.87 us -> 10.1 us  [body(): pl.pallas_call(first_kernel, grid=(blocks,), in_specs=layer_specs(0) + [w...]
    pallas_call x1, Pallas kernels: 10.1 us -> 13.6 us  [body(): pl.pallas_call(functools.partial(second_kernel, scale=scale), grid=(block...]
    ppermute x8 -> x10, starting transfers between devices: 24 us -> 26.9 us  [the longest x8 19.6 us: shift(): return (lax.ppermute(high, axis, up), lax.ppermute(low, axis, down))]
    ppermute x8 -> x10, waiting for transfers between devices: 2.67 us -> 5.32 us  [the longest x8 3 us: shift(): return (lax.ppermute(high, axis, up), lax.ppermute(low, axis, down))]
  transfers between devices with their start and end apart: 8 -> 10, of which waited for: 3 -> 4; matrix products, arithmetic and copies ran while one was open for 0% -> 0% of each run, Pallas kernels for 6% -> 9%
where the time goes in v4:
time: 109 us
  blocking collectives  38.8 us (36%)
  Pallas kernels  35.2 us (32%)
  starting transfers between devices  26.9 us (25%)
  waiting for transfers between devices  5.32 us (5%)
  between operations  1.51 us (1%)
    all_to_all x1, blocking collectives, body(): parts = lax.all_to_all(keep + swap_cores(send), chips, 0, 0, tiled=True)  24.5 us
    ppermute x8, starting transfers between devices, shift(): return (lax.ppermute(high, axis, up), lax.ppermute(low, axis, down))  19.6 us
    all_to_all x1, blocking collectives, body(): lax.all_to_all(jnp.broadcast_to(share[None], (64, 8, 128)), chips, 0, 0,...  14.2 us
    pallas_call x1, Pallas kernels, body(): pl.pallas_call(functools.partial(second_kernel, scale=scale), grid=(block...  13.6 us
    pallas_call x1, Pallas kernels, body(): pl.pallas_call(first_kernel, grid=(blocks,), in_specs=layer_specs(0) + [w...  10.1 us
    ppermute x2, starting transfers between devices, swap_cores(): return lax.ppermute(x, 'core', [(0, 1), (1, 0)])  7.31 us
    pallas_call x1, Pallas kernels, first_part(): pl.pallas_call(first_part_kernel, grid=(blocks,), in_specs=[SCALAR, whole...  5.48 us
    ppermute x8, waiting for transfers between devices, shift(): return (lax.ppermute(high, axis, up), lax.ppermute(low, axis, down))  3 us
  transfers between devices with their start and end apart: 10, of which 4 were waited for; matrix products, arithmetic and copies ran while one was open for 0% of the time, Pallas kernels for 9%

profile of v4, /device:TPU:1, one launch (start us, length us, event | category | flops | bytes accessed | tf_op | source)
XLA Modules:
  0.0 109.3 jit_solution(17726227804328737201)
XLA Ops:
  0.6 1.2 %shard_map.139 = (bf16[2,64,256]{2,1,0:T(8,128)(2,1)S(1)}, bf16[2,64,256]{2,1,0:T(8,128)(2,1)S(1)}) custom-call(bf16[256,256]{1,0:T(8,128)(2,1)} %nodes_ref.3, s32[2,2,64]{2,1,0:T(2,128)} %bitcast.26), custom_call_target="tpu_custom_call" | custom-call | tf_op jit(solution)/shard_map/pallas_call | solution.py:410
  1.8 3.8 %collective-permute-start = (bf16[2,64,256]{2,1,0:T(8,128)(2,1)S(1)}, bf16[2,64,256]{2,1,0:T(8,128)(2,1)S(1)}, u32[]{:S(2)}, u32[]{:S(2)}) collective-permute-start(bf16[2,64,256]{2,1,0:T(8,128)(2,1)S(1)} %get-tuple-element.22.c1_ref), channel_id=1, source_target_pairs={{0,4},{4,8},{8,12},{12,16},{16,20},{20,24},{24,28},{28,0},{1,5},{5... | collective-permute-start | bytes 196616 | tf_op jit(solution)/shard_map/ppermute | solution.py:343
  5.6 3.6 %collective-permute-start.1 = (bf16[2,64,256]{2,1,0:T(8,128)(2,1)S(1)}, bf16[2,64,256]{2,1,0:T(8,128)(2,1)S(1)}, u32[]{:S(2)}, u32[]{:S(2)}) collective-permute-start(bf16[2,64,256]{2,1,0:T(8,128)(2,1)S(1)} %get-tuple-element.23.c0_ref), channel_id=1, source_target_pairs={{4,0},{8,4},{12,8},{16,12},{20,16},{24,20},{28,24},{0,28},{5,1},{9... | collective-permute-start | bytes 196616 | tf_op jit(solution)/shard_map/ppermute | solution.py:343
  9.8 0.9 collective-permute-done.before_ref
  10.7 0.0 collective-permute-done.1.after_ref
  10.8 1.3 %collective-permute-start.2 = (bf16[4,64,256]{2,1,0:T(8,128)(2,1)S(1)}, bf16[4,64,256]{2,1,0:T(8,128)(2,1)S(1)}, u32[]{:S(2)}, u32[]{:S(2)}) collective-permute-start(bf16[4,64,256]{2,1,0:T(8,128)(2,1)S(1)} %get-tuple-element.24), channel_id=1, source_target_pairs={{0,1},{1,2},{2,3},{3,0},{4,5},{5,6},{6,7},{7,4},{8,9},{9,10},{10,1... | collective-permute-start | bytes 393224 | tf_op jit(solution)/shard_map/ppermute | solution.py:343
  12.0 1.5 %collective-permute-start.3 = (bf16[4,64,256]{2,1,0:T(8,128)(2,1)S(1)}, bf16[4,64,256]{2,1,0:T(8,128)(2,1)S(1)}, u32[]{:S(2)}, u32[]{:S(2)}) collective-permute-start(bf16[4,64,256]{2,1,0:T(8,128)(2,1)S(1)} %get-tuple-element.25), channel_id=1, source_target_pairs={{1,0},{2,1},{3,2},{0,3},{5,4},{6,5},{7,6},{4,7},{9,8},{10,9},{11,1... | collective-permute-start | bytes 393224 | tf_op jit(solution)/shard_map/ppermute | solution.py:343
  13.5 0.0 copy-start.8
  13.5 0.0 copy-start.9
  13.5 5.5 %shard_map.141 = (bf16[4,256,2048]{2,1,0:T(8,128)(2,1)S(1)}, f32[4,256,2048]{2,1,0:T(8,128)S(1)}, bf16[4,256,2048]{2,1,0:T(8,128)(2,1)S(1)}) custom-call(s32[1]{0:T(128)S(6)} %copy.15.count_ref, bf16[2,64,256]{2,1,0:T(8,128)(2,1)S(1)} %collective-permute-done.before_ref, bf16[2,64,256]{2,1,0:T(8,128)(2,1)S(1)} %collective-permute-done.1.after_ref, ...), custom_call_target="tpu_custom_call" | custom-call | flops 4294967296 | bytes 25165824 | tf_op jit(solution)/shard_map/pallas_call | solution.py:374
  19.1 0.0 copy-start.4
  19.1 10.1 %shard_map.142 = (bf16[256,256]{1,0:T(8,128)(2,1)S(1)}, bf16[2,64,256]{2,1,0:T(8,128)(2,1)S(1)}, bf16[2,64,256]{2,1,0:T(8,128)(2,1)S(1)}, bf16[4,256,2048]{2,1,0:T(8,128)(2,1)S(1)}) custom-call(s32[1]{0:T(128)S(6)} %copy.15.count_ref, bf16[256,256]{1,0:T(8,128)(2,1)S(1)} %copy-done.2, bf16[4,64,256]{2,1,0:T(8,128)(2,1)S(1)} %collective-permute-done.2.low_ref, ...), custom_call_target="tpu_custom_call" | custom-call | tf_op jit(solution)/shard_map/pallas_call | solution.py:414
  29.2 6.7 %collective-permute-start.4 = (bf16[2,64,256]{2,1,0:T(8,128)(2,1)S(1)}, bf16[2,64,256]{2,1,0:T(8,128)(2,1)S(1)}, u32[]{:S(2)}, u32[]{:S(2)}) collective-permute-start(bf16[2,64,256]{2,1,0:T(8,128)(2,1)S(1)} %get-tuple-element.30.c1_ref), channel_id=1, source_target_pairs={{0,4},{4,8},{8,12},{12,16},{16,20},{20,24},{24,28},{28,0},{1,5},{5... | collective-permute-start | bytes 196616 | tf_op jit(solution)/shard_map/ppermute | solution.py:343
  36.0 2.5 %shard_map.143.part_ref = f32[4,256,2048]{2,1,0:T(8,128)S(1)} custom-call(s32[1]{0:T(128)S(6)} %copy.15.count_ref, bf16[256,256]{1,0:T(8,128)(2,1)S(1)} %get-tuple-element.29.nodes_ref, bf16[2,256,768]{2,1,0:T(8,128)(2,1)S(1)} %copy-done, bf16[2,256,256]{2,1,0:T(8,128)(2,1)S(1)} %copy-done.4, s32[4,1,2048]{2,1,0:T(1,128)S(1)} %bitcast.19, ...), custom_call_target="tpu_custom_call" | custom-call | flops 2147483648 | bytes 12582912 | tf_op jit(solution)/shard_map/pallas_call | solution.py:387
  38.5 0.0 copy-start.1
  38.5 0.0 copy-start.5
  38.5 0.0 copy-start.7
  38.5 2.1 %collective-permute-done.5.after_ref = bf16[2,64,256]{2,1,0:T(8,128)(2,1)S(1)} collective-permute-done((bf16[2,64,256]{2,1,0:T(8,128)(2,1)S(1)}, bf16[2,64,256]{2,1,0:T(8,128)(2,1)S(1)}, u32[]{:S(2)}, u32[]{:S(2)}) %collective-permute-start.5) | collective-permute-done | bytes 65568 | tf_op jit(solution)/shard_map/ppermute | solution.py:343
  40.6 0.1 collective-permute-start.6
  40.7 2.7 %collective-permute-start.7 = (bf16[4,64,256]{2,1,0:T(8,128)(2,1)S(1)}, bf16[4,64,256]{2,1,0:T(8,128)(2,1)S(1)}, u32[]{:S(2)}, u32[]{:S(2)}) collective-permute-start(bf16[4,64,256]{2,1,0:T(8,128)(2,1)S(1)} %get-tuple-element.36), channel_id=1, source_target_pairs={{1,0},{2,1},{3,2},{0,3},{5,4},{6,5},{7,6},{4,7},{9,8},{10,9},{11,1... | collective-permute-start | bytes 393224 | tf_op jit(solution)/shard_map/ppermute | solution.py:343
  43.3 2.3 %shard_map.145.near_ref = bf16[4,256,2048]{2,1,0:T(8,128)(2,1)S(1)} custom-call(s32[1]{0:T(128)S(6)} %copy.15.count_ref, bf16[256,256]{1,0:T(8,128)(2,1)S(1)} %get-tuple-element.29.nodes_ref, bf16[2,64,256]{2,1,0:T(8,128)(2,1)S(1)} %collective-permute-done.4.before_ref, bf16[2,64,256]{2,1,0:T(8,128)(2,1)S(1)} %collective-permute-done.5.after_ref, ...), custom_call_target="tpu_custom_call" | custom-call | flops 2147483648 | bytes 12582912 | tf_op jit(solution)/shard_map/pallas_call | solution.py:399
  45.7 0.0 collective-permute-done.6.low_ref
  45.7 13.6 %shard_map.146 = (bf16[256,256]{1,0:T(8,128)(2,1)}, f32[64,8,128]{2,1,0:T(8,128)S(1)}, f32[64,8,128]{2,1,0:T(8,128)S(1)}) custom-call(s32[1]{0:T(128)S(6)} %copy.15.count_ref, bf16[256,256]{1,0:T(8,128)(2,1)S(1)} %get-tuple-element.29.nodes_ref, bf16[4,64,256]{2,1,0:T(8,128)(2,1)S(1)} %collective-permute-done.6.low_ref, ...), custom_call_target="tpu_custom_call" | custom-call | tf_op jit(solution)/shard_map/pallas_call | solution.py:431
  59.4 4.2 %collective-permute-start.8 = (f32[64,8,128]{2,1,0:T(8,128)S(1)}, f32[64,8,128]{2,1,0:T(8,128)S(1)}, u32[]{:S(2)}, u32[]{:S(2)}) collective-permute-start(f32[64,8,128]{2,1,0:T(8,128)S(1)} %get-tuple-element.40), channel_id=1, source_target_pairs={{0,32},{32,0},{1,33},{33,1},{2,34},{34,2},{3,35},{35,3},{4,36},{36... | collective-permute-start | bytes 786440 | tf_op jit(solution)/shard_map/ppermute | solution.py:353
  63.5 1.2 %collective-permute-done.8 = f32[64,8,128]{2,1,0:T(8,128)S(1)} collective-permute-done((f32[64,8,128]{2,1,0:T(8,128)S(1)}, f32[64,8,128]{2,1,0:T(8,128)S(1)}, u32[]{:S(2)}, u32[]{:S(2)}) %collective-permute-start.8) | collective-permute-done | bytes 262176 | tf_op jit(solution)/shard_map/ppermute | solution.py:353
  64.8 24.5 %all_to_all.10 = f32[64,8,128]{2,1,0:T(8,128)S(1)} all-to-all(f32[64,8,128]{2,1,0:T(8,128)S(1)} %add.3), channel_id=1, replica_groups=mesh['pair'=2,'core'=2,'gx'=8,'gy'=4] {'pair','gx','gy'}, dimensions={0} | all-to-all | bytes 524288 | tf_op jit(solution)/shard_map/all_to_all | solution.py:448
  89.3 0.1 reduce_sum.9
  89.4 14.2 %all_to_all.11 = f32[64,8,128]{2,1,0:T(8,128)S(1)} all-to-all(f32[64,8,128]{2,1,0:T(8,128)S(1)} %broadcast_in_dim.2), channel_id=1, replica_groups=mesh['pair'=2,'core'=2,'gx'=8,'gy'=4] {'pair','gx','gy'}, dimensions={0} | all-to-all | bytes 524288 | tf_op jit(solution)/shard_map/all_to_all | solution.py:450
  103.6 3.1 %collective-permute-start.9 = (f32[64,8,128]{2,1,0:T(8,128)S(1)}, f32[64,8,128]{2,1,0:T(8,128)S(1)}, u32[]{:S(2)}, u32[]{:S(2)}) collective-permute-start(f32[64,8,128]{2,1,0:T(8,128)S(1)} %all_to_all.11), channel_id=1, source_target_pairs={{0,32},{32,0},{1,33},{33,1},{2,34},{34,2},{3,35},{35,3},{4,36},{36... | collective-permute-start | bytes 786440 | tf_op jit(solution)/shard_map/ppermute | solution.py:353
  106.7 1.2 %collective-permute-done.9 = f32[64,8,128]{2,1,0:T(8,128)S(1)} collective-permute-done((f32[64,8,128]{2,1,0:T(8,128)S(1)}, f32[64,8,128]{2,1,0:T(8,128)S(1)}, u32[]{:S(2)}, u32[]{:S(2)}) %collective-permute-start.9) | collective-permute-done | bytes 262176 | tf_op jit(solution)/shard_map/ppermute | solution.py:353
  107.9 0.7 slice_bitcast_fusion
  108.6 0.7 broadcast_select_fusion
  (24 shorter events, 0.2 us)
Async XLA Ops:
  1.8 8.9 %collective-permute-start = (bf16[2,64,256]{2,1,0:T(8,128)(2,1)S(1)}, bf16[2,64,256]{2,1,0:T(8,128)(2,1)S(1)}, u32[]{:S(2)}, u32[]{:S(2)}) collective-permute-start(bf16[2,64,256]{2,1,0:T(8,128)(2,1)S(1)} %get-tuple-element.22.c1_ref), channel_id=1, source_target_pairs={{0,4},{4,8},{8,12},{12,16},{16,20},{20,24},{24,28},{28,0},{1,5},{5... | collective-permute-start | bytes 196616 | tf_op jit(solution)/shard_map/ppermute | solution.py:343
  5.6 5.1 %collective-permute-start.1 = (bf16[2,64,256]{2,1,0:T(8,128)(2,1)S(1)}, bf16[2,64,256]{2,1,0:T(8,128)(2,1)S(1)}, u32[]{:S(2)}, u32[]{:S(2)}) collective-permute-start(bf16[2,64,256]{2,1,0:T(8,128)(2,1)S(1)} %get-tuple-element.23.c0_ref), channel_id=1, source_target_pairs={{4,0},{8,4},{12,8},{16,12},{20,16},{24,20},{28,24},{0,28},{5,1},{9... | collective-permute-start | bytes 196616 | tf_op jit(solution)/shard_map/ppermute | solution.py:343
  10.8 8.3 %collective-permute-start.2 = (bf16[4,64,256]{2,1,0:T(8,128)(2,1)S(1)}, bf16[4,64,256]{2,1,0:T(8,128)(2,1)S(1)}, u32[]{:S(2)}, u32[]{:S(2)}) collective-permute-start(bf16[4,64,256]{2,1,0:T(8,128)(2,1)S(1)} %get-tuple-element.24), channel_id=1, source_target_pairs={{0,1},{1,2},{2,3},{3,0},{4,5},{5,6},{6,7},{7,4},{8,9},{9,10},{10,1... | collective-permute-start | bytes 393224 | tf_op jit(solution)/shard_map/ppermute | solution.py:343
  12.0 7.0 %collective-permute-start.3 = (bf16[4,64,256]{2,1,0:T(8,128)(2,1)S(1)}, bf16[4,64,256]{2,1,0:T(8,128)(2,1)S(1)}, u32[]{:S(2)}, u32[]{:S(2)}) collective-permute-start(bf16[4,64,256]{2,1,0:T(8,128)(2,1)S(1)} %get-tuple-element.25), channel_id=1, source_target_pairs={{1,0},{2,1},{3,2},{0,3},{5,4},{6,5},{7,6},{4,7},{9,8},{10,9},{11,1... | collective-permute-start | bytes 393224 | tf_op jit(solution)/shard_map/ppermute | solution.py:343
  13.5 5.5 %copy-start = (bf16[2,256,768]{2,1,0:T(8,128)(2,1)S(1)}, bf16[2,256,768]{2,1,0:T(8,128)(2,1)}, u32[]{:S(2)}) copy-start(bf16[2,256,768]{2,1,0:T(8,128)(2,1)} %wqkv_ref.5) | copy-start | bytes 2359300
  13.5 5.6 %copy-start.2 = (bf16[256,256]{1,0:T(8,128)(2,1)S(1)}, bf16[256,256]{1,0:T(8,128)(2,1)}, u32[]{:S(2)}) copy-start(bf16[256,256]{1,0:T(8,128)(2,1)} %nodes_ref.3) | copy-start | bytes 393220
  13.5 5.6 %copy-start.3 = (s32[8192]{0:T(1024)S(1)}, s32[8192]{0:T(1024)}, u32[]{:S(2)}) copy-start(s32[8192]{0:T(1024)} %param.15) | copy-start | bytes 98308
  13.5 5.6 %copy-start.6 = (s32[8192]{0:T(1024)S(1)}, s32[8192]{0:T(1024)}, u32[]{:S(2)}) copy-start(s32[8192]{0:T(1024)} %param.14) | copy-start | bytes 98308
  13.5 5.6 %copy-start.8 = (s32[1,1,1,2,2,64]{5,4,3,2,1,0:T(2,128)S(1)}, s32[1,1,1,2,2,64]{5,4,3,2,1,0:T(2,128)}, u32[]{:S(2)}) copy-start(s32[1,1,1,2,2,64]{5,4,3,2,1,0:T(2,128)} %param.17) | copy-start | bytes 3076
  13.5 5.6 %copy-start.9 = (f32[2,256]{1,0:T(2,128)S(1)}, f32[2,256]{1,0:T(2,128)}, u32[]{:S(2)}) copy-start(f32[2,256]{1,0:T(2,128)} %gain_ref.3) | copy-start | bytes 6148
  19.1 16.8 %copy-start.4 = (bf16[2,256,256]{2,1,0:T(8,128)(2,1)S(1)}, bf16[2,256,256]{2,1,0:T(8,128)(2,1)}, u32[]{:S(2)}) copy-start(bf16[2,256,256]{2,1,0:T(8,128)(2,1)} %wedge_ref.1) | copy-start | bytes 786436
  29.2 9.3 %collective-permute-start.4 = (bf16[2,64,256]{2,1,0:T(8,128)(2,1)S(1)}, bf16[2,64,256]{2,1,0:T(8,128)(2,1)S(1)}, u32[]{:S(2)}, u32[]{:S(2)}) collective-permute-start(bf16[2,64,256]{2,1,0:T(8,128)(2,1)S(1)} %get-tuple-element.30.c1_ref), channel_id=1, source_target_pairs={{0,4},{4,8},{8,12},{12,16},{16,20},{20,24},{24,28},{28,0},{1,5},{5... | collective-permute-start | bytes 196616 | tf_op jit(solution)/shard_map/ppermute | solution.py:343
  36.0 4.6 %collective-permute-start.5 = (bf16[2,64,256]{2,1,0:T(8,128)(2,1)S(1)}, bf16[2,64,256]{2,1,0:T(8,128)(2,1)S(1)}, u32[]{:S(2)}, u32[]{:S(2)}) collective-permute-start(bf16[2,64,256]{2,1,0:T(8,128)(2,1)S(1)} %get-tuple-element.31.c0_ref), channel_id=1, source_target_pairs={{4,0},{8,4},{12,8},{16,12},{20,16},{24,20},{28,24},{0,28},{5,1},{9... | collective-permute-start | bytes 196616 | tf_op jit(solution)/shard_map/ppermute | solution.py:343
  38.5 7.2 %copy-start.1 = (bf16[169,8192]{1,0:T(8,128)(2,1)S(1)}, bf16[169,8192]{1,0:T(8,128)(2,1)}, u32[]{:S(2)}) copy-start(bf16[169,8192]{1,0:T(8,128)(2,1)} %goal_ref.1) | copy-start | bytes 8306692
  38.5 7.2 %copy-start.5 = (bf16[256,256]{1,0:T(8,128)(2,1)S(1)}, bf16[256,256]{1,0:T(8,128)(2,1)}, u32[]{:S(2)}) copy-start(bf16[256,256]{1,0:T(8,128)(2,1)} %hin_ref.1) | copy-start | bytes 393220
  38.5 7.2 %copy-start.7 = (bf16[256,169]{0,1:T(8,128)(2,1)S(1)}, bf16[256,169]{0,1:T(8,128)(2,1)}, u32[]{:S(2)}) copy-start(bf16[256,169]{0,1:T(8,128)(2,1)} %param.22) | copy-start | bytes 259588
  40.6 5.1 %collective-permute-start.6 = (bf16[4,64,256]{2,1,0:T(8,128)(2,1)S(1)}, bf16[4,64,256]{2,1,0:T(8,128)(2,1)S(1)}, u32[]{:S(2)}, u32[]{:S(2)}) collective-permute-start(bf16[4,64,256]{2,1,0:T(8,128)(2,1)S(1)} %get-tuple-element.35), channel_id=1, source_target_pairs={{0,1},{1,2},{2,3},{3,0},{4,5},{5,6},{6,7},{7,4},{8,9},{9,10},{10,1... | collective-permute-start | bytes 393224 | tf_op jit(solution)/shard_map/ppermute | solution.py:343
  40.7 5.0 %collective-permute-start.7 = (bf16[4,64,256]{2,1,0:T(8,128)(2,1)S(1)}, bf16[4,64,256]{2,1,0:T(8,128)(2,1)S(1)}, u32[]{:S(2)}, u32[]{:S(2)}) collective-permute-start(bf16[4,64,256]{2,1,0:T(8,128)(2,1)S(1)} %get-tuple-element.36), channel_id=1, source_target_pairs={{1,0},{2,1},{3,2},{0,3},{5,4},{6,5},{7,6},{4,7},{9,8},{10,9},{11,1... | collective-permute-start | bytes 393224 | tf_op jit(solution)/shard_map/ppermute | solution.py:343
  59.4 5.3 %collective-permute-start.8 = (f32[64,8,128]{2,1,0:T(8,128)S(1)}, f32[64,8,128]{2,1,0:T(8,128)S(1)}, u32[]{:S(2)}, u32[]{:S(2)}) collective-permute-start(f32[64,8,128]{2,1,0:T(8,128)S(1)} %get-tuple-element.40), channel_id=1, source_target_pairs={{0,32},{32,0},{1,33},{33,1},{2,34},{34,2},{3,35},{35,3},{4,36},{36... | collective-permute-start | bytes 786440 | tf_op jit(solution)/shard_map/ppermute | solution.py:353
  103.6 4.3 %collective-permute-start.9 = (f32[64,8,128]{2,1,0:T(8,128)S(1)}, f32[64,8,128]{2,1,0:T(8,128)S(1)}, u32[]{:S(2)}, u32[]{:S(2)}) collective-permute-start(f32[64,8,128]{2,1,0:T(8,128)S(1)} %all_to_all.11), channel_id=1, source_target_pairs={{0,32},{32,0},{1,33},{33,1},{2,34},{34,2},{3,35},{35,3},{4,36},{36... | collective-permute-start | bytes 786440 | tf_op jit(solution)/shard_map/ppermute | solution.py:353

commit v5 on v4

--- a/solution.py
+++ b/solution.py
@@ -174,7 +174,7 @@
             near_ref[0, :, at] = nn(near_t[...], near_hot(src_ref[0, :, at])).astype(BF)
 
 
-def message_stages(first, count, src_ref, dst_ref, near_ref, part_ref, edge_ref, far_t, wkv_t, hl, target_hot, keep_edges):
+def message_stages(first, count, src_ref, dst_ref, near_ref, part_ref, edge_ref, far_t, wkv_t, hl, target_hot, keep_edges, lag):
     def gather(held, at, start):
         held["rows"] = nn(far_t[...], far_hot(src_ref[0, :, at])).astype(BF) + near_ref[0, :, at]
 
@@ -193,7 +193,7 @@
         held["live"] = first + start + lax.broadcasted_iota(jnp.int32, (1, SUB), 1) < count
         target_hot[:, at] = hot(jnp.where(held["live"], target, -1), 0, 256)
 
-    return [(gather, 0), (message, 1)]
+    return [(gather, 0), (message, lag)]
 
 
 def first_kernel(
@@ -217,7 +217,7 @@
 
         staged(
             message_stages(
-                step * BLOCK, count, src_ref, dst_ref, near_ref, part_ref, edge_ref, far_t, wkv_t, hl, target_hot, keep_edges
+                step * BLOCK, count, src_ref, dst_ref, near_ref, part_ref, edge_ref, far_t, wkv_t, hl, target_hot, keep_edges, 0
             )
         )
         acc[...] += nt(hl[...], target_hot[...])
@@ -272,7 +272,7 @@
 
         staged(
             message_stages(
-                step * BLOCK, count, src_ref, dst_ref, near_ref, part_ref, edge_ref, far_t, wkv_t, hl, target_hot, keep_edges
+                step * BLOCK, count, src_ref, dst_ref, near_ref, part_ref, edge_ref, far_t, wkv_t, hl, target_hot, keep_edges, 1
             )
             + [(activate, LAGS[0]), (compare, LAGS[1]), (back, LAGS[2])]
         )
@@ -447,10 +447,10 @@
     chips = ("pair", "gx", "gy")
     parts = lax.all_to_all(keep + swap_cores(send), chips, 0, 0, tiled=True)
     share = jnp.sum(parts, axis=0)
-    mine = lax.all_to_all(jnp.broadcast_to(share[None], (64, 8, 128)), chips, 0, 0, tiled=True)
-    other = swap_cores(mine)
-    grad_in = jnp.where(core == 0, mine, other)
-    grad_out = jnp.where(core == 0, other, mine)[0:44]
+    full = lax.all_to_all(jnp.broadcast_to(share[None], (128, 8, 128)), AXES, 0, 0, tiled=True)
+    full = full.reshape(2, 2, 32, 8, 128)
+    grad_in = full[:, 0].reshape(64, 8, 128)
+    grad_out = full[:, 1].reshape(64, 8, 128)[0:44]
     grad_in = grad_in.reshape(32, 2, 8, 128).transpose(0, 2, 1, 3).reshape(256, 256)
     grad_out = grad_out.reshape(22, 2, 8, 128).transpose(0, 2, 1, 3).reshape(176, 256)[0:169].T
     return nodes, grad_in, grad_out

time: 109 us -> 106 us (0.972)
  Pallas kernels: 35.2 us -> 41.6 us
  starting transfers between devices: 26.9 us -> 21.3 us
  waiting for transfers between devices: 5.32 us -> 2.1 us
    all_to_all x1, blocking collectives: 24.5 us -> 19.3 us  [body(): parts = lax.all_to_all(keep + swap_cores(send), chips, 0, 0, tiled=True)]
    all_to_all x1, blocking collectives: 14.2 us -> 19.4 us  [body(): lax.all_to_all(jnp.broadcast_to(share[None], (128, 8, 128)), AXES, 0, 0,...]
    ppermute x2 -> x1, starting transfers between devices: 7.31 us -> 3.27 us  [swap_cores(): return lax.ppermute(x, 'core', [(0, 1), (1, 0)])]
    pallas_call x1, Pallas kernels: 13.6 us -> 17.6 us  [body(): pl.pallas_call(functools.partial(second_kernel, scale=scale), grid=(block...]
    ppermute x8, waiting for transfers between devices: 3 us -> 0.94 us  [shift(): return (lax.ppermute(high, axis, up), lax.ppermute(low, axis, down))]
    ppermute x8, starting transfers between devices: 19.6 us -> 18 us  [shift(): return (lax.ppermute(high, axis, up), lax.ppermute(low, axis, down))]
    pallas_call x1, Pallas kernels: 5.48 us -> 6.74 us  [first_part(): pl.pallas_call(first_part_kernel, grid=(blocks,), in_specs=[SCALAR, whole...]
    ppermute x2 -> x1, waiting for transfers between devices: 2.32 us -> 1.16 us  [swap_cores(): return lax.ppermute(x, 'core', [(0, 1), (1, 0)])]
  transfers between devices with their start and end apart: 10 -> 9, of which waited for: 4 -> 2; matrix products, arithmetic and copies ran while one was open for 0% -> 0% of each run, Pallas kernels for 9% -> 12%
where the time goes in v5:
time: 106 us; the launch traced here: 107 us
  Pallas kernels  41.6 us (39%)
  blocking collectives  38.7 us (37%)
  starting transfers between devices  21.3 us (20%)
  waiting for transfers between devices  2.1 us (2%)
  between operations  1.54 us (1%)
  local copies, waits for them, and re-layouts  1.52 us (1%)
    all_to_all x1, blocking collectives, body(): lax.all_to_all(jnp.broadcast_to(share[None], (128, 8, 128)), AXES, 0, 0,...  19.4 us
    all_to_all x1, blocking collectives, body(): parts = lax.all_to_all(keep + swap_cores(send), chips, 0, 0, tiled=True)  19.3 us
    ppermute x8, starting transfers between devices, shift(): return (lax.ppermute(high, axis, up), lax.ppermute(low, axis, down))  18 us
    pallas_call x1, Pallas kernels, body(): pl.pallas_call(functools.partial(second_kernel, scale=scale), grid=(block...  17.6 us
    pallas_call x1, Pallas kernels, body(): pl.pallas_call(first_kernel, grid=(blocks,), in_specs=layer_specs(0) + [w...  9.84 us
    pallas_call x1, Pallas kernels, first_part(): pl.pallas_call(first_part_kernel, grid=(blocks,), in_specs=[SCALAR, whole...  6.74 us
    ppermute x1, starting transfers between devices, swap_cores(): return lax.ppermute(x, 'core', [(0, 1), (1, 0)])  3.27 us
    pallas_call x1, Pallas kernels, second_part(): pl.pallas_call(part_kernel, grid=(blocks,), in_specs=[SCALAR, whole(256,...  3.21 us
  transfers between devices with their start and end apart: 9, of which 2 were waited for; matrix products, arithmetic and copies ran while one was open for 0% of the time, Pallas kernels for 12%

profile of v5, /device:TPU:1, one launch (start us, length us, event | category | flops | bytes accessed | tf_op | source)
XLA Modules:
  0.0 106.9 jit_solution(10745615657269716298)
XLA Ops:
  0.6 1.2 %shard_map.139 = (bf16[2,64,256]{2,1,0:T(8,128)(2,1)S(1)}, bf16[2,64,256]{2,1,0:T(8,128)(2,1)S(1)}) custom-call(bf16[256,256]{1,0:T(8,128)(2,1)} %nodes_ref.3, s32[2,2,64]{2,1,0:T(2,128)} %bitcast.28), custom_call_target="tpu_custom_call" | custom-call | tf_op jit(solution)/shard_map/pallas_call | solution.py:410
  1.8 3.8 %collective-permute-start = (bf16[2,64,256]{2,1,0:T(8,128)(2,1)S(1)}, bf16[2,64,256]{2,1,0:T(8,128)(2,1)S(1)}, u32[]{:S(2)}, u32[]{:S(2)}) collective-permute-start(bf16[2,64,256]{2,1,0:T(8,128)(2,1)S(1)} %get-tuple-element.22.c1_ref), channel_id=1, source_target_pairs={{0,4},{4,8},{8,12},{12,16},{16,20},{20,24},{24,28},{28,0},{1,5},{5... | collective-permute-start | bytes 196616 | tf_op jit(solution)/shard_map/ppermute | solution.py:343
  5.6 3.6 %collective-permute-start.1 = (bf16[2,64,256]{2,1,0:T(8,128)(2,1)S(1)}, bf16[2,64,256]{2,1,0:T(8,128)(2,1)S(1)}, u32[]{:S(2)}, u32[]{:S(2)}) collective-permute-start(bf16[2,64,256]{2,1,0:T(8,128)(2,1)S(1)} %get-tuple-element.23.c0_ref), channel_id=1, source_target_pairs={{4,0},{8,4},{12,8},{16,12},{20,16},{24,20},{28,24},{0,28},{5,1},{9... | collective-permute-start | bytes 196616 | tf_op jit(solution)/shard_map/ppermute | solution.py:343
  9.8 0.9 collective-permute-done.before_ref
  10.7 0.0 collective-permute-done.1.after_ref
  10.8 1.3 %collective-permute-start.2 = (bf16[4,64,256]{2,1,0:T(8,128)(2,1)S(1)}, bf16[4,64,256]{2,1,0:T(8,128)(2,1)S(1)}, u32[]{:S(2)}, u32[]{:S(2)}) collective-permute-start(bf16[4,64,256]{2,1,0:T(8,128)(2,1)S(1)} %get-tuple-element.24), channel_id=1, source_target_pairs={{0,1},{1,2},{2,3},{3,0},{4,5},{5,6},{6,7},{7,4},{8,9},{9,10},{10,1... | collective-permute-start | bytes 393224 | tf_op jit(solution)/shard_map/ppermute | solution.py:343
  12.0 1.5 %collective-permute-start.3 = (bf16[4,64,256]{2,1,0:T(8,128)(2,1)S(1)}, bf16[4,64,256]{2,1,0:T(8,128)(2,1)S(1)}, u32[]{:S(2)}, u32[]{:S(2)}) collective-permute-start(bf16[4,64,256]{2,1,0:T(8,128)(2,1)S(1)} %get-tuple-element.25), channel_id=1, source_target_pairs={{1,0},{2,1},{3,2},{0,3},{5,4},{6,5},{7,6},{4,7},{9,8},{10,9},{11,1... | collective-permute-start | bytes 393224 | tf_op jit(solution)/shard_map/ppermute | solution.py:343
  13.5 0.0 copy-start.8
  13.5 0.0 copy-start.9
  13.5 6.7 %shard_map.141 = (bf16[4,256,2048]{2,1,0:T(8,128)(2,1)S(1)}, f32[4,256,2048]{2,1,0:T(8,128)S(1)}, bf16[4,256,2048]{2,1,0:T(8,128)(2,1)S(1)}) custom-call(s32[1]{0:T(128)S(6)} %copy.15.count_ref, bf16[2,64,256]{2,1,0:T(8,128)(2,1)S(1)} %collective-permute-done.before_ref, bf16[2,64,256]{2,1,0:T(8,128)(2,1)S(1)} %collective-permute-done.1.after_ref, ...), custom_call_target="tpu_custom_call" | custom-call | flops 4294967296 | bytes 25165824 | tf_op jit(solution)/shard_map/pallas_call | solution.py:374
  20.3 0.0 collective-permute-done.2.low_ref
  20.3 0.0 collective-permute-done.3.high_ref
  20.4 0.0 copy-start.4
  20.4 9.8 %shard_map.142 = (bf16[256,256]{1,0:T(8,128)(2,1)S(1)}, bf16[2,64,256]{2,1,0:T(8,128)(2,1)S(1)}, bf16[2,64,256]{2,1,0:T(8,128)(2,1)S(1)}, bf16[4,256,2048]{2,1,0:T(8,128)(2,1)S(1)}) custom-call(s32[1]{0:T(128)S(6)} %copy.15.count_ref, bf16[256,256]{1,0:T(8,128)(2,1)S(1)} %copy-done.2, bf16[4,64,256]{2,1,0:T(8,128)(2,1)S(1)} %collective-permute-done.2.low_ref, ...), custom_call_target="tpu_custom_call" | custom-call | tf_op jit(solution)/shard_map/pallas_call | solution.py:414
  30.2 0.1 collective-permute-start.4
  30.3 5.1 %collective-permute-start.5 = (bf16[2,64,256]{2,1,0:T(8,128)(2,1)S(1)}, bf16[2,64,256]{2,1,0:T(8,128)(2,1)S(1)}, u32[]{:S(2)}, u32[]{:S(2)}) collective-permute-start(bf16[2,64,256]{2,1,0:T(8,128)(2,1)S(1)} %get-tuple-element.31.c0_ref), channel_id=1, source_target_pairs={{4,0},{8,4},{12,8},{16,12},{20,16},{24,20},{28,24},{0,28},{5,1},{9... | collective-permute-start | bytes 196616 | tf_op jit(solution)/shard_map/ppermute | solution.py:343
  35.4 3.2 %shard_map.143.part_ref = f32[4,256,2048]{2,1,0:T(8,128)S(1)} custom-call(s32[1]{0:T(128)S(6)} %copy.15.count_ref, bf16[256,256]{1,0:T(8,128)(2,1)S(1)} %get-tuple-element.29.nodes_ref, bf16[2,256,768]{2,1,0:T(8,128)(2,1)S(1)} %copy-done, bf16[2,256,256]{2,1,0:T(8,128)(2,1)S(1)} %copy-done.4, s32[4,1,2048]{2,1,0:T(1,128)S(1)} %bitcast.21, ...), custom_call_target="tpu_custom_call" | custom-call | flops 2147483648 | bytes 12582912 | tf_op jit(solution)/shard_map/pallas_call | solution.py:387
  38.6 0.0 copy-start.1
  38.6 0.0 copy-start.5
  38.6 0.0 copy-start.7
  38.7 0.1 collective-permute-start.6
  38.8 2.7 %collective-permute-start.7 = (bf16[4,64,256]{2,1,0:T(8,128)(2,1)S(1)}, bf16[4,64,256]{2,1,0:T(8,128)(2,1)S(1)}, u32[]{:S(2)}, u32[]{:S(2)}) collective-permute-start(bf16[4,64,256]{2,1,0:T(8,128)(2,1)S(1)} %get-tuple-element.36), channel_id=1, source_target_pairs={{1,0},{2,1},{3,2},{0,3},{5,4},{6,5},{7,6},{4,7},{9,8},{10,9},{11,1... | collective-permute-start | bytes 393224 | tf_op jit(solution)/shard_map/ppermute | solution.py:343
  41.4 3.0 %shard_map.145.near_ref = bf16[4,256,2048]{2,1,0:T(8,128)(2,1)S(1)} custom-call(s32[1]{0:T(128)S(6)} %copy.15.count_ref, bf16[256,256]{1,0:T(8,128)(2,1)S(1)} %get-tuple-element.29.nodes_ref, bf16[2,64,256]{2,1,0:T(8,128)(2,1)S(1)} %collective-permute-done.4.before_ref, bf16[2,64,256]{2,1,0:T(8,128)(2,1)S(1)} %collective-permute-done.5.after_ref, ...), custom_call_target="tpu_custom_call" | custom-call | flops 2147483648 | bytes 12582912 | tf_op jit(solution)/shard_map/pallas_call | solution.py:399
  44.5 0.0 collective-permute-done.7.high_ref
  44.5 17.6 %shard_map.146 = (bf16[256,256]{1,0:T(8,128)(2,1)}, f32[64,8,128]{2,1,0:T(8,128)S(1)}, f32[64,8,128]{2,1,0:T(8,128)S(1)}) custom-call(s32[1]{0:T(128)S(6)} %copy.15.count_ref, bf16[256,256]{1,0:T(8,128)(2,1)S(1)} %get-tuple-element.29.nodes_ref, bf16[4,64,256]{2,1,0:T(8,128)(2,1)S(1)} %collective-permute-done.6.low_ref, ...), custom_call_target="tpu_custom_call" | custom-call | tf_op jit(solution)/shard_map/pallas_call | solution.py:431
  62.2 3.3 %collective-permute-start.8 = (f32[64,8,128]{2,1,0:T(8,128)S(1)}, f32[64,8,128]{2,1,0:T(8,128)S(1)}, u32[]{:S(2)}, u32[]{:S(2)}) collective-permute-start(f32[64,8,128]{2,1,0:T(8,128)S(1)} %get-tuple-element.40), channel_id=1, source_target_pairs={{0,32},{32,0},{1,33},{33,1},{2,34},{34,2},{3,35},{35,3},{4,36},{36... | collective-permute-start | bytes 786440 | tf_op jit(solution)/shard_map/ppermute | solution.py:353
  65.4 1.2 %collective-permute-done.8 = f32[64,8,128]{2,1,0:T(8,128)S(1)} collective-permute-done((f32[64,8,128]{2,1,0:T(8,128)S(1)}, f32[64,8,128]{2,1,0:T(8,128)S(1)}, u32[]{:S(2)}, u32[]{:S(2)}) %collective-permute-start.8) | collective-permute-done | bytes 262176 | tf_op jit(solution)/shard_map/ppermute | solution.py:353
  66.6 19.3 %all_to_all.10 = f32[64,8,128]{2,1,0:T(8,128)S(1)} all-to-all(f32[64,8,128]{2,1,0:T(8,128)S(1)} %add.3), channel_id=1, replica_groups=mesh['pair'=2,'core'=2,'gx'=8,'gy'=4] {'pair','gx','gy'}, dimensions={0} | all-to-all | bytes 524288 | tf_op jit(solution)/shard_map/all_to_all | solution.py:448
  85.9 0.1 reduce_sum.9
  86.0 19.4 %all_to_all.11 = f32[128,8,128]{2,1,0:T(8,128)S(1)} all-to-all(f32[128,8,128]{2,1,0:T(8,128)S(1)} %broadcast_in_dim.2), channel_id=1, replica_groups=mesh['pair'=2,'core'=2,'gx'=8,'gy'=4] {'pair','core','gx','gy'}, dimensions={0} | all-to-all | bytes 1048576 | tf_op jit(solution)/shard_map/all_to_all | solution.py:450
  105.4 0.7 fusion
  106.2 0.7 slice_bitcast_fusion
  (22 shorter events, 0.2 us)
Async XLA Ops:
  1.8 8.9 %collective-permute-start = (bf16[2,64,256]{2,1,0:T(8,128)(2,1)S(1)}, bf16[2,64,256]{2,1,0:T(8,128)(2,1)S(1)}, u32[]{:S(2)}, u32[]{:S(2)}) collective-permute-start(bf16[2,64,256]{2,1,0:T(8,128)(2,1)S(1)} %get-tuple-element.22.c1_ref), channel_id=1, source_target_pairs={{0,4},{4,8},{8,12},{12,16},{16,20},{20,24},{24,28},{28,0},{1,5},{5... | collective-permute-start | bytes 196616 | tf_op jit(solution)/shard_map/ppermute | solution.py:343
  5.6 5.1 %collective-permute-start.1 = (bf16[2,64,256]{2,1,0:T(8,128)(2,1)S(1)}, bf16[2,64,256]{2,1,0:T(8,128)(2,1)S(1)}, u32[]{:S(2)}, u32[]{:S(2)}) collective-permute-start(bf16[2,64,256]{2,1,0:T(8,128)(2,1)S(1)} %get-tuple-element.23.c0_ref), channel_id=1, source_target_pairs={{4,0},{8,4},{12,8},{16,12},{20,16},{24,20},{28,24},{0,28},{5,1},{9... | collective-permute-start | bytes 196616 | tf_op jit(solution)/shard_map/ppermute | solution.py:343
  10.8 9.5 %collective-permute-start.2 = (bf16[4,64,256]{2,1,0:T(8,128)(2,1)S(1)}, bf16[4,64,256]{2,1,0:T(8,128)(2,1)S(1)}, u32[]{:S(2)}, u32[]{:S(2)}) collective-permute-start(bf16[4,64,256]{2,1,0:T(8,128)(2,1)S(1)} %get-tuple-element.24), channel_id=1, source_target_pairs={{0,1},{1,2},{2,3},{3,0},{4,5},{5,6},{6,7},{7,4},{8,9},{9,10},{10,1... | collective-permute-start | bytes 393224 | tf_op jit(solution)/shard_map/ppermute | solution.py:343
  12.0 8.3 %collective-permute-start.3 = (bf16[4,64,256]{2,1,0:T(8,128)(2,1)S(1)}, bf16[4,64,256]{2,1,0:T(8,128)(2,1)S(1)}, u32[]{:S(2)}, u32[]{:S(2)}) collective-permute-start(bf16[4,64,256]{2,1,0:T(8,128)(2,1)S(1)} %get-tuple-element.25), channel_id=1, source_target_pairs={{1,0},{2,1},{3,2},{0,3},{5,4},{6,5},{7,6},{4,7},{9,8},{10,9},{11,1... | collective-permute-start | bytes 393224 | tf_op jit(solution)/shard_map/ppermute | solution.py:343
  13.5 6.8 %copy-start = (bf16[2,256,768]{2,1,0:T(8,128)(2,1)S(1)}, bf16[2,256,768]{2,1,0:T(8,128)(2,1)}, u32[]{:S(2)}) copy-start(bf16[2,256,768]{2,1,0:T(8,128)(2,1)} %wqkv_ref.5) | copy-start | bytes 2359300
  13.5 6.8 %copy-start.2 = (bf16[256,256]{1,0:T(8,128)(2,1)S(1)}, bf16[256,256]{1,0:T(8,128)(2,1)}, u32[]{:S(2)}) copy-start(bf16[256,256]{1,0:T(8,128)(2,1)} %nodes_ref.3) | copy-start | bytes 393220
  13.5 6.8 %copy-start.3 = (s32[8192]{0:T(1024)S(1)}, s32[8192]{0:T(1024)}, u32[]{:S(2)}) copy-start(s32[8192]{0:T(1024)} %param.15) | copy-start | bytes 98308
  13.5 6.8 %copy-start.6 = (s32[8192]{0:T(1024)S(1)}, s32[8192]{0:T(1024)}, u32[]{:S(2)}) copy-start(s32[8192]{0:T(1024)} %param.14) | copy-start | bytes 98308
  13.5 6.8 %copy-start.8 = (s32[1,1,1,2,2,64]{5,4,3,2,1,0:T(2,128)S(1)}, s32[1,1,1,2,2,64]{5,4,3,2,1,0:T(2,128)}, u32[]{:S(2)}) copy-start(s32[1,1,1,2,2,64]{5,4,3,2,1,0:T(2,128)} %param.17) | copy-start | bytes 3076
  13.5 6.8 %copy-start.9 = (f32[2,256]{1,0:T(2,128)S(1)}, f32[2,256]{1,0:T(2,128)}, u32[]{:S(2)}) copy-start(f32[2,256]{1,0:T(2,128)} %gain_ref.3) | copy-start | bytes 6148
  20.4 15.0 %copy-start.4 = (bf16[2,256,256]{2,1,0:T(8,128)(2,1)S(1)}, bf16[2,256,256]{2,1,0:T(8,128)(2,1)}, u32[]{:S(2)}) copy-start(bf16[2,256,256]{2,1,0:T(8,128)(2,1)} %wedge_ref.1) | copy-start | bytes 786436
  30.2 8.4 %collective-permute-start.4 = (bf16[2,64,256]{2,1,0:T(8,128)(2,1)S(1)}, bf16[2,64,256]{2,1,0:T(8,128)(2,1)S(1)}, u32[]{:S(2)}, u32[]{:S(2)}) collective-permute-start(bf16[2,64,256]{2,1,0:T(8,128)(2,1)S(1)} %get-tuple-element.30.c1_ref), channel_id=1, source_target_pairs={{0,4},{4,8},{8,12},{12,16},{16,20},{20,24},{24,28},{28,0},{1,5},{5... | collective-permute-start | bytes 196616 | tf_op jit(solution)/shard_map/ppermute | solution.py:343
  30.3 8.3 %collective-permute-start.5 = (bf16[2,64,256]{2,1,0:T(8,128)(2,1)S(1)}, bf16[2,64,256]{2,1,0:T(8,128)(2,1)S(1)}, u32[]{:S(2)}, u32[]{:S(2)}) collective-permute-start(bf16[2,64,256]{2,1,0:T(8,128)(2,1)S(1)} %get-tuple-element.31.c0_ref), channel_id=1, source_target_pairs={{4,0},{8,4},{12,8},{16,12},{20,16},{24,20},{28,24},{0,28},{5,1},{9... | collective-permute-start | bytes 196616 | tf_op jit(solution)/shard_map/ppermute | solution.py:343
  38.6 5.9 %copy-start.1 = (bf16[169,8192]{1,0:T(8,128)(2,1)S(1)}, bf16[169,8192]{1,0:T(8,128)(2,1)}, u32[]{:S(2)}) copy-start(bf16[169,8192]{1,0:T(8,128)(2,1)} %goal_ref.1) | copy-start | bytes 8306692
  38.6 5.9 %copy-start.5 = (bf16[256,256]{1,0:T(8,128)(2,1)S(1)}, bf16[256,256]{1,0:T(8,128)(2,1)}, u32[]{:S(2)}) copy-start(bf16[256,256]{1,0:T(8,128)(2,1)} %hin_ref.1) | copy-start | bytes 393220
  38.6 5.9 %copy-start.7 = (bf16[256,169]{0,1:T(8,128)(2,1)S(1)}, bf16[256,169]{0,1:T(8,128)(2,1)}, u32[]{:S(2)}) copy-start(bf16[256,169]{0,1:T(8,128)(2,1)} %param.22) | copy-start | bytes 259588
  38.7 5.8 %collective-permute-start.6 = (bf16[4,64,256]{2,1,0:T(8,128)(2,1)S(1)}, bf16[4,64,256]{2,1,0:T(8,128)(2,1)S(1)}, u32[]{:S(2)}, u32[]{:S(2)}) collective-permute-start(bf16[4,64,256]{2,1,0:T(8,128)(2,1)S(1)} %get-tuple-element.35), channel_id=1, source_target_pairs={{0,1},{1,2},{2,3},{3,0},{4,5},{5,6},{6,7},{7,4},{8,9},{9,10},{10,1... | collective-permute-start | bytes 393224 | tf_op jit(solution)/shard_map/ppermute | solution.py:343
  38.8 5.7 %collective-permute-start.7 = (bf16[4,64,256]{2,1,0:T(8,128)(2,1)S(1)}, bf16[4,64,256]{2,1,0:T(8,128)(2,1)S(1)}, u32[]{:S(2)}, u32[]{:S(2)}) collective-permute-start(bf16[4,64,256]{2,1,0:T(8,128)(2,1)S(1)} %get-tuple-element.36), channel_id=1, source_target_pairs={{1,0},{2,1},{3,2},{0,3},{5,4},{6,5},{7,6},{4,7},{9,8},{10,9},{11,1... | collective-permute-start | bytes 393224 | tf_op jit(solution)/shard_map/ppermute | solution.py:343
  62.2 4.4 %collective-permute-start.8 = (f32[64,8,128]{2,1,0:T(8,128)S(1)}, f32[64,8,128]{2,1,0:T(8,128)S(1)}, u32[]{:S(2)}, u32[]{:S(2)}) collective-permute-start(f32[64,8,128]{2,1,0:T(8,128)S(1)} %get-tuple-element.40), channel_id=1, source_target_pairs={{0,32},{32,0},{1,33},{33,1},{2,34},{34,2},{3,35},{35,3},{4,36},{36... | collective-permute-start | bytes 786440 | tf_op jit(solution)/shard_map/ppermute | solution.py:353

commit v6 on v5

--- a/solution.py
+++ b/solution.py
@@ -99,16 +99,9 @@
     return nn(wqe_t[...], jnp.concatenate([hot(target, 0, 256), edges], axis=0))
 
 
-def near_tables(nodes, before_ref, after_ref, near_t):
-    near_t[:, 0:256] = nodes[...].T
-    cells = [before_ref[0], before_ref[1], after_ref[0], after_ref[1]]
-    near_t[:, 256:512] = jnp.concatenate(cells, axis=0).T
-
-
 def first_part_kernel(
-    count_ref, before_ref, after_ref, nodes_hbm, wqkv_hbm, wedge_hbm, src_hbm, dst_hbm, edge_hbm,
-    near_ref, part_ref, turned_ref,
-    near_t, wqe_t, nodes, wqkv, wedge, src, dst, edge, sems,
+    count_ref, nodes_hbm, wqkv_hbm, wedge_hbm, dst_hbm, edge_hbm, part_ref, turned_ref,
+    wqe_t, nodes, wqkv, wedge, dst, edge, sems,
 ):
     step = pl.program_id(0)
     steps = edge.shape[0]
@@ -116,12 +109,11 @@
         pltpu.make_async_copy(nodes_hbm, nodes, sems.at[0]),
         pltpu.make_async_copy(wqkv_hbm.at[0, :, pl.ds(0, 256)], wqkv, sems.at[1]),
         pltpu.make_async_copy(wedge_hbm.at[0], wedge, sems.at[2]),
-        pltpu.make_async_copy(src_hbm, src, sems.at[3]),
-        pltpu.make_async_copy(dst_hbm, dst, sems.at[4]),
+        pltpu.make_async_copy(dst_hbm, dst, sems.at[3]),
     ]
 
     def edge_copy(i):
-        return pltpu.make_async_copy(edge_hbm.at[pl.ds(i * BLOCK, BLOCK), :], edge.at[i], sems.at[5 + i])
+        return pltpu.make_async_copy(edge_hbm.at[pl.ds(i * BLOCK, BLOCK), :], edge.at[i], sems.at[4 + i])
 
     @pl.when(step == 0)
     def _():
@@ -132,7 +124,6 @@
         for copy in small:
             copy.wait()
         prepare_own(nodes, wqkv, wedge, wqe_t)
-        near_tables(nodes, before_ref, after_ref, near_t)
 
     edge_copy(step).wait()
 
@@ -140,7 +131,6 @@
     def _():
         for j in range(BLOCK // SUB):
             at = slice(j * SUB, (j + 1) * SUB)
-            near_ref[0, :, at] = nn(near_t[...], near_hot(src[step, :, at])).astype(BF)
             edges = edge[step, at, :].T
             turned_ref[0, :, at] = edges
             part_ref[0, :, at] = part_of(dst[step, :, at], edges, wqe_t)
@@ -165,7 +155,9 @@
 
     @pl.when(step == 0)
     def _():
-        near_tables(nodes_ref, before_ref, after_ref, near_t)
+        near_t[:, 0:256] = nodes_ref[...].T
+        cells = [before_ref[0], before_ref[1], after_ref[0], after_ref[1]]
+        near_t[:, 256:512] = jnp.concatenate(cells, axis=0).T
 
     @pl.when(step * BLOCK < count_ref[0])
     def _():
@@ -357,7 +349,8 @@
     slots = edge_feat.shape[0]
     blocks = slots // BLOCK
     scale = 0.125 / (slots * lax.axis_size(AXES)) ** 0.5
-    index = send_idx.reshape(2, 2, 64)
+    core = lax.axis_index("core").astype(jnp.int32).reshape(1)
+    index, core = lax.optimization_barrier((send_idx.reshape(2, 2, 64), core))
     source = edge_src.reshape(blocks, 1, BLOCK)
     target = edge_dst.reshape(blocks, 1, BLOCK)
 
@@ -368,20 +361,22 @@
     def cost(units):
         return pl.CostEstimate(flops=2 * units * slots * 65536, bytes_accessed=units * 6 * 2**20, transcendentals=0)
 
-    def first_part(before, after):
+    def first_part(nodes):
         stay = pl.BlockSpec(memory_space=pltpu.HBM)
-        index_rows = pltpu.VMEM((blocks, 1, BLOCK), jnp.int32)
         return pl.pallas_call(
             first_part_kernel,
             grid=(blocks,),
-            in_specs=[SCALAR, whole(2, 64, 256), whole(2, 64, 256)] + [stay] * 6,
-            out_specs=[TURNED] * 3,
-            out_shape=[turned, wide, turned],
-            scratch_shapes=[pltpu.VMEM((256, 512), BF)] * 2 + [pltpu.VMEM((256, 256), BF)] * 3
-            + [index_rows, index_rows, pltpu.VMEM((blocks, BLOCK, 256), BF), pltpu.SemaphoreType.DMA((5 + blocks,))],
-            compiler_params=PARAMS,
-            cost_estimate=cost(4),
-        )(edge_count, before, after, *stays(node_feat, w_qkv, w_edge, source, target, edge_feat))
+            in_specs=[SCALAR] + [stay] * 5,
+            out_specs=[TURNED] * 2,
+            out_shape=[wide, turned],
+            scratch_shapes=[pltpu.VMEM((256, 512), BF)] + [pltpu.VMEM((256, 256), BF)] * 3
+            + [
+                pltpu.VMEM((blocks, 1, BLOCK), jnp.int32), pltpu.VMEM((blocks, BLOCK, 256), BF),
+                pltpu.SemaphoreType.DMA((4 + blocks,)),
+            ],
+            compiler_params=LIGHT,
+            cost_estimate=cost(2),
+        )(edge_count, *stays(nodes, w_qkv, w_edge, target, edge_feat))
 
     def second_part(nodes, edges):
         return pl.pallas_call(
@@ -409,8 +404,11 @@
 
     c0, c1 = pl.pallas_call(corner_kernel, out_shape=[CORNER, CORNER], compiler_params=SMALL)(*stays(node_feat, index))
     before, after = shift(c0, c1, "gx")
+    later_nodes, _ = lax.optimization_barrier((node_feat, c0))
+    part, edges = first_part(later_nodes)
+    before, after, part = lax.optimization_barrier((before, after, part))
     low, high = turn_sides(before, after, c0, c1)
-    rows, part, edges = first_part(before, after)
+    rows = near(node_feat, before, after)
     nodes, c0, c1, edges = pl.pallas_call(
         first_kernel,
         grid=(blocks,),
@@ -427,7 +425,6 @@
     low, high = turn_sides(before, after, c0, c1)
     rows = near(nodes, before, after)
     half = jax.ShapeDtypeStruct((64, 8, 128), F32)
-    core = lax.axis_index("core")
     nodes, keep, send = pl.pallas_call(
         functools.partial(second_kernel, scale=scale),
         grid=(blocks,),
@@ -442,7 +439,7 @@
         compiler_params=PARAMS,
     )(
         edge_count, nodes, low, high, w_qkv, gains, source, target, rows, part, edges,
-        core.astype(jnp.int32).reshape(1), head_in, head_out.T, targets,
+        core, head_in, head_out.T, targets,
     )
     chips = ("pair", "gx", "gy")
     parts = lax.all_to_all(keep + swap_cores(send), chips, 0, 0, tiled=True)

time: 106 us -> 105 us (level)
  blocking collectives: 38.7 us -> 47 us
  Pallas kernels: 41.6 us -> 33.6 us
  starting transfers between devices: 21.3 us -> 18.6 us
    all_to_all x1, blocking collectives: 19.3 us -> 27.6 us  [body(): parts = lax.all_to_all(keep + swap_cores(send), chips, 0, 0, tiled=True)]
    pallas_call x1, Pallas kernels: 17.6 us -> 13.6 us  [body(): pl.pallas_call(functools.partial(second_kernel, scale=scale), grid=(block...]
    ppermute x1, starting transfers between devices: 3.27 us -> 0.01 us  [swap_cores(): return lax.ppermute(x, 'core', [(0, 1), (1, 0)])]
    pallas_call x1, Pallas kernels: 6.74 us -> 3.83 us  [first_part(): pl.pallas_call(first_part_kernel, grid=(blocks,), in_specs=[SCALAR] + [st...]
    pallas_call x1, Pallas kernels: 9.84 us -> 7.72 us  [body(): pl.pallas_call(first_kernel, grid=(blocks,), in_specs=layer_specs(0) + [w...]
    pallas_call x1 -> x2, Pallas kernels: 3.04 us -> 4.66 us  [near(): pl.pallas_call(near_kernel, grid=(blocks,), in_specs=[SCALAR, whole(256,...]
  transfers between devices with their start and end apart: 9 -> 9, of which waited for: 2 -> 2; matrix products, arithmetic and copies ran while one was open for 0% -> 0% of each run, Pallas kernels for 12% -> 10%
where the time goes in v6:
time: 105 us
  blocking collectives  47 us (45%)
  Pallas kernels  33.6 us (32%)
  starting transfers between devices  18.6 us (18%)
  waiting for transfers between devices  2.63 us (3%)
  local copies, waits for them, and re-layouts  1.53 us (1%)
  between operations  1.53 us (1%)
    all_to_all x1, blocking collectives, body(): parts = lax.all_to_all(keep + swap_cores(send), chips, 0, 0, tiled=True)  27.6 us
    all_to_all x1, blocking collectives, body(): lax.all_to_all(jnp.broadcast_to(share[None], (128, 8, 128)), AXES, 0, 0,...  19.4 us
    ppermute x8, starting transfers between devices, shift(): return (lax.ppermute(high, axis, up), lax.ppermute(low, axis, down))  18.6 us
    pallas_call x1, Pallas kernels, body(): pl.pallas_call(functools.partial(second_kernel, scale=scale), grid=(block...  13.6 us
    pallas_call x1, Pallas kernels, body(): pl.pallas_call(first_kernel, grid=(blocks,), in_specs=layer_specs(0) + [w...  7.72 us
    pallas_call x2, Pallas kernels, near(): pl.pallas_call(near_kernel, grid=(blocks,), in_specs=[SCALAR, whole(256,...  4.66 us
    pallas_call x1, Pallas kernels, first_part(): pl.pallas_call(first_part_kernel, grid=(blocks,), in_specs=[SCALAR] + [st...  3.83 us
    pallas_call x1, Pallas kernels, second_part(): pl.pallas_call(part_kernel, grid=(blocks,), in_specs=[SCALAR, whole(256,...  2.51 us
  transfers between devices with their start and end apart: 9, of which 2 were waited for; matrix products, arithmetic and copies ran while one was open for 0% of the time, Pallas kernels for 10%

profile of v6, /device:TPU:1, one launch (start us, length us, event | category | flops | bytes accessed | tf_op | source)
XLA Modules:
  0.0 105.0 jit_solution(16211011251312447744)
XLA Ops:
  0.6 0.0 copy-start.2
  0.7 1.2 %shard_map.139 = (bf16[2,64,256]{2,1,0:T(8,128)(2,1)S(1)}, bf16[2,64,256]{2,1,0:T(8,128)(2,1)S(1)}) custom-call(bf16[256,256]{1,0:T(8,128)(2,1)} %nodes_ref.5, s32[2,2,64]{2,1,0:T(2,128)} %bitcast.28), custom_call_target="tpu_custom_call" | custom-call | tf_op jit(solution)/shard_map/pallas_call | solution.py:405
  1.9 3.8 %collective-permute-start = (bf16[2,64,256]{2,1,0:T(8,128)(2,1)S(1)}, bf16[2,64,256]{2,1,0:T(8,128)(2,1)S(1)}, u32[]{:S(2)}, u32[]{:S(2)}) collective-permute-start(bf16[2,64,256]{2,1,0:T(8,128)(2,1)S(1)} %get-tuple-element.28.c1_ref), channel_id=1, source_target_pairs={{0,4},{4,8},{8,12},{12,16},{16,20},{20,24},{24,28},{28,0},{1,5},{5... | collective-permute-start | bytes 196616 | tf_op jit(solution)/shard_map/ppermute | solution.py:335
  5.7 3.6 %collective-permute-start.1 = (bf16[2,64,256]{2,1,0:T(8,128)(2,1)S(1)}, bf16[2,64,256]{2,1,0:T(8,128)(2,1)S(1)}, u32[]{:S(2)}, u32[]{:S(2)}) collective-permute-start(bf16[2,64,256]{2,1,0:T(8,128)(2,1)S(1)} %get-tuple-element.29.c0_ref), channel_id=1, source_target_pairs={{4,0},{8,4},{12,8},{16,12},{20,16},{24,20},{28,24},{0,28},{5,1},{9... | collective-permute-start | bytes 196616 | tf_op jit(solution)/shard_map/ppermute | solution.py:335
  9.9 3.8 %shard_map.140 = (f32[4,256,2048]{2,1,0:T(8,128)S(1)}, bf16[4,256,2048]{2,1,0:T(8,128)(2,1)S(1)}) custom-call(s32[1]{0:T(128)S(6)} %copy.15.count_ref, bf16[256,256]{1,0:T(8,128)(2,1)} %nodes_ref.5, bf16[2,256,768]{2,1,0:T(8,128)(2,1)} %wqkv_ref.5, bf16[2,256,256]{2,1,0:T(8,128)(2,1)} %wedge_ref.1, s32[4,1,2048]{2,1,0:T(1,128)} %bitcast.19, ...), custom_call_target="tpu_custom_call" | custom-call | flops 2147483648 | bytes 12582912 | tf_op jit(solution)/shard_map/pallas_call | solution.py:366
  13.7 0.0 copy-start
  13.7 0.0 copy-start.3
  13.7 0.0 copy-start.8
  13.8 0.0 copy-start.9
  13.8 1.3 %collective-permute-start.2 = (bf16[4,64,256]{2,1,0:T(8,128)(2,1)S(1)}, bf16[4,64,256]{2,1,0:T(8,128)(2,1)S(1)}, u32[]{:S(2)}, u32[]{:S(2)}) collective-permute-start(bf16[4,64,256]{2,1,0:T(8,128)(2,1)S(1)} %get-tuple-element.34), channel_id=1, source_target_pairs={{0,1},{1,2},{2,3},{3,0},{4,5},{5,6},{6,7},{7,4},{8,9},{9,10},{10,1... | collective-permute-start | bytes 393224 | tf_op jit(solution)/shard_map/ppermute | solution.py:335
  15.1 1.5 %collective-permute-start.3 = (bf16[4,64,256]{2,1,0:T(8,128)(2,1)S(1)}, bf16[4,64,256]{2,1,0:T(8,128)(2,1)S(1)}, u32[]{:S(2)}, u32[]{:S(2)}) collective-permute-start(bf16[4,64,256]{2,1,0:T(8,128)(2,1)S(1)} %get-tuple-element.35), channel_id=1, source_target_pairs={{1,0},{2,1},{3,2},{0,3},{5,4},{6,5},{7,6},{4,7},{9,8},{10,9},{11,1... | collective-permute-start | bytes 393224 | tf_op jit(solution)/shard_map/ppermute | solution.py:335
  16.6 2.3 %shard_map.142.near_ref = bf16[4,256,2048]{2,1,0:T(8,128)(2,1)S(1)} custom-call(s32[1]{0:T(128)S(6)} %copy.15.count_ref, bf16[256,256]{1,0:T(8,128)(2,1)S(1)} %copy-done.2, bf16[2,64,256]{2,1,0:T(8,128)(2,1)S(1)} %collective-permute-done.before_ref, bf16[2,64,256]{2,1,0:T(8,128)(2,1)S(1)} %collective-permute-done.1.after_ref, s32[4,1,2048]{2,1,0:T(1,128)S(1)} %bitcast.23), custom_call_target="tpu_custom_call" | custom-call | flops 2147483648 | bytes 12582912 | tf_op jit(solution)/shard_map/pallas_call | solution.py:394
  18.9 1.1 %collective-permute-done.2.low_ref = bf16[4,64,256]{2,1,0:T(8,128)(2,1)S(1)} collective-permute-done((bf16[4,64,256]{2,1,0:T(8,128)(2,1)S(1)}, bf16[4,64,256]{2,1,0:T(8,128)(2,1)S(1)}, u32[]{:S(2)}, u32[]{:S(2)}) %collective-permute-start.2) | collective-permute-done | bytes 131104 | tf_op jit(solution)/shard_map/ppermute | solution.py:335
  20.0 0.0 copy-start.4
  20.0 7.7 %shard_map.143 = (bf16[256,256]{1,0:T(8,128)(2,1)S(1)}, bf16[2,64,256]{2,1,0:T(8,128)(2,1)S(1)}, bf16[2,64,256]{2,1,0:T(8,128)(2,1)S(1)}, bf16[4,256,2048]{2,1,0:T(8,128)(2,1)S(1)}) custom-call(s32[1]{0:T(128)S(6)} %copy.15.count_ref, bf16[256,256]{1,0:T(8,128)(2,1)S(1)} %copy-done.2, bf16[4,64,256]{2,1,0:T(8,128)(2,1)S(1)} %collective-permute-done.2.low_ref, ...), custom_call_target="tpu_custom_call" | custom-call | tf_op jit(solution)/shard_map/pallas_call | solution.py:412
  27.8 2.2 %collective-permute-start.4 = (bf16[2,64,256]{2,1,0:T(8,128)(2,1)S(1)}, bf16[2,64,256]{2,1,0:T(8,128)(2,1)S(1)}, u32[]{:S(2)}, u32[]{:S(2)}) collective-permute-start(bf16[2,64,256]{2,1,0:T(8,128)(2,1)S(1)} %get-tuple-element.39.c1_ref), channel_id=1, source_target_pairs={{0,4},{4,8},{8,12},{12,16},{16,20},{20,24},{24,28},{28,0},{1,5},{5... | collective-permute-start | bytes 196616 | tf_op jit(solution)/shard_map/ppermute | solution.py:335
  29.9 3.6 %collective-permute-start.5 = (bf16[2,64,256]{2,1,0:T(8,128)(2,1)S(1)}, bf16[2,64,256]{2,1,0:T(8,128)(2,1)S(1)}, u32[]{:S(2)}, u32[]{:S(2)}) collective-permute-start(bf16[2,64,256]{2,1,0:T(8,128)(2,1)S(1)} %get-tuple-element.40.c0_ref), channel_id=1, source_target_pairs={{4,0},{8,4},{12,8},{16,12},{20,16},{24,20},{28,24},{0,28},{5,1},{9... | collective-permute-start | bytes 196616 | tf_op jit(solution)/shard_map/ppermute | solution.py:335
  33.5 2.5 %shard_map.144.part_ref = f32[4,256,2048]{2,1,0:T(8,128)S(1)} custom-call(s32[1]{0:T(128)S(6)} %copy.15.count_ref, bf16[256,256]{1,0:T(8,128)(2,1)S(1)} %get-tuple-element.38.nodes_ref, bf16[2,256,768]{2,1,0:T(8,128)(2,1)S(1)} %copy-done, bf16[2,256,256]{2,1,0:T(8,128)(2,1)S(1)} %copy-done.4, s32[4,1,2048]{2,1,0:T(1,128)S(1)} %bitcast.21, ...), custom_call_target="tpu_custom_call" | custom-call | flops 2147483648 | bytes 12582912 | tf_op jit(solution)/shard_map/pallas_call | solution.py:382
  36.0 0.0 copy-start.1
  36.0 0.0 copy-start.5
  36.1 0.0 copy-start.7
  36.1 0.3 collective-permute-start.6
  36.4 2.5 %collective-permute-start.7 = (bf16[4,64,256]{2,1,0:T(8,128)(2,1)S(1)}, bf16[4,64,256]{2,1,0:T(8,128)(2,1)S(1)}, u32[]{:S(2)}, u32[]{:S(2)}) collective-permute-start(bf16[4,64,256]{2,1,0:T(8,128)(2,1)S(1)} %get-tuple-element.45), channel_id=1, source_target_pairs={{1,0},{2,1},{3,2},{0,3},{5,4},{6,5},{7,6},{4,7},{9,8},{10,9},{11,1... | collective-permute-start | bytes 393224 | tf_op jit(solution)/shard_map/ppermute | solution.py:335
  38.9 2.3 %shard_map.146.near_ref = bf16[4,256,2048]{2,1,0:T(8,128)(2,1)S(1)} custom-call(s32[1]{0:T(128)S(6)} %copy.15.count_ref, bf16[256,256]{1,0:T(8,128)(2,1)S(1)} %get-tuple-element.38.nodes_ref, bf16[2,64,256]{2,1,0:T(8,128)(2,1)S(1)} %collective-permute-done.4.before_ref, bf16[2,64,256]{2,1,0:T(8,128)(2,1)S(1)} %collective-permute-done.5.after_ref, ...), custom_call_target="tpu_custom_call" | custom-call | flops 2147483648 | bytes 12582912 | tf_op jit(solution)/shard_map/pallas_call | solution.py:394
  41.2 0.0 collective-permute-done.6.low_ref
  41.3 13.6 %shard_map.147 = (bf16[256,256]{1,0:T(8,128)(2,1)}, f32[64,8,128]{2,1,0:T(8,128)S(1)}, f32[64,8,128]{2,1,0:T(8,128)S(1)}) custom-call(s32[1]{0:T(128)S(6)} %copy.15.count_ref, bf16[256,256]{1,0:T(8,128)(2,1)S(1)} %get-tuple-element.38.nodes_ref, bf16[4,64,256]{2,1,0:T(8,128)(2,1)S(1)} %collective-permute-done.6.low_ref, ...), custom_call_target="tpu_custom_call" | custom-call | tf_op jit(solution)/shard_map/pallas_call | solution.py:428
  54.9 1.5 %collective-permute-done.8 = f32[64,8,128]{2,1,0:T(8,128)S(1)} collective-permute-done((f32[64,8,128]{2,1,0:T(8,128)S(1)}, f32[64,8,128]{2,1,0:T(8,128)S(1)}, u32[]{:S(2)}, u32[]{:S(2)}) %collective-permute-start.8) | collective-permute-done | bytes 262176 | tf_op jit(solution)/shard_map/ppermute | solution.py:345
  56.5 27.6 %all_to_all.10 = f32[64,8,128]{2,1,0:T(8,128)S(1)} all-to-all(f32[64,8,128]{2,1,0:T(8,128)S(1)} %add.3), channel_id=1, replica_groups=mesh['pair'=2,'core'=2,'gx'=8,'gy'=4] {'pair','gx','gy'}, dimensions={0} | all-to-all | bytes 524288 | tf_op jit(solution)/shard_map/all_to_all | solution.py:445
  84.0 0.1 reduce_sum.9
  84.1 19.4 %all_to_all.11 = f32[128,8,128]{2,1,0:T(8,128)S(1)} all-to-all(f32[128,8,128]{2,1,0:T(8,128)S(1)} %broadcast_in_dim.2), channel_id=1, replica_groups=mesh['pair'=2,'core'=2,'gx'=8,'gy'=4] {'pair','core','gx','gy'}, dimensions={0} | all-to-all | bytes 1048576 | tf_op jit(solution)/shard_map/all_to_all | solution.py:447
  103.5 0.7 fusion
  104.3 0.7 slice_bitcast_fusion
  (23 shorter events, 0.2 us)
Async XLA Ops:
  0.6 15.9 %copy-start.2 = (bf16[256,256]{1,0:T(8,128)(2,1)S(1)}, bf16[256,256]{1,0:T(8,128)(2,1)}, u32[]{:S(2)}) copy-start(bf16[256,256]{1,0:T(8,128)(2,1)} %nodes_ref.5) | copy-start | bytes 393220
  0.6 15.9 %copy-start.6 = (s32[8192]{0:T(1024)S(1)}, s32[8192]{0:T(1024)}, u32[]{:S(2)}) copy-start(s32[8192]{0:T(1024)} %param.14) | copy-start | bytes 98308
  1.9 11.9 %collective-permute-start = (bf16[2,64,256]{2,1,0:T(8,128)(2,1)S(1)}, bf16[2,64,256]{2,1,0:T(8,128)(2,1)S(1)}, u32[]{:S(2)}, u32[]{:S(2)}) collective-permute-start(bf16[2,64,256]{2,1,0:T(8,128)(2,1)S(1)} %get-tuple-element.28.c1_ref), channel_id=1, source_target_pairs={{0,4},{4,8},{8,12},{12,16},{16,20},{20,24},{24,28},{28,0},{1,5},{5... | collective-permute-start | bytes 196616 | tf_op jit(solution)/shard_map/ppermute | solution.py:335
  5.7 8.1 %collective-permute-start.1 = (bf16[2,64,256]{2,1,0:T(8,128)(2,1)S(1)}, bf16[2,64,256]{2,1,0:T(8,128)(2,1)S(1)}, u32[]{:S(2)}, u32[]{:S(2)}) collective-permute-start(bf16[2,64,256]{2,1,0:T(8,128)(2,1)S(1)} %get-tuple-element.29.c0_ref), channel_id=1, source_target_pairs={{4,0},{8,4},{12,8},{16,12},{20,16},{24,20},{28,24},{0,28},{5,1},{9... | collective-permute-start | bytes 196616 | tf_op jit(solution)/shard_map/ppermute | solution.py:335
  13.7 6.3 %copy-start = (bf16[2,256,768]{2,1,0:T(8,128)(2,1)S(1)}, bf16[2,256,768]{2,1,0:T(8,128)(2,1)}, u32[]{:S(2)}) copy-start(bf16[2,256,768]{2,1,0:T(8,128)(2,1)} %wqkv_ref.5) | copy-start | bytes 2359300
  13.7 6.3 %copy-start.3 = (s32[8192]{0:T(1024)S(1)}, s32[8192]{0:T(1024)}, u32[]{:S(2)}) copy-start(s32[8192]{0:T(1024)} %param.15) | copy-start | bytes 98308
  13.7 6.3 %copy-start.8 = (s32[1,1,1,2,2,64]{5,4,3,2,1,0:T(2,128)S(1)}, s32[1,1,1,2,2,64]{5,4,3,2,1,0:T(2,128)}, u32[]{:S(2)}) copy-start(s32[1,1,1,2,2,64]{5,4,3,2,1,0:T(2,128)} %param.17) | copy-start | bytes 3076
  13.8 6.3 %copy-start.9 = (f32[2,256]{1,0:T(2,128)S(1)}, f32[2,256]{1,0:T(2,128)}, u32[]{:S(2)}) copy-start(f32[2,256]{1,0:T(2,128)} %gain_ref.3) | copy-start | bytes 6148
  13.8 6.2 %collective-permute-start.2 = (bf16[4,64,256]{2,1,0:T(8,128)(2,1)S(1)}, bf16[4,64,256]{2,1,0:T(8,128)(2,1)S(1)}, u32[]{:S(2)}, u32[]{:S(2)}) collective-permute-start(bf16[4,64,256]{2,1,0:T(8,128)(2,1)S(1)} %get-tuple-element.34), channel_id=1, source_target_pairs={{0,1},{1,2},{2,3},{3,0},{4,5},{5,6},{6,7},{7,4},{8,9},{9,10},{10,1... | collective-permute-start | bytes 393224 | tf_op jit(solution)/shard_map/ppermute | solution.py:335
  15.1 4.9 %collective-permute-start.3 = (bf16[4,64,256]{2,1,0:T(8,128)(2,1)S(1)}, bf16[4,64,256]{2,1,0:T(8,128)(2,1)S(1)}, u32[]{:S(2)}, u32[]{:S(2)}) collective-permute-start(bf16[4,64,256]{2,1,0:T(8,128)(2,1)S(1)} %get-tuple-element.35), channel_id=1, source_target_pairs={{1,0},{2,1},{3,2},{0,3},{5,4},{6,5},{7,6},{4,7},{9,8},{10,9},{11,1... | collective-permute-start | bytes 393224 | tf_op jit(solution)/shard_map/ppermute | solution.py:335
  20.0 13.5 %copy-start.4 = (bf16[2,256,256]{2,1,0:T(8,128)(2,1)S(1)}, bf16[2,256,256]{2,1,0:T(8,128)(2,1)}, u32[]{:S(2)}) copy-start(bf16[2,256,256]{2,1,0:T(8,128)(2,1)} %wedge_ref.1) | copy-start | bytes 786436
  27.8 8.3 %collective-permute-start.4 = (bf16[2,64,256]{2,1,0:T(8,128)(2,1)S(1)}, bf16[2,64,256]{2,1,0:T(8,128)(2,1)S(1)}, u32[]{:S(2)}, u32[]{:S(2)}) collective-permute-start(bf16[2,64,256]{2,1,0:T(8,128)(2,1)S(1)} %get-tuple-element.39.c1_ref), channel_id=1, source_target_pairs={{0,4},{4,8},{8,12},{12,16},{16,20},{20,24},{24,28},{28,0},{1,5},{5... | collective-permute-start | bytes 196616 | tf_op jit(solution)/shard_map/ppermute | solution.py:335
  29.9 6.1 %collective-permute-start.5 = (bf16[2,64,256]{2,1,0:T(8,128)(2,1)S(1)}, bf16[2,64,256]{2,1,0:T(8,128)(2,1)S(1)}, u32[]{:S(2)}, u32[]{:S(2)}) collective-permute-start(bf16[2,64,256]{2,1,0:T(8,128)(2,1)S(1)} %get-tuple-element.40.c0_ref), channel_id=1, source_target_pairs={{4,0},{8,4},{12,8},{16,12},{20,16},{24,20},{28,24},{0,28},{5,1},{9... | collective-permute-start | bytes 196616 | tf_op jit(solution)/shard_map/ppermute | solution.py:335
  36.0 5.2 %copy-start.1 = (bf16[169,8192]{1,0:T(8,128)(2,1)S(1)}, bf16[169,8192]{1,0:T(8,128)(2,1)}, u32[]{:S(2)}) copy-start(bf16[169,8192]{1,0:T(8,128)(2,1)} %goal_ref.1) | copy-start | bytes 8306692
  36.0 5.2 %copy-start.5 = (bf16[256,256]{1,0:T(8,128)(2,1)S(1)}, bf16[256,256]{1,0:T(8,128)(2,1)}, u32[]{:S(2)}) copy-start(bf16[256,256]{1,0:T(8,128)(2,1)} %hin_ref.1) | copy-start | bytes 393220
  36.1 5.2 %copy-start.7 = (bf16[256,169]{0,1:T(8,128)(2,1)S(1)}, bf16[256,169]{0,1:T(8,128)(2,1)}, u32[]{:S(2)}) copy-start(bf16[256,169]{0,1:T(8,128)(2,1)} %param.22) | copy-start | bytes 259588
  36.1 5.1 %collective-permute-start.6 = (bf16[4,64,256]{2,1,0:T(8,128)(2,1)S(1)}, bf16[4,64,256]{2,1,0:T(8,128)(2,1)S(1)}, u32[]{:S(2)}, u32[]{:S(2)}) collective-permute-start(bf16[4,64,256]{2,1,0:T(8,128)(2,1)S(1)} %get-tuple-element.44), channel_id=1, source_target_pairs={{0,1},{1,2},{2,3},{3,0},{4,5},{5,6},{6,7},{7,4},{8,9},{9,10},{10,1... | collective-permute-start | bytes 393224 | tf_op jit(solution)/shard_map/ppermute | solution.py:335
  36.4 4.8 %collective-permute-start.7 = (bf16[4,64,256]{2,1,0:T(8,128)(2,1)S(1)}, bf16[4,64,256]{2,1,0:T(8,128)(2,1)S(1)}, u32[]{:S(2)}, u32[]{:S(2)}) collective-permute-start(bf16[4,64,256]{2,1,0:T(8,128)(2,1)S(1)} %get-tuple-element.45), channel_id=1, source_target_pairs={{1,0},{2,1},{3,2},{0,3},{5,4},{6,5},{7,6},{4,7},{9,8},{10,9},{11,1... | collective-permute-start | bytes 393224 | tf_op jit(solution)/shard_map/ppermute | solution.py:335
  54.9 1.5 %collective-permute-start.8 = (f32[64,8,128]{2,1,0:T(8,128)S(1)}, f32[64,8,128]{2,1,0:T(8,128)S(1)}, u32[]{:S(2)}, u32[]{:S(2)}) collective-permute-start(f32[64,8,128]{2,1,0:T(8,128)S(1)} %get-tuple-element.50), channel_id=1, source_target_pairs={{0,32},{32,0},{1,33},{33,1},{2,34},{34,2},{3,35},{35,3},{4,36},{36... | collective-permute-start | bytes 786440 | tf_op jit(solution)/shard_map/ppermute | solution.py:345

commit v7 on v6

--- a/solution.py
+++ b/solution.py
@@ -5,10 +5,9 @@
 from jax import lax
 from jax.experimental import pallas as pl
 from jax.experimental.pallas import tpu as pltpu
-from jax.sharding import Mesh
 from jax.sharding import PartitionSpec as P
 
-AXES = ("pair", "core", "gx", "gy")
+AXES = ("rep", "gx", "gy")
 BF = jnp.bfloat16
 F32 = jnp.float32
 BLOCK = 2048
@@ -223,8 +222,8 @@
 
 def second_kernel(
     count_ref, nodes_ref, low_ref, high_ref, wqkv_ref, gain_ref,
-    src_ref, dst_ref, near_ref, part_ref, edge_ref, core_ref, hin_ref, hout_ref, goal_ref,
-    out_nodes_ref, keep_ref, send_ref,
+    src_ref, dst_ref, near_ref, part_ref, edge_ref, hin_ref, hout_ref, goal_ref,
+    out_nodes_ref, grad_ref,
     far_t, wkv_t, acc, hl, target_hot, hin_t, hout, edges_s, dact_s, hidden_s, dpred_s, grad_in, grad_out,
     *, scale,
 ):
@@ -275,23 +274,13 @@
     @pl.when(step == pl.num_programs(0) - 1)
     def _():
         out_nodes_ref[...] = new_nodes(nodes_ref, acc, gain_ref[1:2, :])
-
-        def tiles_to(total, rows, to_ref):
+        tile = 0
+        for total, rows in ((grad_in, 32), (grad_out, 22)):
             for i in range(rows):
                 for j in range(2):
-                    to_ref[2 * i + j] = total[8 * i : 8 * i + 8, 128 * j : 128 * j + 128]
-            if rows < 32:
-                to_ref[2 * rows : 64] = jnp.zeros((64 - 2 * rows, 8, 128), F32)
-
-        @pl.when(core_ref[0] == 0)
-        def _():
-            tiles_to(grad_in, 32, keep_ref)
-            tiles_to(grad_out, 22, send_ref)
-
-        @pl.when(core_ref[0] == 1)
-        def _():
-            tiles_to(grad_out, 22, keep_ref)
-            tiles_to(grad_in, 32, send_ref)
+                    grad_ref[tile] = total[8 * i : 8 * i + 8, 128 * j : 128 * j + 128]
+                    tile += 1
+        grad_ref[tile:128] = jnp.zeros((128 - tile, 8, 128), F32)
 
 
 def whole(*shape):
@@ -341,16 +330,11 @@
     return shift(low, high, "gy")
 
 
-def swap_cores(x):
-    return lax.ppermute(x, "core", [(0, 1), (1, 0)])
-
-
 def body(node_feat, edge_feat, edge_src, edge_dst, edge_count, send_idx, w_qkv, w_edge, gains, head_in, head_out, targets):
     slots = edge_feat.shape[0]
     blocks = slots // BLOCK
     scale = 0.125 / (slots * lax.axis_size(AXES)) ** 0.5
-    core = lax.axis_index("core").astype(jnp.int32).reshape(1)
-    index, core = lax.optimization_barrier((send_idx.reshape(2, 2, 64), core))
+    index = send_idx.reshape(2, 2, 64)
     source = edge_src.reshape(blocks, 1, BLOCK)
     target = edge_dst.reshape(blocks, 1, BLOCK)
 
@@ -424,13 +408,12 @@
     before, after, part = lax.optimization_barrier((before, after, part))
     low, high = turn_sides(before, after, c0, c1)
     rows = near(nodes, before, after)
-    half = jax.ShapeDtypeStruct((64, 8, 128), F32)
-    nodes, keep, send = pl.pallas_call(
+    nodes, grads = pl.pallas_call(
         functools.partial(second_kernel, scale=scale),
         grid=(blocks,),
-        in_specs=layer_specs(1) + [SCALAR, whole(256, 256), whole(169, 256), pl.BlockSpec((169, BLOCK), lambda i: (0, i))],
-        out_specs=[whole(256, 256), whole(64, 8, 128), whole(64, 8, 128)],
-        out_shape=[square, half, half],
+        in_specs=layer_specs(1) + [whole(256, 256), whole(169, 256), pl.BlockSpec((169, BLOCK), lambda i: (0, i))],
+        out_specs=[whole(256, 256), whole(128, 8, 128)],
+        out_shape=[square, jax.ShapeDtypeStruct((128, 8, 128), F32)],
         scratch_shapes=LAYER_SCRATCH + [
             pltpu.VMEM((256, 256), BF), pltpu.VMEM((256, 169), BF), pltpu.VMEM((256, BLOCK), BF),
             pltpu.VMEM((256, BLOCK), BF), pltpu.VMEM((256, BLOCK), BF), pltpu.VMEM((169, BLOCK), BF),
@@ -439,29 +422,23 @@
         compiler_params=PARAMS,
     )(
         edge_count, nodes, low, high, w_qkv, gains, source, target, rows, part, edges,
-        core, head_in, head_out.T, targets,
+        head_in, head_out.T, targets,
     )
-    chips = ("pair", "gx", "gy")
-    parts = lax.all_to_all(keep + swap_cores(send), chips, 0, 0, tiled=True)
+    parts = lax.all_to_all(grads, AXES, 0, 0, tiled=True)
     share = jnp.sum(parts, axis=0)
     full = lax.all_to_all(jnp.broadcast_to(share[None], (128, 8, 128)), AXES, 0, 0, tiled=True)
-    full = full.reshape(2, 2, 32, 8, 128)
-    grad_in = full[:, 0].reshape(64, 8, 128)
-    grad_out = full[:, 1].reshape(64, 8, 128)[0:44]
-    grad_in = grad_in.reshape(32, 2, 8, 128).transpose(0, 2, 1, 3).reshape(256, 256)
-    grad_out = grad_out.reshape(22, 2, 8, 128).transpose(0, 2, 1, 3).reshape(176, 256)[0:169].T
+    grad_in = full[0:64].reshape(32, 2, 8, 128).transpose(0, 2, 1, 3).reshape(256, 256)
+    grad_out = full[64:108].reshape(22, 2, 8, 128).transpose(0, 2, 1, 3).reshape(176, 256)[0:169].T
     return nodes, grad_in, grad_out
 
 
 def solution(mesh):
-    shape = dict(mesh.shape)
-    cut = Mesh(mesh.devices.reshape(shape["rep"] // 2, 2, shape["gx"], shape["gy"]), AXES)
     tile = P(AXES)
     return jax.shard_map(
         body,
-        mesh=cut,
+        mesh=mesh,
         in_specs=(
-            P(AXES, None), P(AXES, None), tile, tile, tile, P(("pair", "core"), "gx", "gy", None, None, None),
+            P(AXES, None), P(AXES, None), tile, tile, tile, P("rep", "gx", "gy", None, None, None),
             P(), P(), P(), P(), P(), P(None, AXES),
         ),
         out_specs=(P(AXES, None), P(), P()),

time: 105 us -> 105 us (level)
  Pallas kernels: 33.6 us -> 24.5 us
  blocking collectives: 47 us -> 51.6 us
  starting transfers between devices: 18.6 us -> 21.7 us
  waiting for transfers between devices: 2.63 us -> 4.9 us
    all_to_all x1, blocking collectives: 27.6 us -> 34 us  [body(): parts = lax.all_to_all(grads, AXES, 0, 0, tiled=True)]
    pallas_call x1, Pallas kernels: 13.6 us -> 9.67 us  [body(): pl.pallas_call(functools.partial(second_kernel, scale=scale), grid=(block...]
    ppermute x8, waiting for transfers between devices: 1.1 us -> 4.9 us  [shift(): return (lax.ppermute(high, axis, up), lax.ppermute(low, axis, down))]
    ppermute x8, starting transfers between devices: 18.6 us -> 21.7 us  [shift(): return (lax.ppermute(high, axis, up), lax.ppermute(low, axis, down))]
    pallas_call x1, Pallas kernels: 7.72 us -> 5.42 us  [body(): pl.pallas_call(first_kernel, grid=(blocks,), in_specs=layer_specs(0) + [w...]
    all_to_all x1, blocking collectives: 19.4 us -> 17.6 us  [body(): lax.all_to_all(jnp.broadcast_to(share[None], (128, 8, 128)), AXES, 0, 0,...]
    ppermute x1 -> x0, waiting for transfers between devices: 1.53 us -> none  [swap_cores(): return lax.ppermute(x, 'core', [(0, 1), (1, 0)])]
    pallas_call x2, Pallas kernels: 4.66 us -> 3.25 us  [near(): pl.pallas_call(near_kernel, grid=(blocks,), in_specs=[SCALAR, whole(256,...]
  transfers between devices with their start and end apart: 9 -> 8, of which waited for: 2 -> 4; matrix products, arithmetic and copies ran while one was open for 0% -> 0% of each run, Pallas kernels for 10% -> 8%
where the time goes in v7:
time: 105 us; the launch traced here: 106 us
  blocking collectives  51.6 us (49%)
  Pallas kernels  24.5 us (23%)
  starting transfers between devices  21.7 us (21%)
  waiting for transfers between devices  4.9 us (5%)
  local copies, waits for them, and re-layouts  1.52 us (1%)
  between operations  1.49 us (1%)
    all_to_all x1, blocking collectives, body(): parts = lax.all_to_all(grads, AXES, 0, 0, tiled=True)  34 us
    ppermute x8, starting transfers between devices, shift(): return (lax.ppermute(high, axis, up), lax.ppermute(low, axis, down))  21.7 us
    all_to_all x1, blocking collectives, body(): lax.all_to_all(jnp.broadcast_to(share[None], (128, 8, 128)), AXES, 0, 0,...  17.6 us
    pallas_call x1, Pallas kernels, body(): pl.pallas_call(functools.partial(second_kernel, scale=scale), grid=(block...  9.67 us
    pallas_call x1, Pallas kernels, body(): pl.pallas_call(first_kernel, grid=(blocks,), in_specs=layer_specs(0) + [w...  5.42 us
    ppermute x8, waiting for transfers between devices, shift(): return (lax.ppermute(high, axis, up), lax.ppermute(low, axis, down))  4.9 us
    pallas_call x2, Pallas kernels, near(): pl.pallas_call(near_kernel, grid=(blocks,), in_specs=[SCALAR, whole(256,...  3.25 us
    pallas_call x1, Pallas kernels, first_part(): pl.pallas_call(first_part_kernel, grid=(blocks,), in_specs=[SCALAR] + [st...  3.1 us
  transfers between devices with their start and end apart: 8, of which 4 were waited for; matrix products, arithmetic and copies ran while one was open for 0% of the time, Pallas kernels for 8%

profile of v7, /device:TPU:1, one launch (start us, length us, event | category | flops | bytes accessed | tf_op | source)
XLA Modules:
  0.0 105.8 jit_solution(12839874674969282742)
XLA Ops:
  0.6 0.0 copy-start.2
  0.7 1.2 %shard_map.139 = (bf16[2,64,256]{2,1,0:T(8,128)(2,1)S(1)}, bf16[2,64,256]{2,1,0:T(8,128)(2,1)S(1)}) custom-call(bf16[256,256]{1,0:T(8,128)(2,1)} %nodes_ref.5, s32[2,2,64]{2,1,0:T(2,128)} %bitcast.25), custom_call_target="tpu_custom_call" | custom-call | tf_op jit(solution)/shard_map/pallas_call | solution.py:389
  1.9 3.8 %collective-permute-start = (bf16[2,64,256]{2,1,0:T(8,128)(2,1)S(1)}, bf16[2,64,256]{2,1,0:T(8,128)(2,1)S(1)}, u32[]{:S(2)}, u32[]{:S(2)}) collective-permute-start(bf16[2,64,256]{2,1,0:T(8,128)(2,1)S(1)} %get-tuple-element.24.c1_ref), channel_id=1, source_target_pairs={{0,4},{4,8},{8,12},{12,16},{16,20},{20,24},{24,28},{28,0},{1,5},{5... | collective-permute-start | bytes 196616 | tf_op jit(solution)/shard_map/ppermute | solution.py:324
  5.7 3.6 %collective-permute-start.1 = (bf16[2,64,256]{2,1,0:T(8,128)(2,1)S(1)}, bf16[2,64,256]{2,1,0:T(8,128)(2,1)S(1)}, u32[]{:S(2)}, u32[]{:S(2)}) collective-permute-start(bf16[2,64,256]{2,1,0:T(8,128)(2,1)S(1)} %get-tuple-element.25.c0_ref), channel_id=1, source_target_pairs={{4,0},{8,4},{12,8},{16,12},{20,16},{24,20},{28,24},{0,28},{5,1},{9... | collective-permute-start | bytes 196616 | tf_op jit(solution)/shard_map/ppermute | solution.py:324
  9.9 3.1 %shard_map.140 = (f32[4,256,2048]{2,1,0:T(8,128)S(1)}, bf16[4,256,2048]{2,1,0:T(8,128)(2,1)S(1)}) custom-call(s32[1]{0:T(128)S(6)} %copy.15.count_ref, bf16[256,256]{1,0:T(8,128)(2,1)} %nodes_ref.5, bf16[2,256,768]{2,1,0:T(8,128)(2,1)} %wqkv_ref.5, bf16[2,256,256]{2,1,0:T(8,128)(2,1)} %wedge_ref.1, s32[4,1,2048]{2,1,0:T(1,128)} %bitcast.16, ...), custom_call_target="tpu_custom_call" | custom-call | flops 2147483648 | bytes 12582912 | tf_op jit(solution)/shard_map/pallas_call | solution.py:350
  13.0 0.0 copy-start
  13.0 0.0 copy-start.3
  13.0 0.0 copy-start.8
  13.0 0.0 copy-start.9
  13.1 2.0 %collective-permute-start.2 = (bf16[4,64,256]{2,1,0:T(8,128)(2,1)S(1)}, bf16[4,64,256]{2,1,0:T(8,128)(2,1)S(1)}, u32[]{:S(2)}, u32[]{:S(2)}) collective-permute-start(bf16[4,64,256]{2,1,0:T(8,128)(2,1)S(1)} %get-tuple-element.30), channel_id=1, source_target_pairs={{0,1},{1,2},{2,3},{3,0},{4,5},{5,6},{6,7},{7,4},{8,9},{9,10},{10,1... | collective-permute-start | bytes 393224 | tf_op jit(solution)/shard_map/ppermute | solution.py:324
  15.1 0.7 collective-permute-start.3
  15.8 1.6 %shard_map.142.near_ref = bf16[4,256,2048]{2,1,0:T(8,128)(2,1)S(1)} custom-call(s32[1]{0:T(128)S(6)} %copy.15.count_ref, bf16[256,256]{1,0:T(8,128)(2,1)S(1)} %copy-done.2, bf16[2,64,256]{2,1,0:T(8,128)(2,1)S(1)} %collective-permute-done.before_ref, bf16[2,64,256]{2,1,0:T(8,128)(2,1)S(1)} %collective-permute-done.1.after_ref, s32[4,1,2048]{2,1,0:T(1,128)S(1)} %bitcast.20), custom_call_target="tpu_custom_call" | custom-call | flops 2147483648 | bytes 12582912 | tf_op jit(solution)/shard_map/pallas_call | solution.py:378
  17.5 0.7 collective-permute-done.2.low_ref
  18.2 1.2 %collective-permute-done.3.high_ref = bf16[4,64,256]{2,1,0:T(8,128)(2,1)S(1)} collective-permute-done((bf16[4,64,256]{2,1,0:T(8,128)(2,1)S(1)}, bf16[4,64,256]{2,1,0:T(8,128)(2,1)S(1)}, u32[]{:S(2)}, u32[]{:S(2)}) %collective-permute-start.3) | collective-permute-done | bytes 131104 | tf_op jit(solution)/shard_map/ppermute | solution.py:324
  19.4 0.0 copy-start.4
  19.4 5.4 %shard_map.143 = (bf16[256,256]{1,0:T(8,128)(2,1)S(1)}, bf16[2,64,256]{2,1,0:T(8,128)(2,1)S(1)}, bf16[2,64,256]{2,1,0:T(8,128)(2,1)S(1)}, bf16[4,256,2048]{2,1,0:T(8,128)(2,1)S(1)}) custom-call(s32[1]{0:T(128)S(6)} %copy.15.count_ref, bf16[256,256]{1,0:T(8,128)(2,1)S(1)} %copy-done.2, bf16[4,64,256]{2,1,0:T(8,128)(2,1)S(1)} %collective-permute-done.2.low_ref, ...), custom_call_target="tpu_custom_call" | custom-call | tf_op jit(solution)/shard_map/pallas_call | solution.py:396
  24.9 5.1 %collective-permute-start.4 = (bf16[2,64,256]{2,1,0:T(8,128)(2,1)S(1)}, bf16[2,64,256]{2,1,0:T(8,128)(2,1)S(1)}, u32[]{:S(2)}, u32[]{:S(2)}) collective-permute-start(bf16[2,64,256]{2,1,0:T(8,128)(2,1)S(1)} %get-tuple-element.35.c1_ref), channel_id=1, source_target_pairs={{0,4},{4,8},{8,12},{12,16},{16,20},{20,24},{24,28},{28,0},{1,5},{5... | collective-permute-start | bytes 196616 | tf_op jit(solution)/shard_map/ppermute | solution.py:324
  30.0 3.7 %collective-permute-start.5 = (bf16[2,64,256]{2,1,0:T(8,128)(2,1)S(1)}, bf16[2,64,256]{2,1,0:T(8,128)(2,1)S(1)}, u32[]{:S(2)}, u32[]{:S(2)}) collective-permute-start(bf16[2,64,256]{2,1,0:T(8,128)(2,1)S(1)} %get-tuple-element.36.c0_ref), channel_id=1, source_target_pairs={{4,0},{8,4},{12,8},{16,12},{20,16},{24,20},{28,24},{0,28},{5,1},{9... | collective-permute-start | bytes 196616 | tf_op jit(solution)/shard_map/ppermute | solution.py:324
  33.7 1.8 %shard_map.144.part_ref = f32[4,256,2048]{2,1,0:T(8,128)S(1)} custom-call(s32[1]{0:T(128)S(6)} %copy.15.count_ref, bf16[256,256]{1,0:T(8,128)(2,1)S(1)} %get-tuple-element.34.nodes_ref, bf16[2,256,768]{2,1,0:T(8,128)(2,1)S(1)} %copy-done, bf16[2,256,256]{2,1,0:T(8,128)(2,1)S(1)} %copy-done.4, s32[4,1,2048]{2,1,0:T(1,128)S(1)} %bitcast.18, ...), custom_call_target="tpu_custom_call" | custom-call | flops 2147483648 | bytes 12582912 | tf_op jit(solution)/shard_map/pallas_call | solution.py:366
  35.5 0.0 copy-start.1
  35.5 0.0 copy-start.5
  35.6 1.6 %collective-permute-start.6 = (bf16[4,64,256]{2,1,0:T(8,128)(2,1)S(1)}, bf16[4,64,256]{2,1,0:T(8,128)(2,1)S(1)}, u32[]{:S(2)}, u32[]{:S(2)}) collective-permute-start(bf16[4,64,256]{2,1,0:T(8,128)(2,1)S(1)} %get-tuple-element.40), channel_id=1, source_target_pairs={{0,1},{1,2},{2,3},{3,0},{4,5},{5,6},{6,7},{7,4},{8,9},{9,10},{10,1... | collective-permute-start | bytes 393224 | tf_op jit(solution)/shard_map/ppermute | solution.py:324
  37.2 1.1 %collective-permute-start.7 = (bf16[4,64,256]{2,1,0:T(8,128)(2,1)S(1)}, bf16[4,64,256]{2,1,0:T(8,128)(2,1)S(1)}, u32[]{:S(2)}, u32[]{:S(2)}) collective-permute-start(bf16[4,64,256]{2,1,0:T(8,128)(2,1)S(1)} %get-tuple-element.41), channel_id=1, source_target_pairs={{1,0},{2,1},{3,2},{0,3},{5,4},{6,5},{7,6},{4,7},{9,8},{10,9},{11,1... | collective-permute-start | bytes 393224 | tf_op jit(solution)/shard_map/ppermute | solution.py:324
  38.3 1.6 %shard_map.146.near_ref = bf16[4,256,2048]{2,1,0:T(8,128)(2,1)S(1)} custom-call(s32[1]{0:T(128)S(6)} %copy.15.count_ref, bf16[256,256]{1,0:T(8,128)(2,1)S(1)} %get-tuple-element.34.nodes_ref, bf16[2,64,256]{2,1,0:T(8,128)(2,1)S(1)} %collective-permute-done.4.before_ref, bf16[2,64,256]{2,1,0:T(8,128)(2,1)S(1)} %collective-permute-done.5.after_ref, ...), custom_call_target="tpu_custom_call" | custom-call | flops 2147483648 | bytes 12582912 | tf_op jit(solution)/shard_map/pallas_call | solution.py:378
  40.0 0.7 collective-permute-done.6.low_ref
  40.7 2.2 %collective-permute-done.7.high_ref = bf16[4,64,256]{2,1,0:T(8,128)(2,1)S(1)} collective-permute-done((bf16[4,64,256]{2,1,0:T(8,128)(2,1)S(1)}, bf16[4,64,256]{2,1,0:T(8,128)(2,1)S(1)}, u32[]{:S(2)}, u32[]{:S(2)}) %collective-permute-start.7) | collective-permute-done | bytes 131104 | tf_op jit(solution)/shard_map/ppermute | solution.py:324
  42.9 9.7 %shard_map.147 = (bf16[256,256]{1,0:T(8,128)(2,1)}, f32[128,8,128]{2,1,0:T(8,128)S(1)}) custom-call(s32[1]{0:T(128)S(6)} %copy.15.count_ref, bf16[256,256]{1,0:T(8,128)(2,1)S(1)} %get-tuple-element.34.nodes_ref, bf16[4,64,256]{2,1,0:T(8,128)(2,1)S(1)} %collective-permute-done.6.low_ref, bf16[4,64,256]{2,1,0:T(8,128)(2,1)S(1)} %collective-permute-done.7.high_ref, ...), custom_call_target="tpu_custom_call" | custom-call | tf_op jit(solution)/shard_map/pallas_call | solution.py:411
  52.6 34.0 %all_to_all.10 = f32[128,8,128]{2,1,0:T(8,128)S(1)} all-to-all(f32[128,8,128]{2,1,0:T(8,128)S(1)} %get-tuple-element.44), channel_id=1, replica_groups=mesh['rep'=4,'gx'=8,'gy'=4] {'rep','gx','gy'}, dimensions={0} | all-to-all | bytes 1048576 | tf_op jit(solution)/shard_map/all_to_all | solution.py:427
  86.6 0.1 reduce_sum.9
  86.8 17.6 %all_to_all.11 = f32[128,8,128]{2,1,0:T(8,128)S(1)} all-to-all(f32[128,8,128]{2,1,0:T(8,128)S(1)} %broadcast_in_dim.2), channel_id=1, replica_groups=mesh['rep'=4,'gx'=8,'gy'=4] {'rep','gx','gy'}, dimensions={0} | all-to-all | bytes 1048576 | tf_op jit(solution)/shard_map/all_to_all | solution.py:429
  104.4 0.7 slice_bitcast_fusion
  105.1 0.7 slice.12
  (20 shorter events, 0.1 us)
Async XLA Ops:
  0.6 15.2 %copy-start.2 = (bf16[256,256]{1,0:T(8,128)(2,1)S(1)}, bf16[256,256]{1,0:T(8,128)(2,1)}, u32[]{:S(2)}) copy-start(bf16[256,256]{1,0:T(8,128)(2,1)} %nodes_ref.5) | copy-start | bytes 393220
  0.6 15.2 %copy-start.6 = (s32[8192]{0:T(1024)S(1)}, s32[8192]{0:T(1024)}, u32[]{:S(2)}) copy-start(s32[8192]{0:T(1024)} %param.14) | copy-start | bytes 98308
  1.9 11.2 %collective-permute-start = (bf16[2,64,256]{2,1,0:T(8,128)(2,1)S(1)}, bf16[2,64,256]{2,1,0:T(8,128)(2,1)S(1)}, u32[]{:S(2)}, u32[]{:S(2)}) collective-permute-start(bf16[2,64,256]{2,1,0:T(8,128)(2,1)S(1)} %get-tuple-element.24.c1_ref), channel_id=1, source_target_pairs={{0,4},{4,8},{8,12},{12,16},{16,20},{20,24},{24,28},{28,0},{1,5},{5... | collective-permute-start | bytes 196616 | tf_op jit(solution)/shard_map/ppermute | solution.py:324
  5.7 7.4 %collective-permute-start.1 = (bf16[2,64,256]{2,1,0:T(8,128)(2,1)S(1)}, bf16[2,64,256]{2,1,0:T(8,128)(2,1)S(1)}, u32[]{:S(2)}, u32[]{:S(2)}) collective-permute-start(bf16[2,64,256]{2,1,0:T(8,128)(2,1)S(1)} %get-tuple-element.25.c0_ref), channel_id=1, source_target_pairs={{4,0},{8,4},{12,8},{16,12},{20,16},{24,20},{28,24},{0,28},{5,1},{9... | collective-permute-start | bytes 196616 | tf_op jit(solution)/shard_map/ppermute | solution.py:324
  13.0 6.4 %copy-start = (bf16[2,256,768]{2,1,0:T(8,128)(2,1)S(1)}, bf16[2,256,768]{2,1,0:T(8,128)(2,1)}, u32[]{:S(2)}) copy-start(bf16[2,256,768]{2,1,0:T(8,128)(2,1)} %wqkv_ref.5) | copy-start | bytes 2359300
  13.0 6.4 %copy-start.3 = (s32[8192]{0:T(1024)S(1)}, s32[8192]{0:T(1024)}, u32[]{:S(2)}) copy-start(s32[8192]{0:T(1024)} %param.15) | copy-start | bytes 98308
  13.0 6.4 %copy-start.8 = (s32[1,1,1,2,2,64]{5,4,3,2,1,0:T(2,128)S(1)}, s32[1,1,1,2,2,64]{5,4,3,2,1,0:T(2,128)}, u32[]{:S(2)}) copy-start(s32[1,1,1,2,2,64]{5,4,3,2,1,0:T(2,128)} %param.17) | copy-start | bytes 3076
  13.0 6.4 %copy-start.9 = (f32[2,256]{1,0:T(2,128)S(1)}, f32[2,256]{1,0:T(2,128)}, u32[]{:S(2)}) copy-start(f32[2,256]{1,0:T(2,128)} %gain_ref.3) | copy-start | bytes 6148
  13.1 5.1 %collective-permute-start.2 = (bf16[4,64,256]{2,1,0:T(8,128)(2,1)S(1)}, bf16[4,64,256]{2,1,0:T(8,128)(2,1)S(1)}, u32[]{:S(2)}, u32[]{:S(2)}) collective-permute-start(bf16[4,64,256]{2,1,0:T(8,128)(2,1)S(1)} %get-tuple-element.30), channel_id=1, source_target_pairs={{0,1},{1,2},{2,3},{3,0},{4,5},{5,6},{6,7},{7,4},{8,9},{9,10},{10,1... | collective-permute-start | bytes 393224 | tf_op jit(solution)/shard_map/ppermute | solution.py:324
  15.1 4.3 %collective-permute-start.3 = (bf16[4,64,256]{2,1,0:T(8,128)(2,1)S(1)}, bf16[4,64,256]{2,1,0:T(8,128)(2,1)S(1)}, u32[]{:S(2)}, u32[]{:S(2)}) collective-permute-start(bf16[4,64,256]{2,1,0:T(8,128)(2,1)S(1)} %get-tuple-element.31), channel_id=1, source_target_pairs={{1,0},{2,1},{3,2},{0,3},{5,4},{6,5},{7,6},{4,7},{9,8},{10,9},{11,1... | collective-permute-start | bytes 393224 | tf_op jit(solution)/shard_map/ppermute | solution.py:324
  19.4 14.3 %copy-start.4 = (bf16[2,256,256]{2,1,0:T(8,128)(2,1)S(1)}, bf16[2,256,256]{2,1,0:T(8,128)(2,1)}, u32[]{:S(2)}) copy-start(bf16[2,256,256]{2,1,0:T(8,128)(2,1)} %wedge_ref.1) | copy-start | bytes 786436
  24.9 10.7 %collective-permute-start.4 = (bf16[2,64,256]{2,1,0:T(8,128)(2,1)S(1)}, bf16[2,64,256]{2,1,0:T(8,128)(2,1)S(1)}, u32[]{:S(2)}, u32[]{:S(2)}) collective-permute-start(bf16[2,64,256]{2,1,0:T(8,128)(2,1)S(1)} %get-tuple-element.35.c1_ref), channel_id=1, source_target_pairs={{0,4},{4,8},{8,12},{12,16},{16,20},{20,24},{24,28},{28,0},{1,5},{5... | collective-permute-start | bytes 196616 | tf_op jit(solution)/shard_map/ppermute | solution.py:324
  30.0 5.6 %collective-permute-start.5 = (bf16[2,64,256]{2,1,0:T(8,128)(2,1)S(1)}, bf16[2,64,256]{2,1,0:T(8,128)(2,1)S(1)}, u32[]{:S(2)}, u32[]{:S(2)}) collective-permute-start(bf16[2,64,256]{2,1,0:T(8,128)(2,1)S(1)} %get-tuple-element.36.c0_ref), channel_id=1, source_target_pairs={{4,0},{8,4},{12,8},{16,12},{20,16},{24,20},{28,24},{0,28},{5,1},{9... | collective-permute-start | bytes 196616 | tf_op jit(solution)/shard_map/ppermute | solution.py:324
  35.5 7.4 %copy-start.1 = (bf16[169,8192]{1,0:T(8,128)(2,1)S(1)}, bf16[169,8192]{1,0:T(8,128)(2,1)}, u32[]{:S(2)}) copy-start(bf16[169,8192]{1,0:T(8,128)(2,1)} %goal_ref.1) | copy-start | bytes 8306692
  35.5 7.4 %copy-start.5 = (bf16[256,256]{1,0:T(8,128)(2,1)S(1)}, bf16[256,256]{1,0:T(8,128)(2,1)}, u32[]{:S(2)}) copy-start(bf16[256,256]{1,0:T(8,128)(2,1)} %hin_ref.1) | copy-start | bytes 393220
  35.5 7.4 %copy-start.7 = (bf16[256,169]{0,1:T(8,128)(2,1)S(1)}, bf16[256,169]{0,1:T(8,128)(2,1)}, u32[]{:S(2)}) copy-start(bf16[256,169]{0,1:T(8,128)(2,1)} %param.22) | copy-start | bytes 259588
  35.6 5.1 %collective-permute-start.6 = (bf16[4,64,256]{2,1,0:T(8,128)(2,1)S(1)}, bf16[4,64,256]{2,1,0:T(8,128)(2,1)S(1)}, u32[]{:S(2)}, u32[]{:S(2)}) collective-permute-start(bf16[4,64,256]{2,1,0:T(8,128)(2,1)S(1)} %get-tuple-element.40), channel_id=1, source_target_pairs={{0,1},{1,2},{2,3},{3,0},{4,5},{5,6},{6,7},{7,4},{8,9},{9,10},{10,1... | collective-permute-start | bytes 393224 | tf_op jit(solution)/shard_map/ppermute | solution.py:324
  37.2 5.7 %collective-permute-start.7 = (bf16[4,64,256]{2,1,0:T(8,128)(2,1)S(1)}, bf16[4,64,256]{2,1,0:T(8,128)(2,1)S(1)}, u32[]{:S(2)}, u32[]{:S(2)}) collective-permute-start(bf16[4,64,256]{2,1,0:T(8,128)(2,1)S(1)} %get-tuple-element.41), channel_id=1, source_target_pairs={{1,0},{2,1},{3,2},{0,3},{5,4},{6,5},{7,6},{4,7},{9,8},{10,9},{11,1... | collective-permute-start | bytes 393224 | tf_op jit(solution)/shard_map/ppermute | solution.py:324

commit v8 on v6

--- a/solution.py
+++ b/solution.py
@@ -224,7 +224,7 @@
 def second_kernel(
     count_ref, nodes_ref, low_ref, high_ref, wqkv_ref, gain_ref,
     src_ref, dst_ref, near_ref, part_ref, edge_ref, core_ref, hin_ref, hout_ref, goal_ref,
-    out_nodes_ref, keep_ref, send_ref,
+    acc_ref, keep_ref, send_ref,
     far_t, wkv_t, acc, hl, target_hot, hin_t, hout, edges_s, dact_s, hidden_s, dpred_s, grad_in, grad_out,
     *, scale,
 ):
@@ -274,7 +274,7 @@
 
     @pl.when(step == pl.num_programs(0) - 1)
     def _():
-        out_nodes_ref[...] = new_nodes(nodes_ref, acc, gain_ref[1:2, :])
+        acc_ref[...] = acc[...]
 
         def tiles_to(total, rows, to_ref):
             for i in range(rows):
@@ -292,6 +292,10 @@
         def _():
             tiles_to(grad_out, 22, keep_ref)
             tiles_to(grad_in, 32, send_ref)
+
+
+def update_kernel(nodes_ref, acc_ref, gain_ref, out_nodes_ref):
+    out_nodes_ref[...] = new_nodes(nodes_ref, acc_ref, gain_ref[1:2, :])
 
 
 def whole(*shape):
@@ -425,12 +429,12 @@
     low, high = turn_sides(before, after, c0, c1)
     rows = near(nodes, before, after)
     half = jax.ShapeDtypeStruct((64, 8, 128), F32)
-    nodes, keep, send = pl.pallas_call(
+    acc, keep, send = pl.pallas_call(
         functools.partial(second_kernel, scale=scale),
         grid=(blocks,),
         in_specs=layer_specs(1) + [SCALAR, whole(256, 256), whole(169, 256), pl.BlockSpec((169, BLOCK), lambda i: (0, i))],
-        out_specs=[whole(256, 256), whole(64, 8, 128), whole(64, 8, 128)],
-        out_shape=[square, half, half],
+        out_specs=[whole(512, 256), whole(64, 8, 128), whole(64, 8, 128)],
+        out_shape=[jax.ShapeDtypeStruct((512, 256), F32), half, half],
         scratch_shapes=LAYER_SCRATCH + [
             pltpu.VMEM((256, 256), BF), pltpu.VMEM((256, 169), BF), pltpu.VMEM((256, BLOCK), BF),
             pltpu.VMEM((256, BLOCK), BF), pltpu.VMEM((256, BLOCK), BF), pltpu.VMEM((169, BLOCK), BF),
@@ -442,7 +446,10 @@
         core, head_in, head_out.T, targets,
     )
     chips = ("pair", "gx", "gy")
-    parts = lax.all_to_all(keep + swap_cores(send), chips, 0, 0, tiled=True)
+    other = swap_cores(send)
+    nodes = pl.pallas_call(update_kernel, out_shape=square, compiler_params=SMALL, cost_estimate=cost(1))(nodes, acc, gains)
+    other, nodes = lax.optimization_barrier((other, nodes))
+    parts = lax.all_to_all(keep + other, chips, 0, 0, tiled=True)
     share = jnp.sum(parts, axis=0)
     full = lax.all_to_all(jnp.broadcast_to(share[None], (128, 8, 128)), AXES, 0, 0, tiled=True)
     full = full.reshape(2, 2, 32, 8, 128)

time: 105 us -> 103 us (0.981)
  starting transfers between devices: 18.6 us -> 24.3 us
  blocking collectives: 47 us -> 42.4 us
  waiting for transfers between devices: 2.63 us -> 0.19 us
    all_to_all x1, blocking collectives: 27.6 us -> 23 us  [body(): parts = lax.all_to_all(keep + other, chips, 0, 0, tiled=True)]
    ppermute x1, starting transfers between devices: 0.01 us -> 4.46 us  [swap_cores(): return lax.ppermute(x, 'core', [(0, 1), (1, 0)])]
    ppermute x1, waiting for transfers between devices: 1.53 us -> 0.16 us  [swap_cores(): return lax.ppermute(x, 'core', [(0, 1), (1, 0)])]
    ppermute x8, starting transfers between devices: 18.6 us -> 19.8 us  [shift(): return (lax.ppermute(high, axis, up), lax.ppermute(low, axis, down))]
    ppermute x8, waiting for transfers between devices: 1.1 us -> 0.03 us  [shift(): return (lax.ppermute(high, axis, up), lax.ppermute(low, axis, down))]
  transfers between devices with their start and end apart: 9 -> 9, of which waited for: 2 -> 1; matrix products, arithmetic and copies ran while one was open for 0% -> 0% of each run, Pallas kernels for 10% -> 12%
where the time goes in v8:
time: 103 us; the launch traced here: 104 us
  blocking collectives  42.4 us (41%)
  Pallas kernels  33.7 us (33%)
  starting transfers between devices  24.3 us (24%)
  between operations  1.57 us (2%)
  local copies, waits for them, and re-layouts  1.53 us (1%)
    all_to_all x1, blocking collectives, body(): parts = lax.all_to_all(keep + other, chips, 0, 0, tiled=True)  23 us
    ppermute x8, starting transfers between devices, shift(): return (lax.ppermute(high, axis, up), lax.ppermute(low, axis, down))  19.8 us
    all_to_all x1, blocking collectives, body(): lax.all_to_all(jnp.broadcast_to(share[None], (128, 8, 128)), AXES, 0, 0,...  19.4 us
    pallas_call x1, Pallas kernels, body(): pl.pallas_call(functools.partial(second_kernel, scale=scale), grid=(block...  12.7 us
    pallas_call x1, Pallas kernels, body(): pl.pallas_call(first_kernel, grid=(blocks,), in_specs=layer_specs(0) + [w...  7.72 us
    pallas_call x2, Pallas kernels, near(): pl.pallas_call(near_kernel, grid=(blocks,), in_specs=[SCALAR, whole(256,...  4.66 us
    ppermute x1, starting transfers between devices, swap_cores(): return lax.ppermute(x, 'core', [(0, 1), (1, 0)])  4.46 us
    pallas_call x1, Pallas kernels, first_part(): pl.pallas_call(first_part_kernel, grid=(blocks,), in_specs=[SCALAR] + [st...  3.83 us
  transfers between devices with their start and end apart: 9, of which 1 were waited for; matrix products, arithmetic and copies ran while one was open for 0% of the time, Pallas kernels for 12%

profile of v8, /device:TPU:1, one launch (start us, length us, event | category | flops | bytes accessed | tf_op | source)
XLA Modules:
  0.0 103.7 jit_solution(2622901196307419513)
XLA Ops:
  0.6 0.0 copy-start.2
  0.7 1.2 %shard_map.139 = (bf16[2,64,256]{2,1,0:T(8,128)(2,1)S(1)}, bf16[2,64,256]{2,1,0:T(8,128)(2,1)S(1)}) custom-call(bf16[256,256]{1,0:T(8,128)(2,1)} %nodes_ref.5, s32[2,2,64]{2,1,0:T(2,128)} %bitcast.28), custom_call_target="tpu_custom_call" | custom-call | tf_op jit(solution)/shard_map/pallas_call | solution.py:409
  1.9 3.8 %collective-permute-start = (bf16[2,64,256]{2,1,0:T(8,128)(2,1)S(1)}, bf16[2,64,256]{2,1,0:T(8,128)(2,1)S(1)}, u32[]{:S(2)}, u32[]{:S(2)}) collective-permute-start(bf16[2,64,256]{2,1,0:T(8,128)(2,1)S(1)} %get-tuple-element.30.c1_ref), channel_id=1, source_target_pairs={{0,4},{4,8},{8,12},{12,16},{16,20},{20,24},{24,28},{28,0},{1,5},{5... | collective-permute-start | bytes 196616 | tf_op jit(solution)/shard_map/ppermute | solution.py:339
  5.7 3.6 %collective-permute-start.1 = (bf16[2,64,256]{2,1,0:T(8,128)(2,1)S(1)}, bf16[2,64,256]{2,1,0:T(8,128)(2,1)S(1)}, u32[]{:S(2)}, u32[]{:S(2)}) collective-permute-start(bf16[2,64,256]{2,1,0:T(8,128)(2,1)S(1)} %get-tuple-element.31.c0_ref), channel_id=1, source_target_pairs={{4,0},{8,4},{12,8},{16,12},{20,16},{24,20},{28,24},{0,28},{5,1},{9... | collective-permute-start | bytes 196616 | tf_op jit(solution)/shard_map/ppermute | solution.py:339
  9.9 3.8 %shard_map.140 = (f32[4,256,2048]{2,1,0:T(8,128)S(1)}, bf16[4,256,2048]{2,1,0:T(8,128)(2,1)S(1)}) custom-call(s32[1]{0:T(128)S(6)} %copy.15.count_ref, bf16[256,256]{1,0:T(8,128)(2,1)} %nodes_ref.5, bf16[2,256,768]{2,1,0:T(8,128)(2,1)} %wqkv_ref.5, bf16[2,256,256]{2,1,0:T(8,128)(2,1)} %wedge_ref.1, s32[4,1,2048]{2,1,0:T(1,128)} %bitcast.19, ...), custom_call_target="tpu_custom_call" | custom-call | flops 2147483648 | bytes 12582912 | tf_op jit(solution)/shard_map/pallas_call | solution.py:370
  13.7 0.0 copy-start
  13.7 0.0 copy-start.3
  13.7 0.0 copy-start.8
  13.8 0.0 copy-start.9
  13.8 1.3 %collective-permute-start.2 = (bf16[4,64,256]{2,1,0:T(8,128)(2,1)S(1)}, bf16[4,64,256]{2,1,0:T(8,128)(2,1)S(1)}, u32[]{:S(2)}, u32[]{:S(2)}) collective-permute-start(bf16[4,64,256]{2,1,0:T(8,128)(2,1)S(1)} %get-tuple-element.36), channel_id=1, source_target_pairs={{0,1},{1,2},{2,3},{3,0},{4,5},{5,6},{6,7},{7,4},{8,9},{9,10},{10,1... | collective-permute-start | bytes 393224 | tf_op jit(solution)/shard_map/ppermute | solution.py:339
  15.1 1.5 %collective-permute-start.3 = (bf16[4,64,256]{2,1,0:T(8,128)(2,1)S(1)}, bf16[4,64,256]{2,1,0:T(8,128)(2,1)S(1)}, u32[]{:S(2)}, u32[]{:S(2)}) collective-permute-start(bf16[4,64,256]{2,1,0:T(8,128)(2,1)S(1)} %get-tuple-element.37), channel_id=1, source_target_pairs={{1,0},{2,1},{3,2},{0,3},{5,4},{6,5},{7,6},{4,7},{9,8},{10,9},{11,1... | collective-permute-start | bytes 393224 | tf_op jit(solution)/shard_map/ppermute | solution.py:339
  16.6 2.3 %shard_map.142.near_ref = bf16[4,256,2048]{2,1,0:T(8,128)(2,1)S(1)} custom-call(s32[1]{0:T(128)S(6)} %copy.15.count_ref, bf16[256,256]{1,0:T(8,128)(2,1)S(1)} %copy-done.2, bf16[2,64,256]{2,1,0:T(8,128)(2,1)S(1)} %collective-permute-done.before_ref, bf16[2,64,256]{2,1,0:T(8,128)(2,1)S(1)} %collective-permute-done.1.after_ref, s32[4,1,2048]{2,1,0:T(1,128)S(1)} %bitcast.23), custom_call_target="tpu_custom_call" | custom-call | flops 2147483648 | bytes 12582912 | tf_op jit(solution)/shard_map/pallas_call | solution.py:398
  18.9 0.0 collective-permute-done.2.low_ref
  19.0 0.0 copy-start.4
  19.0 7.7 %shard_map.143 = (bf16[256,256]{1,0:T(8,128)(2,1)S(1)}, bf16[2,64,256]{2,1,0:T(8,128)(2,1)S(1)}, bf16[2,64,256]{2,1,0:T(8,128)(2,1)S(1)}, bf16[4,256,2048]{2,1,0:T(8,128)(2,1)S(1)}) custom-call(s32[1]{0:T(128)S(6)} %copy.15.count_ref, bf16[256,256]{1,0:T(8,128)(2,1)S(1)} %copy-done.2, bf16[4,64,256]{2,1,0:T(8,128)(2,1)S(1)} %collective-permute-done.2.low_ref, ...), custom_call_target="tpu_custom_call" | custom-call | tf_op jit(solution)/shard_map/pallas_call | solution.py:416
  26.7 0.1 collective-permute-start.4
  26.8 6.9 %collective-permute-start.5 = (bf16[2,64,256]{2,1,0:T(8,128)(2,1)S(1)}, bf16[2,64,256]{2,1,0:T(8,128)(2,1)S(1)}, u32[]{:S(2)}, u32[]{:S(2)}) collective-permute-start(bf16[2,64,256]{2,1,0:T(8,128)(2,1)S(1)} %get-tuple-element.42.c0_ref), channel_id=1, source_target_pairs={{4,0},{8,4},{12,8},{16,12},{20,16},{24,20},{28,24},{0,28},{5,1},{9... | collective-permute-start | bytes 196616 | tf_op jit(solution)/shard_map/ppermute | solution.py:339
  33.7 2.5 %shard_map.144.part_ref = f32[4,256,2048]{2,1,0:T(8,128)S(1)} custom-call(s32[1]{0:T(128)S(6)} %copy.15.count_ref, bf16[256,256]{1,0:T(8,128)(2,1)S(1)} %get-tuple-element.40.nodes_ref, bf16[2,256,768]{2,1,0:T(8,128)(2,1)S(1)} %copy-done, bf16[2,256,256]{2,1,0:T(8,128)(2,1)S(1)} %copy-done.4, s32[4,1,2048]{2,1,0:T(1,128)S(1)} %bitcast.21, ...), custom_call_target="tpu_custom_call" | custom-call | flops 2147483648 | bytes 12582912 | tf_op jit(solution)/shard_map/pallas_call | solution.py:386
  36.2 0.0 copy-start.7
  36.3 0.1 collective-permute-start.6
  36.4 2.7 %collective-permute-start.7 = (bf16[4,64,256]{2,1,0:T(8,128)(2,1)S(1)}, bf16[4,64,256]{2,1,0:T(8,128)(2,1)S(1)}, u32[]{:S(2)}, u32[]{:S(2)}) collective-permute-start(bf16[4,64,256]{2,1,0:T(8,128)(2,1)S(1)} %get-tuple-element.47), channel_id=1, source_target_pairs={{1,0},{2,1},{3,2},{0,3},{5,4},{6,5},{7,6},{4,7},{9,8},{10,9},{11,1... | collective-permute-start | bytes 393224 | tf_op jit(solution)/shard_map/ppermute | solution.py:339
  39.0 2.3 %shard_map.146.near_ref = bf16[4,256,2048]{2,1,0:T(8,128)(2,1)S(1)} custom-call(s32[1]{0:T(128)S(6)} %copy.15.count_ref, bf16[256,256]{1,0:T(8,128)(2,1)S(1)} %get-tuple-element.40.nodes_ref, bf16[2,64,256]{2,1,0:T(8,128)(2,1)S(1)} %collective-permute-done.4.before_ref, bf16[2,64,256]{2,1,0:T(8,128)(2,1)S(1)} %collective-permute-done.5.after_ref, ...), custom_call_target="tpu_custom_call" | custom-call | flops 2147483648 | bytes 12582912 | tf_op jit(solution)/shard_map/pallas_call | solution.py:398
  41.4 0.0 collective-permute-done.6.low_ref
  41.4 12.7 %shard_map.147 = (f32[512,256]{1,0:T(8,128)S(1)}, f32[64,8,128]{2,1,0:T(8,128)S(1)}, f32[64,8,128]{2,1,0:T(8,128)S(1)}) custom-call(s32[1]{0:T(128)S(6)} %copy.15.count_ref, bf16[256,256]{1,0:T(8,128)(2,1)S(1)} %get-tuple-element.40.nodes_ref, bf16[4,64,256]{2,1,0:T(8,128)(2,1)S(1)} %collective-permute-done.6.low_ref, ...), custom_call_target="tpu_custom_call" | custom-call | tf_op jit(solution)/shard_map/pallas_call | solution.py:432
  54.1 4.5 %collective-permute-start.8 = (f32[64,8,128]{2,1,0:T(8,128)S(1)}, f32[64,8,128]{2,1,0:T(8,128)S(1)}, u32[]{:S(2)}, u32[]{:S(2)}) collective-permute-start(f32[64,8,128]{2,1,0:T(8,128)S(1)} %get-tuple-element.50), channel_id=1, source_target_pairs={{0,32},{32,0},{1,33},{33,1},{2,34},{34,2},{3,35},{35,3},{4,36},{36... | collective-permute-start | bytes 786440 | tf_op jit(solution)/shard_map/ppermute | solution.py:349
  58.6 1.0 shard_map.148
  59.6 0.2 collective-permute-done.8
  59.8 23.0 %all_to_all.10 = f32[64,8,128]{2,1,0:T(8,128)S(1)} all-to-all(f32[64,8,128]{2,1,0:T(8,128)S(1)} %add.3), channel_id=1, replica_groups=mesh['pair'=2,'core'=2,'gx'=8,'gy'=4] {'pair','gx','gy'}, dimensions={0} | all-to-all | bytes 524288 | tf_op jit(solution)/shard_map/all_to_all | solution.py:452
  82.8 0.1 reduce_sum.9
  82.9 19.4 %all_to_all.11 = f32[128,8,128]{2,1,0:T(8,128)S(1)} all-to-all(f32[128,8,128]{2,1,0:T(8,128)S(1)} %broadcast_in_dim.2), channel_id=1, replica_groups=mesh['pair'=2,'core'=2,'gx'=8,'gy'=4] {'pair','core','gx','gy'}, dimensions={0} | all-to-all | bytes 1048576 | tf_op jit(solution)/shard_map/all_to_all | solution.py:454
  102.3 0.7 fusion
  103.1 0.7 slice_bitcast_fusion
  (24 shorter events, 0.2 us)
Async XLA Ops:
  0.6 15.9 %copy-start.2 = (bf16[256,256]{1,0:T(8,128)(2,1)S(1)}, bf16[256,256]{1,0:T(8,128)(2,1)}, u32[]{:S(2)}) copy-start(bf16[256,256]{1,0:T(8,128)(2,1)} %nodes_ref.5) | copy-start | bytes 393220
  0.6 15.9 %copy-start.6 = (s32[8192]{0:T(1024)S(1)}, s32[8192]{0:T(1024)}, u32[]{:S(2)}) copy-start(s32[8192]{0:T(1024)} %param.14) | copy-start | bytes 98308
  1.9 11.9 %collective-permute-start = (bf16[2,64,256]{2,1,0:T(8,128)(2,1)S(1)}, bf16[2,64,256]{2,1,0:T(8,128)(2,1)S(1)}, u32[]{:S(2)}, u32[]{:S(2)}) collective-permute-start(bf16[2,64,256]{2,1,0:T(8,128)(2,1)S(1)} %get-tuple-element.30.c1_ref), channel_id=1, source_target_pairs={{0,4},{4,8},{8,12},{12,16},{16,20},{20,24},{24,28},{28,0},{1,5},{5... | collective-permute-start | bytes 196616 | tf_op jit(solution)/shard_map/ppermute | solution.py:339
  5.7 8.1 %collective-permute-start.1 = (bf16[2,64,256]{2,1,0:T(8,128)(2,1)S(1)}, bf16[2,64,256]{2,1,0:T(8,128)(2,1)S(1)}, u32[]{:S(2)}, u32[]{:S(2)}) collective-permute-start(bf16[2,64,256]{2,1,0:T(8,128)(2,1)S(1)} %get-tuple-element.31.c0_ref), channel_id=1, source_target_pairs={{4,0},{8,4},{12,8},{16,12},{20,16},{24,20},{28,24},{0,28},{5,1},{9... | collective-permute-start | bytes 196616 | tf_op jit(solution)/shard_map/ppermute | solution.py:339
  13.7 5.2 %copy-start = (bf16[2,256,768]{2,1,0:T(8,128)(2,1)S(1)}, bf16[2,256,768]{2,1,0:T(8,128)(2,1)}, u32[]{:S(2)}) copy-start(bf16[2,256,768]{2,1,0:T(8,128)(2,1)} %wqkv_ref.5) | copy-start | bytes 2359300
  13.7 5.2 %copy-start.3 = (s32[8192]{0:T(1024)S(1)}, s32[8192]{0:T(1024)}, u32[]{:S(2)}) copy-start(s32[8192]{0:T(1024)} %param.15) | copy-start | bytes 98308
  13.7 5.2 %copy-start.8 = (s32[1,1,1,2,2,64]{5,4,3,2,1,0:T(2,128)S(1)}, s32[1,1,1,2,2,64]{5,4,3,2,1,0:T(2,128)}, u32[]{:S(2)}) copy-start(s32[1,1,1,2,2,64]{5,4,3,2,1,0:T(2,128)} %param.17) | copy-start | bytes 3076
  13.8 5.2 %copy-start.9 = (f32[2,256]{1,0:T(2,128)S(1)}, f32[2,256]{1,0:T(2,128)}, u32[]{:S(2)}) copy-start(f32[2,256]{1,0:T(2,128)} %gain_ref.5) | copy-start | bytes 6148
  13.8 5.1 %collective-permute-start.2 = (bf16[4,64,256]{2,1,0:T(8,128)(2,1)S(1)}, bf16[4,64,256]{2,1,0:T(8,128)(2,1)S(1)}, u32[]{:S(2)}, u32[]{:S(2)}) collective-permute-start(bf16[4,64,256]{2,1,0:T(8,128)(2,1)S(1)} %get-tuple-element.36), channel_id=1, source_target_pairs={{0,1},{1,2},{2,3},{3,0},{4,5},{5,6},{6,7},{7,4},{8,9},{9,10},{10,1... | collective-permute-start | bytes 393224 | tf_op jit(solution)/shard_map/ppermute | solution.py:339
  15.1 3.8 %collective-permute-start.3 = (bf16[4,64,256]{2,1,0:T(8,128)(2,1)S(1)}, bf16[4,64,256]{2,1,0:T(8,128)(2,1)S(1)}, u32[]{:S(2)}, u32[]{:S(2)}) collective-permute-start(bf16[4,64,256]{2,1,0:T(8,128)(2,1)S(1)} %get-tuple-element.37), channel_id=1, source_target_pairs={{1,0},{2,1},{3,2},{0,3},{5,4},{6,5},{7,6},{4,7},{9,8},{10,9},{11,1... | collective-permute-start | bytes 393224 | tf_op jit(solution)/shard_map/ppermute | solution.py:339
  19.0 14.7 %copy-start.4 = (bf16[2,256,256]{2,1,0:T(8,128)(2,1)S(1)}, bf16[2,256,256]{2,1,0:T(8,128)(2,1)}, u32[]{:S(2)}) copy-start(bf16[2,256,256]{2,1,0:T(8,128)(2,1)} %wedge_ref.1) | copy-start | bytes 786436
  26.7 9.5 %collective-permute-start.4 = (bf16[2,64,256]{2,1,0:T(8,128)(2,1)S(1)}, bf16[2,64,256]{2,1,0:T(8,128)(2,1)S(1)}, u32[]{:S(2)}, u32[]{:S(2)}) collective-permute-start(bf16[2,64,256]{2,1,0:T(8,128)(2,1)S(1)} %get-tuple-element.41.c1_ref), channel_id=1, source_target_pairs={{0,4},{4,8},{8,12},{12,16},{16,20},{20,24},{24,28},{28,0},{1,5},{5... | collective-permute-start | bytes 196616 | tf_op jit(solution)/shard_map/ppermute | solution.py:339
  26.8 9.4 %collective-permute-start.5 = (bf16[2,64,256]{2,1,0:T(8,128)(2,1)S(1)}, bf16[2,64,256]{2,1,0:T(8,128)(2,1)S(1)}, u32[]{:S(2)}, u32[]{:S(2)}) collective-permute-start(bf16[2,64,256]{2,1,0:T(8,128)(2,1)S(1)} %get-tuple-element.42.c0_ref), channel_id=1, source_target_pairs={{4,0},{8,4},{12,8},{16,12},{20,16},{24,20},{28,24},{0,28},{5,1},{9... | collective-permute-start | bytes 196616 | tf_op jit(solution)/shard_map/ppermute | solution.py:339
  36.2 5.2 %copy-start.1 = (bf16[169,8192]{1,0:T(8,128)(2,1)S(1)}, bf16[169,8192]{1,0:T(8,128)(2,1)}, u32[]{:S(2)}) copy-start(bf16[169,8192]{1,0:T(8,128)(2,1)} %goal_ref.1) | copy-start | bytes 8306692
  36.2 5.2 %copy-start.5 = (bf16[256,256]{1,0:T(8,128)(2,1)S(1)}, bf16[256,256]{1,0:T(8,128)(2,1)}, u32[]{:S(2)}) copy-start(bf16[256,256]{1,0:T(8,128)(2,1)} %hin_ref.1) | copy-start | bytes 393220
  36.2 5.2 %copy-start.7 = (bf16[256,169]{0,1:T(8,128)(2,1)S(1)}, bf16[256,169]{0,1:T(8,128)(2,1)}, u32[]{:S(2)}) copy-start(bf16[256,169]{0,1:T(8,128)(2,1)} %param.22) | copy-start | bytes 259588
  36.3 5.1 %collective-permute-start.6 = (bf16[4,64,256]{2,1,0:T(8,128)(2,1)S(1)}, bf16[4,64,256]{2,1,0:T(8,128)(2,1)S(1)}, u32[]{:S(2)}, u32[]{:S(2)}) collective-permute-start(bf16[4,64,256]{2,1,0:T(8,128)(2,1)S(1)} %get-tuple-element.46), channel_id=1, source_target_pairs={{0,1},{1,2},{2,3},{3,0},{4,5},{5,6},{6,7},{7,4},{8,9},{9,10},{10,1... | collective-permute-start | bytes 393224 | tf_op jit(solution)/shard_map/ppermute | solution.py:339
  36.4 5.0 %collective-permute-start.7 = (bf16[4,64,256]{2,1,0:T(8,128)(2,1)S(1)}, bf16[4,64,256]{2,1,0:T(8,128)(2,1)S(1)}, u32[]{:S(2)}, u32[]{:S(2)}) collective-permute-start(bf16[4,64,256]{2,1,0:T(8,128)(2,1)S(1)} %get-tuple-element.47), channel_id=1, source_target_pairs={{1,0},{2,1},{3,2},{0,3},{5,4},{6,5},{7,6},{4,7},{9,8},{10,9},{11,1... | collective-permute-start | bytes 393224 | tf_op jit(solution)/shard_map/ppermute | solution.py:339
  54.1 5.6 %collective-permute-start.8 = (f32[64,8,128]{2,1,0:T(8,128)S(1)}, f32[64,8,128]{2,1,0:T(8,128)S(1)}, u32[]{:S(2)}, u32[]{:S(2)}) collective-permute-start(f32[64,8,128]{2,1,0:T(8,128)S(1)} %get-tuple-element.50), channel_id=1, source_target_pairs={{0,32},{32,0},{1,33},{33,1},{2,34},{34,2},{3,35},{35,3},{4,36},{36... | collective-permute-start | bytes 786440 | tf_op jit(solution)/shard_map/ppermute | solution.py:349
